TPU v7x, 32 devices: a whole 2x2x4 slice. The times are simulated.
32 devices in a mesh: dp: 8 (over y, x, core), tensor: 4 (over z).
Axes of the slice: x: 2, y: 2, z: 4, core: 2. Of those that a mesh axis runs over, the one named last changes fastest.
Arguments:
- inputs: bfloat16 [8192, 2048], P(('dp', 'tensor')), may hold values from -6 to 6
- norm1_gain: float32 [2048], replicated, may hold values from 0.5 to 1.5
- query_weight: bfloat16 [2048, 1024], P('dp', 'tensor'), may hold values from -0.125 to 0.125
- key_weight: bfloat16 [2048, 1024], P('dp', 'tensor'), may hold values from -0.125 to 0.125
- value_weight: bfloat16 [2048, 2048], P('dp', 'tensor'), may hold values from -0.125 to 0.125
- outgate_weight: bfloat16 [2048, 2048], P('dp', 'tensor'), may hold values from -0.125 to 0.125
- gate_down: bfloat16 [2048, 16], replicated, may hold values from -0.125 to 0.125
- gate_up: float32 [16, 1024], P(None, 'tensor'), may hold values from -1.5 to 1.5
- gate_bias: float32 [1024], P('tensor'), may hold values from 0.5 to 4.5
- group_gain: float32 [2048], P('tensor'), may hold values from 0.5 to 1.5
- proj_weight: bfloat16 [2048, 2048], P('tensor', 'dp'), may hold values from -0.25 to 0.25
- norm2_gain: float32 [2048], replicated, may hold values from 0.5 to 1.5
- ffn_gate: bfloat16 [2048, 5632], P('dp', 'tensor'), may hold values from -0.125 to 0.125
- ffn_up: bfloat16 [2048, 5632], P('dp', 'tensor'), may hold values from -0.125 to 0.125
- ffn_down: bfloat16 [5632, 2048], P('tensor', 'dp'), may hold values from -0.109375 to 0.109375
- cotangent: bfloat16 [8192, 2048], P(('dp', 'tensor')), may hold values from -6 to 6
Outputs:
- output: bfloat16 [8192, 2048], P(('dp', 'tensor'))
- grad_input: float32 [8192, 2048], P(('dp', 'tensor'))
- grad_norm1: float32 [2048], replicated
- grad_query: float32 [2048, 1024], P('dp', 'tensor')
- grad_key: float32 [2048, 1024], P('dp', 'tensor')
- grad_value: float32 [2048, 2048], P('dp', 'tensor')
- grad_outgate: float32 [2048, 2048], P('dp', 'tensor')
- grad_gate_down: float32 [2048, 16], replicated
- grad_gate_up: float32 [16, 1024], P(None, 'tensor')
- grad_gate_bias: float32 [1024], P('tensor')
- grad_group_gain: float32 [2048], P('tensor')
- grad_proj: float32 [2048, 2048], P('tensor', 'dp')
- grad_norm2: float32 [2048], replicated
- grad_ffn_gate: float32 [2048, 5632], P('dp', 'tensor')
- grad_ffn_up: float32 [2048, 5632], P('dp', 'tensor')
- grad_ffn_down: float32 [5632, 2048], P('tensor', 'dp')
All inputs are finite; a program needn't handle non-finite values.
Results may differ from a plain program's by a relative error of at most 0.025.
Values may be sent and summed in bfloat16 or wider, within the bound.
No kernel may reach another device: no remote copies, remote signals or barrier semaphores. Data moves between devices by JAX's collectives and lax.ppermute only.
A program may use at most 192 MiB of HBM per device.

v0:
```python
import jax
import jax.numpy as jnp
from jax import lax
from jax.sharding import PartitionSpec as P

BLOCK = 64
LEN = 1024


eps_norm = 1e-06
eps_group = 1.0
highest = lax.Precision.HIGHEST


def product(former, latter):
    return jnp.dot(former, latter, preferred_element_type=jnp.float32, precision=highest)


def matmul(former, latter):
    return jnp.dot(former, latter, preferred_element_type=jnp.float32)


def times_transposed(former, latter):
    return lax.dot_general(
        former, latter, (((1,), (1,)), ((), ())), preferred_element_type=jnp.float32
    )


def transposed_times(former, latter):
    return lax.dot_general(
        former, latter, (((0,), (0,)), ((), ())), preferred_element_type=jnp.float32
    )


def block_step(carry_state, pieces):
    query_block, key_block, value_block, decay_block = pieces
    length = query_block.shape[0]
    running = jnp.cumsum(decay_block, axis=0)
    middle = running[length // 2]
    query_wide = query_block * jnp.exp(running - middle)
    key_wide = key_block * jnp.exp(middle - running)
    scores = product(query_wide, key_wide.T)
    causal = jnp.arange(length)[:, None] >= jnp.arange(length)[None, :]
    scores = jnp.where(causal, scores, 0.0)
    within = product(scores, value_block)
    across = product(query_block * jnp.exp(running), carry_state)
    final_sum = running[length - 1]
    carried = jnp.exp(final_sum)[:, None] * carry_state + product(
        (key_block * jnp.exp(final_sum - running)).T, value_block
    )
    return (carried, within + across)


def mixer_sequence(pieces):
    query_seq, key_seq, value_seq, decay_seq = pieces
    blocks = query_seq.shape[0] // BLOCK
    key_width = query_seq.shape[1]
    value_width = value_seq.shape[1]
    initial = jnp.zeros((key_width, value_width), jnp.float32)
    stacked = (
        query_seq.reshape(blocks, BLOCK, key_width),
        key_seq.reshape(blocks, BLOCK, key_width),
        value_seq.reshape(blocks, BLOCK, value_width),
        decay_seq.reshape(blocks, BLOCK, key_width),
    )
    _, result = lax.scan(jax.checkpoint(block_step), initial, stacked)
    return result.reshape(blocks * BLOCK, value_width)


def mixer_core(query_all, key_all, value_all, decay_all):
    rows_total = query_all.shape[0]
    count = rows_total // LEN
    key_width = query_all.shape[1]
    value_width = value_all.shape[1]
    scaled = query_all * key_width ** (-0.5)
    result = lax.map(
        mixer_sequence,
        (
            scaled.reshape(count, LEN, key_width),
            key_all.reshape(count, LEN, key_width),
            value_all.reshape(count, LEN, value_width),
            decay_all.reshape(count, LEN, key_width),
        ),
    )
    return result.reshape(rows_total, value_width)


def norm_back(grad_normed, rows_in, scale_rows, gain):
    weighted = grad_normed * gain
    gain_term = jnp.sum(grad_normed * rows_in * scale_rows, axis=0)
    grad_rows = scale_rows * weighted - rows_in * scale_rows**3 * jnp.mean(
        weighted * rows_in, axis=1, keepdims=True
    )
    return (grad_rows, gain_term)


def silu_slope(values_in):
    logistic = jax.nn.sigmoid(values_in)
    return logistic * (1.0 + values_in * (1.0 - logistic))


def on_device(
    inputs,
    norm1_gain,
    query_weight,
    key_weight,
    value_weight,
    outgate_weight,
    gate_down,
    gate_up,
    gate_bias,
    group_gain,
    proj_weight,
    norm2_gain,
    ffn_gate,
    ffn_up,
    ffn_down,
    cotangent,
):

    def fetch_mixer():
        return (
            lax.all_gather(query_weight, "dp", axis=0, tiled=True),
            lax.all_gather(key_weight, "dp", axis=0, tiled=True),
            lax.all_gather(value_weight, "dp", axis=0, tiled=True),
            lax.all_gather(outgate_weight, "dp", axis=0, tiled=True),
            lax.all_gather(proj_weight, "dp", axis=1, tiled=True),
        )

    def fetch_ffn():
        return (
            lax.all_gather(ffn_gate, "dp", axis=0, tiled=True),
            lax.all_gather(ffn_up, "dp", axis=0, tiled=True),
            lax.all_gather(ffn_down, "dp", axis=1, tiled=True),
        )

    inputs_wide = inputs.astype(jnp.float32)
    scale_one = lax.rsqrt(jnp.mean(inputs_wide * inputs_wide, axis=1, keepdims=True) + eps_norm)
    normed_one = (inputs_wide * scale_one * norm1_gain).astype(jnp.bfloat16)
    mixer_full = fetch_mixer()
    rows_one = lax.all_gather(normed_one, "tensor", axis=0, tiled=True)
    query_full, key_full, value_full, outgate_full, proj_full = mixer_full
    queries = matmul(rows_one, query_full).astype(jnp.bfloat16)
    keys_rows = matmul(rows_one, key_full).astype(jnp.bfloat16)
    values_rows = matmul(rows_one, value_full).astype(jnp.bfloat16)
    outgate = matmul(rows_one, outgate_full)
    lowrank = matmul(rows_one, gate_down)
    gate_logit = product(lowrank, gate_up) + gate_bias
    log_decay = jax.nn.log_sigmoid(gate_logit) / 16.0
    mixed_heads, core_back = jax.vjp(
        mixer_core,
        queries.astype(jnp.float32),
        keys_rows.astype(jnp.float32),
        values_rows.astype(jnp.float32),
        log_decay,
    )
    scale_head = lax.rsqrt(jnp.mean(mixed_heads * mixed_heads, axis=1, keepdims=True) + eps_group)
    normed_heads = mixed_heads * scale_head * group_gain
    gate_act = jax.nn.silu(outgate)
    gated = (normed_heads * gate_act).astype(jnp.bfloat16)
    resid = inputs_wide + lax.psum_scatter(
        matmul(gated, proj_full).astype(jnp.bfloat16), "tensor", scatter_dimension=0, tiled=True
    ).astype(jnp.float32)
    scale_two = lax.rsqrt(jnp.mean(resid * resid, axis=1, keepdims=True) + eps_norm)
    normed_two = (resid * scale_two * norm2_gain).astype(jnp.bfloat16)
    ffn_full = fetch_ffn()
    rows_two = lax.all_gather(normed_two, "tensor", axis=0, tiled=True)
    gate_full, up_full, down_full = ffn_full
    gate_pre = matmul(rows_two, gate_full)
    up_pre = matmul(rows_two, up_full)
    hidden = (jax.nn.silu(gate_pre) * up_pre).astype(jnp.bfloat16)
    output = (
        resid
        + lax.psum_scatter(
            matmul(hidden, down_full).astype(jnp.bfloat16),
            "tensor",
            scatter_dimension=0,
            tiled=True,
        ).astype(jnp.float32)
    ).astype(jnp.bfloat16)
    ffn_back = fetch_ffn()
    gate_back, up_back, down_back = ffn_back
    cot_rows = lax.all_gather(cotangent, "tensor", axis=0, tiled=True)
    grad_down_full = transposed_times(hidden, cot_rows)
    grad_hidden = times_transposed(cot_rows, down_back)
    grad_up = (grad_hidden * jax.nn.silu(gate_pre)).astype(jnp.bfloat16)
    grad_gate = (grad_hidden * up_pre * silu_slope(gate_pre)).astype(jnp.bfloat16)
    grad_gate_full = transposed_times(rows_two, grad_gate)
    grad_up_full = transposed_times(rows_two, grad_up)
    ffn_owned = (
        lax.psum_scatter(
            grad_gate_full.astype(jnp.bfloat16), "dp", scatter_dimension=0, tiled=True
        ).astype(jnp.float32),
        lax.psum_scatter(
            grad_up_full.astype(jnp.bfloat16), "dp", scatter_dimension=0, tiled=True
        ).astype(jnp.float32),
        lax.psum_scatter(
            grad_down_full.astype(jnp.bfloat16), "dp", scatter_dimension=1, tiled=True
        ).astype(jnp.float32),
    )
    grad_normed_two = lax.psum_scatter(
        (times_transposed(grad_gate, gate_back) + times_transposed(grad_up, up_back)).astype(
            jnp.bfloat16
        ),
        "tensor",
        scatter_dimension=0,
        tiled=True,
    ).astype(jnp.float32)
    norm_two_part, norm2_term = norm_back(grad_normed_two, resid, scale_two, norm2_gain)
    grad_resid = cotangent.astype(jnp.float32) + norm_two_part
    mixer_back = fetch_mixer()
    query_back, key_back, value_back, outgate_back, proj_back = mixer_back
    grad_branch = lax.all_gather(grad_resid.astype(jnp.bfloat16), "tensor", axis=0, tiled=True)
    grad_proj_full = transposed_times(gated, grad_branch)
    grad_gated = times_transposed(grad_branch, proj_back)
    grad_normed_heads = grad_gated * gate_act
    grad_out_pre = (grad_gated * normed_heads * silu_slope(outgate)).astype(jnp.bfloat16)
    grad_mixed, group_term = norm_back(grad_normed_heads, mixed_heads, scale_head, group_gain)
    query_term, key_term, value_term, grad_log_decay = core_back(grad_mixed)
    grad_queries = query_term.astype(jnp.bfloat16)
    grad_keys = key_term.astype(jnp.bfloat16)
    grad_values = value_term.astype(jnp.bfloat16)
    grad_logit = grad_log_decay * jax.nn.sigmoid(-gate_logit) / 16.0
    bias_term = jnp.sum(grad_logit, axis=0)
    up_term = lax.dot_general(
        lowrank,
        grad_logit,
        (((0,), (0,)), ((), ())),
        precision=highest,
        preferred_element_type=jnp.float32,
    )
    grad_lowrank = lax.dot_general(
        grad_logit,
        gate_up,
        (((1,), (1,)), ((), ())),
        precision=highest,
        preferred_element_type=jnp.float32,
    ).astype(jnp.bfloat16)
    down_term = transposed_times(rows_one, grad_lowrank)
    grad_query_full = transposed_times(rows_one, grad_queries)
    grad_key_full = transposed_times(rows_one, grad_keys)
    grad_value_full = transposed_times(rows_one, grad_values)
    grad_outgate_full = transposed_times(rows_one, grad_out_pre)
    mixer_owned = (
        lax.psum_scatter(
            grad_query_full.astype(jnp.bfloat16), "dp", scatter_dimension=0, tiled=True
        ).astype(jnp.float32),
        lax.psum_scatter(
            grad_key_full.astype(jnp.bfloat16), "dp", scatter_dimension=0, tiled=True
        ).astype(jnp.float32),
        lax.psum_scatter(
            grad_value_full.astype(jnp.bfloat16), "dp", scatter_dimension=0, tiled=True
        ).astype(jnp.float32),
        lax.psum_scatter(
            grad_outgate_full.astype(jnp.bfloat16), "dp", scatter_dimension=0, tiled=True
        ).astype(jnp.float32),
        lax.psum_scatter(
            grad_proj_full.astype(jnp.bfloat16), "dp", scatter_dimension=1, tiled=True
        ).astype(jnp.float32),
    )
    total = times_transposed(grad_queries, query_back)
    total = total + times_transposed(grad_keys, key_back)
    total = total + times_transposed(grad_values, value_back)
    total = total + times_transposed(grad_out_pre, outgate_back)
    grad_normed_one = lax.psum_scatter(
        (total + times_transposed(grad_lowrank, gate_down)).astype(jnp.bfloat16),
        "tensor",
        scatter_dimension=0,
        tiled=True,
    ).astype(jnp.float32)
    norm_one_part, norm1_term = norm_back(grad_normed_one, inputs_wide, scale_one, norm1_gain)
    grad_input = grad_resid + norm_one_part
    head_index = lax.axis_index("tensor")
    owner = (jnp.arange(lax.axis_size("tensor")) == head_index).astype(jnp.float32)
    summed = lax.psum(
        (
            norm1_term,
            norm2_term,
            down_term,
            owner[:, None] * group_term[None, :],
            owner[:, None, None] * up_term[None, :, :],
            owner[:, None] * bias_term[None, :],
        ),
        ("dp", "tensor"),
    )
    grad_norm1, grad_norm2, grad_gate_down, gain_slots, up_slots, bias_slots = summed
    grad_group_gain = lax.dynamic_index_in_dim(gain_slots, head_index, 0, keepdims=False)
    grad_gate_up = lax.dynamic_index_in_dim(up_slots, head_index, 0, keepdims=False)
    grad_gate_bias = lax.dynamic_index_in_dim(bias_slots, head_index, 0, keepdims=False)
    grad_query, grad_key, grad_value, grad_outgate, grad_proj = mixer_owned
    grad_ffn_gate, grad_ffn_up, grad_ffn_down = ffn_owned
    return (
        output,
        grad_input,
        grad_norm1,
        grad_query,
        grad_key,
        grad_value,
        grad_outgate,
        grad_gate_down,
        grad_gate_up,
        grad_gate_bias,
        grad_group_gain,
        grad_proj,
        grad_norm2,
        grad_ffn_gate,
        grad_ffn_up,
        grad_ffn_down,
    )


def solution(mesh):
    placed = (
        P(("dp", "tensor"), None),
        P(),
        P("dp", "tensor"),
        P("dp", "tensor"),
        P("dp", "tensor"),
        P("dp", "tensor"),
        P(),
        P(None, "tensor"),
        P("tensor"),
        P("tensor"),
        P("tensor", "dp"),
        P(),
        P("dp", "tensor"),
        P("dp", "tensor"),
        P("tensor", "dp"),
        P(("dp", "tensor"), None),
    )
    return jax.shard_map(
        on_device,
        mesh=mesh,
        in_specs=placed,
        out_specs=(
            P(("dp", "tensor"), None),
            P(("dp", "tensor"), None),
            P(),
            P("dp", "tensor"),
            P("dp", "tensor"),
            P("dp", "tensor"),
            P("dp", "tensor"),
            P(),
            P(None, "tensor"),
            P("tensor"),
            P("tensor"),
            P("tensor", "dp"),
            P(),
            P("dp", "tensor"),
            P("dp", "tensor"),
            P("tensor", "dp"),
        ),
        check_vma=False,
    )
```

profile of v0, /device:TPU:0, one launch (start us, length us, event | category | flops | bytes accessed | tf_op | source)
XLA Modules:
  0.0 1581.5 jit_solution(16903774207863829336)
XLA Ops:
  15.2 21.0 %all-gather.15.cloned.1.call-done = bf16[2048,256]{1,0:T(8,128)(2,1)} async-done(((bf16[256,256]{1,0:T(8,128)(2,1)}), bf16[2048,256]{1,0:T(8,128)(2,1)}) %all-gather.15.cloned.1.call-update) | async-done | bytes 1048592 | tf_op jit(solution)/shard_map/all_gather | solution.py:124
  36.1 82.9 %all-gather.13.cloned.1.call-done = bf16[1024,2048]{1,0:T(8,128)(2,1)} async-done(((bf16[256,2048]{1,0:T(8,128)(2,1)}), bf16[1024,2048]{1,0:T(8,128)(2,1)}) %all-gather.13.cloned.1.call-update) | async-done | bytes 4194320 | tf_op jit(solution)/shard_map/all_gather | solution.py:141
  119.1 3.7 convolution_convert_fusion.12
  123.9 23.5 %all-gather.17.cloned.1.call-done = bf16[2048,512]{1,0:T(8,128)(2,1)} async-done(((bf16[256,512]{1,0:T(8,128)(2,1)}), bf16[2048,512]{1,0:T(8,128)(2,1)}) %all-gather.17.cloned.1.call-update) | async-done | bytes 2097168 | tf_op jit(solution)/shard_map/all_gather | solution.py:125
  147.4 5.3 convolution_convert_fusion.10
  158.4 14.3 all-gather.19.cloned.1.call-done
  172.7 4.7 fusion.79
  177.4 113.0 %while.67 = (s32[]{:T(128)}, f32[256,512]{1,0:T(8,128)S(1)}, f32[16,64,512]{2,1,0:T(8,128)S(1)}, f32[16,256,512]{2,1,0:T(8,128)}, f32[16,64,256]{2,1,0:T(8,128)}...) while((s32[]{:T(128)}, f32[256,512]{1,0:T(8,128)S(1)}, ...), condition=%wide.region_3.4_spmd.clone.clone, body=%wide.region_1.3_spmd.clone.sunk.clone | while | flops 240918528 | bytes 4110455 | solution.py:66
  291.2 6.7 multiply_convert_fusion.5
  298.0 6.3 convolution_convert_fusion.4
  305.1 76.1 %reduce-scatter.13.cloned.1.call-done = bf16[256,2048]{1,0:T(8,128)(2,1)} async-done(((bf16[1024,2048]{1,0:T(8,128)(2,1)}), bf16[256,2048]{1,0:T(8,128)(2,1)}) %reduce-scatter.13.cloned.1.call-update) | async-done | bytes 1048592 | tf_op jit(solution)/shard_map/reduce_scatter | solution.py:161
  386.6 40.5 %all-gather.27.cloned.1.call-done = bf16[2048,1408]{1,0:T(8,128)(2,1)} async-done(((bf16[256,1408]{1,0:T(8,128)(2,1)}), bf16[2048,1408]{1,0:T(8,128)(2,1)}) %all-gather.27.cloned.1.call-update) | async-done | bytes 5767184 | tf_op jit(solution)/shard_map/all_gather | solution.py:132
  427.0 82.5 %all-gather.25.cloned.1.call-done = bf16[1024,2048]{1,0:T(8,128)(2,1)} async-done(((bf16[256,2048]{1,0:T(8,128)(2,1)}), bf16[1024,2048]{1,0:T(8,128)(2,1)}) %all-gather.25.cloned.1.call-update) | async-done | bytes 4194320 | tf_op jit(solution)/shard_map/all_gather | solution.py:167
  509.5 11.7 fusion.93
  521.2 32.0 %all-gather.29.cloned.1.call-done = bf16[2048,1408]{1,0:T(8,128)(2,1)} async-done(((bf16[256,1408]{1,0:T(8,128)(2,1)}), bf16[2048,1408]{1,0:T(8,128)(2,1)}) %all-gather.29.cloned.1.call-update) | async-done | bytes 5767184 | tf_op jit(solution)/shard_map/all_gather | solution.py:133
  553.3 11.7 fusion.94
  565.0 70.8 %all-gather.33.cloned.1.call-done = bf16[1024,2048]{1,0:T(8,128)(2,1)} async-done(((bf16[256,2048]{1,0:T(8,128)(2,1)}), bf16[1024,2048]{1,0:T(8,128)(2,1)}) %all-gather.33.cloned.1.call-update) | async-done | bytes 4194320 | tf_op jit(solution)/shard_map/all_gather | solution.py:183
  635.7 44.8 %all-gather.31.cloned.1.call-done = bf16[1408,2048]{1,0:T(8,128)(2,1)} async-done(((bf16[1408,256]{1,0:T(8,128)(2,1)}), bf16[1408,2048]{1,0:T(8,128)(2,1)}) %all-gather.31.cloned.1.call-update) | async-done | bytes 5767184 | tf_op jit(solution)/shard_map/all_gather | solution.py:134
  680.5 15.5 multiply_convert_fusion
  696.1 10.9 fusion.95
  707.0 8.3 add_convert_fusion.1
  715.6 76.6 %reduce-scatter.17.cloned.1.call-done = bf16[256,2048]{1,0:T(8,128)(2,1)} async-done(((bf16[1024,2048]{1,0:T(8,128)(2,1)}), bf16[256,2048]{1,0:T(8,128)(2,1)}) %reduce-scatter.17.cloned.1.call-update) | async-done | bytes 1048592 | tf_op jit(solution)/shard_map/reduce_scatter | solution.py:201
  796.2 11.1 convolution_convert_fusion.2
  807.3 11.0 convolution_convert_fusion.1
  820.4 10.5 convolution_convert_fusion
  831.4 46.2 %all-gather.35.cloned.1.call-done = bf16[1024,2048]{1,0:T(8,128)(2,1)} async-done(((bf16[256,2048]{1,0:T(8,128)(2,1)}), bf16[1024,2048]{1,0:T(8,128)(2,1)}) %all-gather.35.cloned.1.call-update) | async-done | bytes 4194320 | tf_op jit(solution)/shard_map/all_gather | solution.py:213
  877.6 7.2 fusion.76
  890.0 166.6 %while.68 = (s32[]{:T(128)}, f32[256,512]{1,0:T(8,128)S(1)}, f32[16,64,256]{2,1,0:T(8,128)}, bf16[16,64,256]{2,1,0:T(8,128)(2,1)}, bf16[16,64,512]{2,1,0:T(8,128...) while((s32[]{:T(128)}, f32[256,512]{1,0:T(8,128)S(1)}, ...), condition=%wide.region_18.19_spmd.clone.clone, body=%wide.region_11.18_spmd.clone.sunk.clone | while | flops 494321664 | bytes 10680503 | solution.py:66
  1062.4 4.6 convolution_convert_fusion.9
  1067.3 4.6 convolution_convert_fusion.8
  1072.0 5.9 convolution_convert_fusion.7
  1079.1 5.9 convolution_convert_fusion.6
  1086.2 5.9 convolution_convert_fusion.5
  1095.3 4.6 fusion.97
  1099.9 5.6 fusion.99
  1105.5 5.6 fusion.98
  1111.1 11.7 add_convert_fusion
  1122.9 10.9 convolution_convert_fusion.3
  1141.0 52.9 %all-reduce.6.cloned.1.call-done = (f32[2048,16]{0,1:T(8,128)}, f32[4,16,256]{2,1,0:T(8,128)}) async-done(((f32[2048,16]{0,1:T(8,128)}, f32[4,16,256]{2,1,0:T(8,128)}), (f32[2048,16]{0,1:T(8,128)}, f32[4,16,256]{2,1,0:T(8,128)})) %all-reduce.6.cloned.1.call-update) | async-done | bytes 196624 | tf_op jit(solution)/shard_map/psum | solution.py:275
  1195.2 39.7 %reduce-scatter.21.cloned.1.call-done = bf16[256,256]{1,0:T(8,128)(2,1)} async-done(((bf16[2048,256]{1,0:T(8,128)(2,1)}), bf16[256,256]{1,0:T(8,128)(2,1)}) %reduce-scatter.21.cloned.1.call-update) | async-done | bytes 131088 | tf_op jit(solution)/shard_map/reduce_scatter | solution.py:245
  1236.5 37.8 %reduce-scatter.23.cloned.1.call-done = bf16[256,256]{1,0:T(8,128)(2,1)} async-done(((bf16[2048,256]{1,0:T(8,128)(2,1)}), bf16[256,256]{1,0:T(8,128)(2,1)}) %reduce-scatter.23.cloned.1.call-update) | async-done | bytes 131088 | tf_op jit(solution)/shard_map/reduce_scatter | solution.py:248
  1276.0 43.8 %reduce-scatter.25.cloned.1.call-done = bf16[256,512]{1,0:T(8,128)(2,1)} async-done(((bf16[2048,512]{1,0:T(8,128)(2,1)}), bf16[256,512]{1,0:T(8,128)(2,1)}) %reduce-scatter.25.cloned.1.call-update) | async-done | bytes 262160 | tf_op jit(solution)/shard_map/reduce_scatter | solution.py:251
  1321.6 42.7 %reduce-scatter.27.cloned.1.call-done = bf16[256,512]{1,0:T(8,128)(2,1)} async-done(((bf16[2048,512]{1,0:T(8,128)(2,1)}), bf16[256,512]{1,0:T(8,128)(2,1)}) %reduce-scatter.27.cloned.1.call-update) | async-done | bytes 262160 | tf_op jit(solution)/shard_map/reduce_scatter | solution.py:254
  1366.1 43.1 %reduce-scatter.29.cloned.1.call-done = bf16[512,256]{1,0:T(8,128)(2,1)} async-done(((bf16[512,2048]{1,0:T(8,128)(2,1)}), bf16[512,256]{1,0:T(8,128)(2,1)}) %reduce-scatter.29.cloned.1.call-update) | async-done | bytes 262160 | tf_op jit(solution)/shard_map/reduce_scatter | solution.py:257
  1411.0 77.1 %reduce-scatter.19.cloned.1.call-done = bf16[256,2048]{1,0:T(8,128)(2,1)} async-done(((bf16[1024,2048]{1,0:T(8,128)(2,1)}), bf16[256,2048]{1,0:T(8,128)(2,1)}) %reduce-scatter.19.cloned.1.call-update) | async-done | bytes 1048592 | tf_op jit(solution)/shard_map/reduce_scatter | solution.py:265
  1490.0 47.2 %all-reduce.2 = (f32[2048]{0:T(1024)}, f32[4,256]{1,0:T(4,128)S(1)}, f32[4,512]{1,0:T(4,128)S(1)}, f32[2048]{0:T(1024)}) all-reduce(f32[2048]{0:T(1024)S(1)} %get-tuple-element.502, f32[4,256]{1,0:T(4,128)S(1)} %broadcast_multiply_fusion.2, ...), channel_id=1, replica_groups=mesh['dp'=8,'tensor'=4] {'dp','tensor'}, use_global_device_ids=true, to_apply=%region_22.23 | all-reduce | flops 7168 | bytes 57344 | tf_op jit(solution)/shard_map/psum | solution.py:275
  1538.4 30.5 %reduce-scatter.15.cloned.1.call-done = bf16[256,2048]{1,0:T(8,128)(2,1)} async-done(((bf16[1024,2048]{1,0:T(8,128)(2,1)}), bf16[256,2048]{1,0:T(8,128)(2,1)}) %reduce-scatter.15.cloned.1.call-update) | async-done | bytes 1048592 | tf_op jit(solution)/shard_map/reduce_scatter | solution.py:174
  1568.9 5.2 fusion.58
  (714 shorter events, 343.1 us)
Async XLA Ops:
  7.2 147.2 %copy-start = (bf16[2048,16]{0,1:T(8,128)(2,1)S(1)}, bf16[2048,16]{0,1:T(8,128)(2,1)}, u32[]{:S(2)}) copy-start(bf16[2048,16]{0,1:T(8,128)(2,1)} %param.26) | copy-start | bytes 196612
  7.2 28.9 %all-gather.15.cloned.1.call-start = ((), (), s32[]{:S(2)}) async-start(), calls=%async_computation.13 | async-start | bytes 1179648 | tf_op jit(solution)/shard_map/all_gather | solution.py:124
  7.9 111.1 %all-gather.13.cloned.1.call-start = ((), (), s32[]{:S(2)}) async-start(), calls=%async_computation.12 | async-start | bytes 5242880 | tf_op jit(solution)/shard_map/all_gather | solution.py:141
  10.1 5.0 copy-start.26
  12.6 134.8 %all-gather.17.cloned.1.call-start = ((), (), s32[]{:S(2)}) async-start(), calls=%async_computation.14 | async-start | bytes 2359296 | tf_op jit(solution)/shard_map/all_gather | solution.py:125
  13.4 159.4 %all-gather.19.cloned.1.call-start = ((), (), s32[]{:S(2)}) async-start(), calls=%async_computation.15 | async-start | bytes 1179648 | tf_op jit(solution)/shard_map/all_gather | solution.py:123
  13.9 276.9 %all-gather.21.cloned.1.call-start = ((), (), s32[]{:S(2)}) async-start(), calls=%async_computation.16 | async-start | bytes 2359296 | tf_op jit(solution)/shard_map/all_gather | solution.py:126
  14.5 283.4 %all-gather.23.cloned.1.call-start = ((), (), s32[]{:S(2)}) async-start(), calls=%async_computation.17 | async-start | bytes 2359296 | tf_op jit(solution)/shard_map/all_gather | solution.py:127
  15.1 366.0 %reduce-scatter.13.cloned.1.call-start = ((), (), s32[]{:S(2)}) async-start(), calls=%async_computation.18 | async-start | bytes 5242880 | tf_op jit(solution)/shard_map/reduce_scatter | solution.py:161
  147.4 6.9 copy-start.4
  155.6 21.9 %copy-start.21 = (f32[1024,16]{0,1:T(8,128)}, f32[1024,16]{0,1:T(8,128)S(1)}, u32[]{:S(2)}) copy-start(f32[1024,16]{0,1:T(8,128)S(1)} %fusion.92) | copy-start | bytes 196612
  290.5 7.5 copy-start.9
  297.9 6.3 copy-start.36
  304.2 76.9 %copy-start.1 = (bf16[256,2048]{1,0:T(8,128)(2,1)S(1)}, bf16[256,2048]{1,0:T(8,128)(2,1)}, u32[]{:S(2)}) copy-start(bf16[256,2048]{1,0:T(8,128)(2,1)} %param.20) | copy-start | bytes 3145732
  304.3 78.6 %copy-start.23 = (f32[2048]{0:T(1024)S(1)}, f32[2048]{0:T(1024)}, u32[]{:S(2)}) copy-start(f32[2048]{0:T(1024)} %param.31) | copy-start | bytes 24580
  304.3 122.8 %all-gather.27.cloned.1.call-start = ((), (), s32[]{:S(2)}) async-start(), calls=%async_computation.20 | async-start | bytes 6488064 | tf_op jit(solution)/shard_map/all_gather | solution.py:132
  305.0 204.5 %all-gather.25.cloned.1.call-start = ((), (), s32[]{:S(2)}) async-start(), calls=%async_computation.19 | async-start | bytes 5242880 | tf_op jit(solution)/shard_map/all_gather | solution.py:167
  384.4 168.8 %all-gather.29.cloned.1.call-start = ((), (), s32[]{:S(2)}) async-start(), calls=%async_computation.21 | async-start | bytes 6488064 | tf_op jit(solution)/shard_map/all_gather | solution.py:133
  385.0 250.7 %all-gather.33.cloned.1.call-start = ((), (), s32[]{:S(2)}) async-start(), calls=%async_computation.24 | async-start | bytes 5242880 | tf_op jit(solution)/shard_map/all_gather | solution.py:183
  385.8 294.8 %all-gather.31.cloned.1.call-start = ((), (), s32[]{:S(2)}) async-start(), calls=%async_computation.22 | async-start | bytes 6488064 | tf_op jit(solution)/shard_map/all_gather | solution.py:134
  386.3 405.9 %reduce-scatter.17.cloned.1.call-start = ((), (), s32[]{:S(2)}) async-start(), calls=%async_computation.25 | async-start | bytes 5242880 | tf_op jit(solution)/shard_map/reduce_scatter | solution.py:201
  696.1 10.9 copy-start.38
  696.1 10.9 copy-start.39
  696.1 10.9 copy-start.32
  715.3 79.0 %copy-start.6 = (bf16[256,2048]{1,0:T(8,128)(2,1)S(1)}, bf16[256,2048]{1,0:T(8,128)(2,1)}, u32[]{:S(2)}) copy-start(bf16[256,2048]{1,0:T(8,128)(2,1)} %param.35) | copy-start | bytes 3145732
  715.3 162.3 %all-gather.35.cloned.1.call-start = ((), (), s32[]{:S(2)}) async-start(), calls=%async_computation.26 | async-start | bytes 5242880 | tf_op jit(solution)/shard_map/all_gather | solution.py:213
  796.2 337.7 %reduce-scatter.31.cloned.1.call-start = ((), (), s32[]{:S(2)}) async-start(), calls=%async_computation.33 | async-start | bytes 6488064 | tf_op jit(solution)/shard_map/reduce_scatter | solution.py:191
  807.3 328.9 %reduce-scatter.33.cloned.1.call-start = ((), (), s32[]{:S(2)}) async-start(), calls=%async_computation.34 | async-start | bytes 6488064 | tf_op jit(solution)/shard_map/reduce_scatter | solution.py:194
  818.4 320.2 %reduce-scatter.35.cloned.1.call-start = ((), (), s32[]{:S(2)}) async-start(), calls=%async_computation.35 | async-start | bytes 6488064 | tf_op jit(solution)/shard_map/reduce_scatter | solution.py:197
  830.9 363.0 %all-reduce.6.cloned.1.call-start = ((), (), s32[]{:S(2)}) async-start(), calls=%async_computation.36 | async-start | bytes 393216 | tf_op jit(solution)/shard_map/psum | solution.py:275
  877.6 7.3 copy-start.10
  877.6 7.3 copy-start.15
  890.0 169.9 %copy-start.29 = (f32[16,256]{1,0:T(8,128)S(1)}, f32[16,256]{1,0:T(8,128)}, u32[]{:S(2)}) copy-start(f32[16,256]{1,0:T(8,128)} %param.27) | copy-start | bytes 49156
  1062.3 172.6 %reduce-scatter.21.cloned.1.call-start = ((), (), s32[]{:S(2)}) async-start(), calls=%async_computation.28 | async-start | bytes 1179648 | tf_op jit(solution)/shard_map/reduce_scatter | solution.py:245
  1067.0 207.3 %reduce-scatter.23.cloned.1.call-start = ((), (), s32[]{:S(2)}) async-start(), calls=%async_computation.29 | async-start | bytes 1179648 | tf_op jit(solution)/shard_map/reduce_scatter | solution.py:248
  1071.9 247.9 %reduce-scatter.25.cloned.1.call-start = ((), (), s32[]{:S(2)}) async-start(), calls=%async_computation.30 | async-start | bytes 2359296 | tf_op jit(solution)/shard_map/reduce_scatter | solution.py:251
  1077.9 286.4 %reduce-scatter.27.cloned.1.call-start = ((), (), s32[]{:S(2)}) async-start(), calls=%async_computation.31 | async-start | bytes 2359296 | tf_op jit(solution)/shard_map/reduce_scatter | solution.py:254
  1085.0 324.2 %reduce-scatter.29.cloned.1.call-start = ((), (), s32[]{:S(2)}) async-start(), calls=%async_computation.32 | async-start | bytes 2359296 | tf_op jit(solution)/shard_map/reduce_scatter | solution.py:257
  1092.2 396.0 %reduce-scatter.19.cloned.1.call-start = ((), (), s32[]{:S(2)}) async-start(), calls=%async_computation.27 | async-start | bytes 5242880 | tf_op jit(solution)/shard_map/reduce_scatter | solution.py:265
  1099.8 5.6 copy-start.18
  1099.8 5.6 copy-start.33
  1122.9 446.0 %reduce-scatter.15.cloned.1.call-start = ((), (), s32[]{:S(2)}) async-start(), calls=%async_computation.23 | async-start | bytes 5242880 | tf_op jit(solution)/shard_map/reduce_scatter | solution.py:174
  1140.8 347.3 %copy-start.25 = (f32[2048]{0:T(1024)S(1)}, f32[2048]{0:T(1024)}, u32[]{:S(2)}) copy-start(f32[2048]{0:T(1024)} %param.21) | copy-start | bytes 24580
  1140.8 347.3 %copy-start.27 = (f32[256]{0:T(256)S(1)}, f32[256]{0:T(256)}, u32[]{:S(2)}) copy-start(f32[256]{0:T(256)} %copy-done.26) | copy-start | bytes 3076
  1276.0 292.9 %copy-start.3 = (bf16[256,2048]{1,0:T(8,128)(2,1)S(1)}, bf16[256,2048]{1,0:T(8,128)(2,1)}, u32[]{:S(2)}) copy-start(bf16[256,2048]{1,0:T(8,128)(2,1)} %reduce-scatter.13.cloned.1.call-done) | copy-start | bytes 3145732
  1276.0 292.9 %copy-start.7 = (bf16[256,2048]{1,0:T(8,128)(2,1)S(1)}, bf16[256,2048]{1,0:T(8,128)(2,1)}, u32[]{:S(2)}) copy-start(bf16[256,2048]{1,0:T(8,128)(2,1)} %param.35) | copy-start | bytes 3145732
  1276.0 292.9 %copy-start.30 = (f32[256]{0:T(256)S(1)}, f32[256]{0:T(256)}, u32[]{:S(2)}) copy-start(f32[256]{0:T(256)} %get-tuple-element.570) | copy-start | bytes 3076
  1568.9 5.2 copy-start.24
  (17 other events, 45.8 us)
Sparse Core Ops, SparseCore 0:
  9.9 26.1 all-gather.14
  38.3 80.7 all-gather.12
  121.0 26.4 all-gather.16
  149.2 23.4 all-gather.18
  174.4 27.8 all-gather.20
  204.1 28.2 all-gather.22
  304.4 76.7 reduce-scatter.12
  383.2 43.8 all-gather.26
  428.7 80.7 all-gather.24
  511.4 41.8 all-gather.28
  554.9 80.7 all-gather.32
  637.6 42.8 all-gather.30
  715.4 76.7 reduce-scatter.16
  796.3 81.2 all-gather.34
  880.9 57.5 reduce-scatter.30
  942.2 58.9 reduce-scatter.32
  1004.5 59.1 reduce-scatter.34
  1070.6 123.2 all-reduce.5
  1198.0 36.9 reduce-scatter.20
  1238.3 36.0 reduce-scatter.22
  1278.5 41.2 reduce-scatter.24
  1323.1 41.1 reduce-scatter.26
  1368.0 41.2 reduce-scatter.28
  1411.4 76.7 reduce-scatter.18
  1490.5 78.3 reduce-scatter.14
where the time goes:
time: 1600 us; the launch traced here: 1580 us
  waiting for transfers between devices  985 us (62%)
  matrix products  361 us (23%)
  local copies, waits for them, and re-layouts  93.9 us (6%)
  other arithmetic  76.2 us (5%)
  blocking collectives  47.2 us (3%)
    dot_general x209, matrix products, product(): jnp.dot(former, latter, preferred_element_type=jnp.float32, precision=hig...  164 us
    all_gather x1, waiting for transfers between devices, on_device(): rows_one = lax.all_gather(normed_one, 'tensor', axis=0, tiled=True)  82.9 us
    all_gather x1, waiting for transfers between devices, on_device(): rows_two = lax.all_gather(normed_two, 'tensor', axis=0, tiled=True)  82.5 us
    reduce_scatter x1, waiting for transfers between devices, on_device(): lax.psum_scatter((total + times_transposed(grad_lowrank, gate_down)).asty...  77.1 us
    reduce_scatter x1, waiting for transfers between devices, on_device(): lax.psum_scatter((times_transposed(grad_gate, gate_back) + times_transpos...  76.6 us
    reduce_scatter x1, waiting for transfers between devices, on_device(): lax.psum_scatter(matmul(gated, proj_full).astype(jnp.bfloat16), 'tensor',...  76.1 us
    squeeze x80, local copies, waits for them, and re-layouts, mixer_sequence(): _, result = lax.scan(jax.checkpoint(block_step), initial, stacked)  75.1 us
    dot_general x9, matrix products, times_transposed(): lax.dot_general(former, latter, (((1,), (1,)), ((), ())), preferred_eleme...  72.3 us
  transfers between devices with their start and end apart: 25, of which 20 were waited for; matrix products, arithmetic and copies ran while one was open for 30% of the time, Pallas kernels for 0%

commit v1 on v0

v1 whole, which is shorter than its diff:
```python
import functools

import jax
import jax.numpy as jnp
from jax import lax
from jax.experimental import pallas as pl
from jax.experimental.pallas import tpu as pltpu
from jax.sharding import PartitionSpec as P

BLOCK = 64
LEN = 1024
HIGHEST = lax.Precision.HIGHEST
EPS_NORM = 1e-06
EPS_GROUP = 1.0
BF = jnp.bfloat16
F32 = jnp.float32


def dot(a, b, ca, cb, precision=None):
    return lax.dot_general(
        a, b, (((ca,), (cb,)), ((), ())), precision=precision, preferred_element_type=F32
    )


def matmul(a, b):
    return dot(a, b, 1, 0)


def times_transposed(a, b):
    return dot(a, b, 1, 1)


def transposed_times(a, b):
    return dot(a, b, 0, 0)


def sigmoid(x):
    return 1.0 / (1.0 + jnp.exp(-x))


def causal(length, lower=True):
    rows = lax.broadcasted_iota(jnp.int32, (length, length), 0)
    columns = lax.broadcasted_iota(jnp.int32, (length, length), 1)
    return rows >= columns if lower else rows <= columns


def gates(lowrank, gate_up, gate_bias):
    logit = dot(lowrank, gate_up, 1, 0, HIGHEST) + gate_bias
    decay = (jnp.minimum(logit, 0.0) - jnp.log(1.0 + jnp.exp(-jnp.abs(logit)))) / 16.0
    ones = jnp.where(causal(BLOCK), 1.0, 0.0).astype(F32)
    return logit, dot(ones, decay, 1, 0, HIGHEST)


def forward_kernel(kw, vw, proj_ref, low_ref, up_ref, bias_ref, gain_ref,
                   gated_ref, mixed_ref, states_ref, state):
    blocks = proj_ref.shape[0] // BLOCK
    root = kw ** (-0.5)
    state[...] = jnp.zeros_like(state)
    mask = causal(BLOCK)

    def step(i, _):
        rows = pl.ds(pl.multiple_of(i * BLOCK, BLOCK), BLOCK)
        query = proj_ref[rows, 0:kw].astype(F32) * root
        key = proj_ref[rows, kw:2 * kw].astype(F32)
        value = proj_ref[rows, 2 * kw:2 * kw + vw]
        outgate = proj_ref[rows, 2 * kw + vw:2 * kw + 2 * vw].astype(F32)
        _, running = gates(low_ref[rows, :], up_ref[...], bias_ref[...])
        middle = running[BLOCK // 2:BLOCK // 2 + 1, :]
        last = running[BLOCK - 1:BLOCK, :]
        query_wide = (query * jnp.exp(running - middle)).astype(BF)
        key_wide = (key * jnp.exp(middle - running)).astype(BF)
        query_in = (query * jnp.exp(running)).astype(BF)
        key_out = (key * jnp.exp(last - running)).astype(BF)
        before = state[...]
        before_low = before.astype(BF)
        states_ref[i, :, :] = before_low
        scores = jnp.where(mask, times_transposed(query_wide, key_wide), 0.0).astype(BF)
        mixed = matmul(scores, value) + times_transposed(query_in, before_low)
        state[...] = before * jnp.exp(last) + transposed_times(value, key_out)
        mixed_ref[rows, :] = mixed.astype(mixed_ref.dtype)
        scale = lax.rsqrt(jnp.mean(mixed * mixed, axis=1, keepdims=True) + EPS_GROUP)
        normed = mixed * scale * gain_ref[...]
        gated_ref[rows, :] = (normed * (outgate * sigmoid(outgate))).astype(BF)
        return 0

    lax.fori_loop(0, blocks, step, 0)


def backward_kernel(kw, vw, proj_ref, low_ref, up_ref, bias_ref, gain_ref, mixed_ref,
                    states_ref, grad_ref, out_ref, down_ref, upgrad_ref, sums_ref, gains_ref, state):
    blocks = proj_ref.shape[0] // BLOCK
    root = kw ** (-0.5)
    state[...] = jnp.zeros_like(state)
    mask = causal(BLOCK)
    suffix = jnp.where(causal(BLOCK, False), 1.0, 0.0).astype(F32)
    upgrad_ref[...] = jnp.zeros_like(upgrad_ref)
    sums_ref[...] = jnp.zeros_like(sums_ref)
    gains_ref[...] = jnp.zeros_like(gains_ref)

    def step(j, _):
        i = blocks - 1 - j
        rows = pl.ds(pl.multiple_of(i * BLOCK, BLOCK), BLOCK)
        query = proj_ref[rows, 0:kw].astype(F32) * root
        key = proj_ref[rows, kw:2 * kw].astype(F32)
        value = proj_ref[rows, 2 * kw:2 * kw + vw]
        outgate = proj_ref[rows, 2 * kw + vw:2 * kw + 2 * vw].astype(F32)
        mixed = mixed_ref[rows, :].astype(F32)
        gain = gain_ref[...]
        grad_gated = grad_ref[rows, :].astype(F32)
        scale = lax.rsqrt(jnp.mean(mixed * mixed, axis=1, keepdims=True) + EPS_GROUP)
        unit = mixed * scale
        logistic = sigmoid(outgate)
        grad_normed = grad_gated * (outgate * logistic)
        out_ref[rows, 2 * kw + vw:2 * kw + 2 * vw] = (
            grad_gated * (unit * gain) * (logistic * (1.0 + outgate * (1.0 - logistic)))
        ).astype(BF)
        gains_ref[...] += jnp.sum(grad_normed * unit, axis=0, keepdims=True)
        weighted = grad_normed * gain
        grad = (scale * (weighted - unit * jnp.mean(weighted * unit, axis=1, keepdims=True))).astype(BF)
        low = low_ref[rows, :]
        logit, running = gates(low, up_ref[...], bias_ref[...])
        middle = running[BLOCK // 2:BLOCK // 2 + 1, :]
        last = running[BLOCK - 1:BLOCK, :]
        rise, fall = jnp.exp(running - middle), jnp.exp(middle - running)
        enter, leave = jnp.exp(running), jnp.exp(last - running)
        query_wide = (query * rise).astype(BF)
        key_wide = (key * fall).astype(BF)
        query_in = (query * enter).astype(BF)
        key_out = (key * leave).astype(BF)
        before = states_ref[i, :, :]
        after = state[...]
        after_low = after.astype(BF)
        carried = transposed_times(value, key_out)
        ended = before.astype(F32) * jnp.exp(last) + carried
        boundary = jnp.sum(ended * after, axis=0, keepdims=True)
        scores = jnp.where(mask, times_transposed(query_wide, key_wide), 0.0).astype(BF)
        grad_scores = jnp.where(mask, times_transposed(grad, value), 0.0).astype(BF)
        grad_value = transposed_times(scores, grad) + times_transposed(key_out, after_low)
        query_term = matmul(grad_scores, key_wide) * rise + matmul(grad, before) * enter
        key_term = transposed_times(grad_scores, query_wide) * fall + matmul(value, after_low) * leave
        state[...] = after * jnp.exp(last) + transposed_times(grad, query_in)
        out_ref[rows, 0:kw] = (query_term * root).astype(BF)
        out_ref[rows, kw:2 * kw] = key_term.astype(BF)
        out_ref[rows, 2 * kw:2 * kw + vw] = grad_value.astype(BF)
        grad_decay = dot(suffix, query * query_term - key * key_term, 1, 0, HIGHEST) + boundary
        grad_logit = grad_decay * (sigmoid(-logit) / 16.0)
        sums_ref[...] += jnp.sum(grad_logit, axis=0, keepdims=True)
        upgrad_ref[...] += dot(low, grad_logit, 0, 0, HIGHEST)
        down_ref[rows, :] = dot(grad_logit, up_ref[...], 1, 1, HIGHEST).astype(BF)
        return 0

    lax.fori_loop(0, blocks, step, 0)


def vmem():
    return pl.BlockSpec(memory_space=pltpu.VMEM)


def mixer_forward(proj, lowrank, gate_up, gate_bias, gain):
    rows, (rank, kw), vw = proj.shape[0], gate_up.shape, gain.shape[1]
    blocks = rows // BLOCK
    return pl.pallas_call(
        functools.partial(forward_kernel, kw, vw),
        out_shape=(
            jax.ShapeDtypeStruct((rows, vw), BF),
            jax.ShapeDtypeStruct((rows, vw), BF),
            jax.ShapeDtypeStruct((blocks, vw, kw), BF),
        ),
        in_specs=[vmem()] * 5,
        out_specs=(vmem(),) * 3,
        scratch_shapes=[pltpu.VMEM((vw, kw), F32)],
        compiler_params=pltpu.CompilerParams(vmem_limit_bytes=40 * 2**20),
        cost_estimate=pl.CostEstimate(flops=20_000_000_000, bytes_accessed=10 * 2**20, transcendentals=0),
        name="mixer_forward",
    )(proj, lowrank, gate_up, gate_bias, gain)


def mixer_backward(proj, lowrank, gate_up, gate_bias, gain, mixed, states, grad):
    rows, (rank, kw), vw = proj.shape[0], gate_up.shape, gain.shape[1]
    return pl.pallas_call(
        functools.partial(backward_kernel, kw, vw),
        out_shape=(
            jax.ShapeDtypeStruct(proj.shape, BF),
            jax.ShapeDtypeStruct((rows, rank), BF),
            jax.ShapeDtypeStruct((rank, kw), F32),
            jax.ShapeDtypeStruct((1, kw), F32),
            jax.ShapeDtypeStruct((1, vw), F32),
        ),
        in_specs=[vmem()] * 8,
        out_specs=(vmem(),) * 5,
        scratch_shapes=[pltpu.VMEM((vw, kw), F32)],
        compiler_params=pltpu.CompilerParams(vmem_limit_bytes=40 * 2**20),
        cost_estimate=pl.CostEstimate(flops=40_000_000_000, bytes_accessed=16 * 2**20, transcendentals=0),
        name="mixer_backward",
    )(proj, lowrank, gate_up, gate_bias, gain, mixed, states, grad)


def swap(array, axis, bit):
    size = lax.axis_size(axis)
    return lax.ppermute(array, axis, [(i, i ^ bit) for i in range(size)])


def reorder(array, dim):
    me, size = lax.axis_index("dp"), lax.axis_size("dp")
    width = array.shape[dim] // size
    return jnp.concatenate(
        [lax.dynamic_slice_in_dim(array, (j ^ me) * width, width, dim) for j in range(size)], dim
    )


def bits_of(size):
    return [1 << k for k in range(size.bit_length() - 1)]


def gather_bits(pieces, bits):
    for bit in bits:
        pieces.update({i ^ bit: swap(piece, "dp", bit) for i, piece in list(pieces.items())})
    return pieces


def scatter_bits(pieces, bits):
    for bit in bits:
        for i in [i for i in pieces if i & bit]:
            pieces[i ^ bit] = pieces[i ^ bit] + swap(pieces.pop(i), "dp", bit)
    return pieces


def in_order(pieces, dim):
    return jnp.concatenate([pieces[i] for i in range(len(pieces))], dim)


def cut(array, dim, count):
    return dict(enumerate(jnp.split(array, count, dim)))


def dp_orders():
    bits = bits_of(lax.axis_size("dp"))
    top, middle = bits[-1], bits[1:-1]
    return [[*middle, top, bits[0]], [top, *middle, bits[0]]]


def gather_dp(shard, dim):
    halves = [
        in_order(gather_bits({0: half}, order), dim)
        for half, order in zip(jnp.split(shard, 2, 1 - dim), dp_orders())
    ]
    return jnp.concatenate(halves, 1 - dim)


def scatter_dp(array, dim):
    halves = [
        scatter_bits(cut(half, dim, lax.axis_size("dp")), order[::-1])[0]
        for half, order in zip(jnp.split(array, 2, 1 - dim), dp_orders())
    ]
    return jnp.concatenate(halves, 1 - dim)


def crossed():
    high = lax.axis_index("tensor") // 2
    return high != lax.axis_index("dp") // (lax.axis_size("dp") // 2)


def gather_square(shard, dim):
    other = swap(shard, "tensor", 2)
    mine = jnp.where(crossed(), other, shard)
    give = jnp.where(crossed(), shard, other)
    bits = bits_of(lax.axis_size("dp"))
    pieces = {0: mine, bits[-1]: swap(give, "dp", bits[-1])}
    return in_order(gather_bits(pieces, [*bits[1:-1], bits[0]]), dim)


def scatter_square(array, dim):
    bits = bits_of(lax.axis_size("dp"))
    pieces = scatter_bits(cut(array, dim, lax.axis_size("dp")), [bits[0], *bits[1:-1][::-1]])
    mine, other = pieces[0], swap(pieces[bits[-1]], "dp", bits[-1])
    keep = jnp.where(crossed(), other, mine)
    send = jnp.where(crossed(), mine, other)
    return keep.astype(F32) + swap(send, "tensor", 2).astype(F32)


def across_y(array):
    return swap(array, "dp", lax.axis_size("dp") // 2)


def across_z(array):
    return swap(array, "tensor", 1)


def gather_tokens(own):
    half = own.shape[1] // 2
    left, right = own[:, :half], own[:, half:]
    y_right, z_right = across_y(left), across_z(right)
    z_left, d_right = across_z(left), across_z(y_right)
    y_left, d_left = across_y(right), across_y(z_right)
    return jnp.concatenate(
        [
            own,
            jnp.concatenate([z_left, z_right], 1),
            jnp.concatenate([y_left, y_right], 1),
            jnp.concatenate([d_left, d_right], 1),
        ],
        0,
    )


def scatter_tokens(partial):
    rows, half = partial.shape[0] // 4, partial.shape[1] // 2
    part = lambda r, c: partial[r * rows:(r + 1) * rows, c * half:(c + 1) * half]
    add = lambda a, b: a.astype(F32) + b.astype(F32)
    y_one, y_two = across_y(part(2, 0)), across_y(part(3, 0))
    z_one, z_two = across_z(part(1, 0)), across_z(part(3, 1))
    right = add(part(0, 1), y_one)
    left = add(part(0, 0), z_one)
    right = add(right, across_z(add(part(1, 1), y_two).astype(BF)))
    left = add(left, across_y(add(part(2, 1), z_two).astype(BF)))
    return jnp.concatenate([left, right], 1)


def everywhere(array, axes):
    for axis in axes:
        for bit in bits_of(lax.axis_size(axis)):
            array = array + swap(array, axis, bit)
    return array


def norm_scale(rows):
    return lax.rsqrt(jnp.mean(rows * rows, axis=1, keepdims=True) + EPS_NORM)


def norm_back(grad_normed, rows, scale, gain):
    weighted = grad_normed * gain
    return scale * weighted - rows * scale**3 * jnp.mean(weighted * rows, axis=1, keepdims=True)


def on_device(inputs, norm1_gain, query_weight, key_weight, value_weight, outgate_weight, gate_down,
              gate_up, gate_bias, group_gain, proj_weight, norm2_gain, ffn_gate, ffn_up, ffn_down, cotangent):
    head, heads = lax.axis_index("tensor"), lax.axis_size("tensor")
    own_rows = inputs.shape[0]
    units = ffn_gate.shape[1]
    kw, vw = query_weight.shape[1], value_weight.shape[1]
    inputs = reorder(inputs, 1)
    cotangent = reorder(cotangent, 1)
    gain_one = reorder(norm1_gain[None, :], 1)
    gain_two = reorder(norm2_gain[None, :], 1)
    gate_down = reorder(gate_down, 0)

    inputs_wide = inputs.astype(F32)
    scale_one = norm_scale(inputs_wide)
    normed_one = (inputs_wide * scale_one * gain_one).astype(BF)
    rows_one = lax.all_gather(normed_one, "tensor", axis=0, tiled=True)
    into = gather_dp(jnp.concatenate([query_weight, key_weight, value_weight, outgate_weight], 1), 0)
    shard_proj = jnp.concatenate([proj_weight] + [swap(proj_weight, "tensor", m) for m in range(1, heads)], 0)
    proj_full = gather_dp(shard_proj, 1)
    gate_up_full = gather_square(jnp.concatenate([ffn_gate, ffn_up], 1), 0)
    down_full = gather_square(ffn_down, 1)
    cot_rows = gather_tokens(cotangent)

    projected = matmul(rows_one, into).astype(BF)
    lowrank = matmul(rows_one, gate_down)
    gate_row, gain_row = gate_bias[None, :], group_gain[None, :]
    gated, mixed, states = mixer_forward(projected, lowrank, gate_up, gate_row, gain_row)
    def rows_of(array, index):
        return lax.dynamic_slice_in_dim(array, index * own_rows, own_rows, 0)
    gated_own = jnp.concatenate(
        [rows_of(gated, head)]
        + [swap(rows_of(gated, head ^ m), "tensor", m) for m in range(1, heads)],
        1,
    )
    resid = inputs_wide + matmul(gated_own, proj_full)
    scale_two = norm_scale(resid)
    normed_two = (resid * scale_two * gain_two).astype(BF)

    rows_two = gather_tokens(normed_two)
    pre = matmul(rows_two, gate_up_full)
    gate_pre, up_pre = pre[:, :units], pre[:, units:]
    logistic = sigmoid(gate_pre)
    act = gate_pre * logistic
    hidden = (act * up_pre).astype(BF)
    grad_hidden = times_transposed(cot_rows, down_full)
    grad_up = (grad_hidden * act).astype(BF)
    grad_gate = (grad_hidden * up_pre * (logistic * (1.0 + gate_pre * (1.0 - logistic)))).astype(BF)
    grad_pre = jnp.concatenate([grad_gate, grad_up], 1)
    grad_two = scatter_tokens(times_transposed(grad_pre, gate_up_full).astype(BF))
    norm2_term = jnp.sum(grad_two * resid * scale_two, axis=0, keepdims=True)
    grad_resid = cotangent.astype(F32) + norm_back(grad_two, resid, scale_two, gain_two)
    output = (resid + scatter_tokens(matmul(hidden, down_full).astype(BF))).astype(BF)
    grad_gate_up_own = scatter_square(transposed_times(rows_two, grad_pre).astype(BF), 0)
    grad_down_own = scatter_square(transposed_times(hidden, cot_rows).astype(BF), 1)

    grad_branch = grad_resid.astype(BF)
    grad_gated_own = times_transposed(grad_branch, proj_full).astype(BF)
    pieces = [grad_gated_own[:, m * vw:(m + 1) * vw] for m in range(heads)]
    pieces = jnp.stack([pieces[0]] + [swap(pieces[m], "tensor", m) for m in range(1, heads)], 0)
    grad_gated = jnp.concatenate(
        [lax.dynamic_index_in_dim(pieces, head ^ t, 0, keepdims=False) for t in range(heads)], 0
    )
    grad_into, grad_low, up_term, bias_term, group_term = mixer_backward(
        projected, lowrank, gate_up, gate_row, gain_row, mixed, states, grad_gated
    )
    grad_proj_part = cut(scatter_dp(transposed_times(gated_own, grad_branch).astype(BF), 1), 0, heads)
    grad_proj = grad_proj_part[0].astype(F32)
    for m in range(1, heads):
        grad_proj = grad_proj + swap(grad_proj_part[m], "tensor", m).astype(F32)
    grad_into_own = scatter_dp(transposed_times(rows_one, grad_into).astype(BF), 0).astype(F32)
    total = (times_transposed(grad_into, into) + times_transposed(grad_low, gate_down)).astype(BF)
    norm1_term = jnp.sum(total.astype(F32) * rows_one.astype(F32), axis=0, keepdims=True) / gain_one
    down_term = transposed_times(grad_low, rows_one)
    grad_one = lax.psum_scatter(total, "tensor", scatter_dimension=0, tiled=True).astype(F32)
    grad_input = grad_resid + norm_back(grad_one, inputs_wide, scale_one, gain_one)

    summed = everywhere(reorder(jnp.concatenate([down_term, norm1_term, norm2_term], 0), 1), ("dp", "tensor"))
    rank = gate_down.shape[1]
    by_head = everywhere(
        jnp.concatenate([up_term, bias_term, group_term[:, :kw], group_term[:, kw:]], 0), ("dp",)
    )
    splits = [kw, 2 * kw, 2 * kw + vw]
    grad_query, grad_key, grad_value, grad_outgate = jnp.split(grad_into_own, splits, 1)
    return (
        reorder(output, 1),
        reorder(grad_input, 1),
        summed[rank],
        grad_query,
        grad_key,
        grad_value,
        grad_outgate,
        summed[:rank].T,
        by_head[:rank],
        by_head[rank],
        by_head[rank + 1:].reshape(-1),
        grad_proj,
        summed[rank + 1],
        grad_gate_up_own[:, :units],
        grad_gate_up_own[:, units:],
        grad_down_own,
    )


def solution(mesh):
    tokens, whole = P(("dp", "tensor"), None), P()
    rows, columns = P("dp", "tensor"), P("tensor", "dp")
    last = P(None, "tensor")
    head = P("tensor")
    return jax.shard_map(
        on_device,
        mesh=mesh,
        in_specs=(tokens, whole, rows, rows, rows, rows, whole, last, head, head, columns, whole, rows, rows,
                  columns, tokens),
        out_specs=(tokens, tokens, whole, rows, rows, rows, rows, whole, last, head, head, columns, whole, rows,
                   rows, columns),
        check_vma=False,
    )
```

time: 1600 us -> 977 us (0.61)
  waiting for transfers between devices: 985 us -> 511 us
  matrix products: 361 us -> 157 us
  starting transfers between devices: 2.18 us -> 93.9 us
  blocking collectives: 47.2 us -> 0 us
  Pallas kernels: 0 us -> 36.4 us
  other arithmetic: 76.2 us -> 59.9 us
    ppermute x0 -> x132, waiting for transfers between devices: none -> 511 us  [swap(): return lax.ppermute(array, axis, [(i, i ^ bit) for i in range(size)])]
    reduce_scatter x12 -> x1, waiting for transfers between devices: 468 us -> 0.01 us  [on_device(): lax.psum_scatter(total, 'tensor', scatter_dimension=0, tiled=True)]
    all_gather x11 -> x0, waiting for transfers between devices: 376 us -> none  [the longest x1 82.5 us: on_device(): rows_two = lax.all_gather(normed_two, 'tensor', axis=0, tiled=True)]
    dot_general x238 -> x15, matrix products: 361 us -> 157 us  [dot(): lax.dot_general(a, b, (((ca,), (cb,)), ((), ())), precision=precision, pr...]
    ppermute x0 -> x132, starting transfers between devices: none -> 93.9 us  [swap(): return lax.ppermute(array, axis, [(i, i ^ bit) for i in range(size)])]
    all_gather x1, waiting for transfers between devices: 82.9 us -> 0.01 us  [on_device(): rows_one = lax.all_gather(normed_one, 'tensor', axis=0, tiled=True)]
    squeeze x81 -> x1, local copies, waits for them, and re-layouts: 76.4 us -> 0.08 us  [on_device(): lax.dynamic_index_in_dim(pieces, head ^ t, 0, keepdims=False)]
    unnamed x81 -> x306, local copies, waits for them, and re-layouts: 3.52 us -> 64.7 us
  transfers between devices with their start and end apart: 25 -> 134, of which waited for: 20 -> 42; matrix products, arithmetic and copies ran while one was open for 30% -> 27% of each run, Pallas kernels for 0% -> 4%
where the time goes in v1:
time: 977 us; the launch traced here: 968 us
  waiting for transfers between devices  511 us (52%)
  matrix products  157 us (16%)
  starting transfers between devices  93.9 us (10%)
  local copies, waits for them, and re-layouts  92.4 us (9%)
  other arithmetic  59.9 us (6%)
  Pallas kernels  36.4 us (4%)
  between operations  16.8 us (2%)
    ppermute x132, waiting for transfers between devices, swap(): return lax.ppermute(array, axis, [(i, i ^ bit) for i in range(size)])  511 us
    dot_general x15, matrix products, dot(): lax.dot_general(a, b, (((ca,), (cb,)), ((), ())), precision=precision, pr...  157 us
    ppermute x132, starting transfers between devices, swap(): return lax.ppermute(array, axis, [(i, i ^ bit) for i in range(size)])  93.9 us
    unnamed x306, local copies, waits for them, and re-layouts  64.7 us
    pallas_call x1, Pallas kernels, mixer_backward(): pl.pallas_call(functools.partial(backward_kernel, kw, vw), out_shape=(jax...  22.6 us
    add x16, other arithmetic, scatter_bits(): pieces[i ^ bit] = pieces[i ^ bit] + swap(pieces.pop(i), 'dp', bit)  22.3 us
  transfers between devices with their start and end apart: 134, of which 42 were waited for; matrix products, arithmetic and copies ran while one was open for 27% of the time, Pallas kernels for 4%

profile of v1, /device:TPU:0, one launch (start us, length us, event | category | flops | bytes accessed | tf_op | source)
XLA Modules:
  0.0 968.0 jit_solution(9688990805380155310)
XLA Ops:
  7.2 4.1 collective-permute-start.25
  54.4 60.1 %collective-permute-done.48 = bf16[1408,256]{1,0:T(8,128)(2,1)S(1)} collective-permute-done((bf16[1408,256]{1,0:T(8,128)(2,1)}, bf16[1408,256]{1,0:T(8,128)(2,1)S(1)}, u32[]{:S(2)}, u32[]{:S(2)}) %collective-permute-start.48) | collective-permute-done | bytes 720928 | tf_op jit(solution)/shard_map/ppermute | solution.py:200
  119.2 10.2 %collective-permute-done.19 = bf16[1024,256]{1,0:T(8,128)(2,1)S(1)} collective-permute-done((bf16[1024,256]{1,0:T(8,128)(2,1)}, bf16[1024,256]{1,0:T(8,128)(2,1)S(1)}, u32[]{:S(2)}, u32[]{:S(2)}) %collective-permute-start.19) | collective-permute-done | bytes 524320 | tf_op jit(solution)/shard_map/ppermute | solution.py:200
  137.2 4.3 collective-permute-done.5
  145.4 7.3 collective-permute-done.30
  157.3 4.5 collective-permute-done.21
  165.7 10.9 %collective-permute-done.32 = bf16[1024,256]{1,0:T(8,128)(2,1)S(1)} collective-permute-done((bf16[1024,256]{1,0:T(8,128)(2,1)S(1)}, bf16[1024,256]{1,0:T(8,128)(2,1)S(1)}, u32[]{:S(2)}, u32[]{:S(2)}) %collective-permute-start.32) | collective-permute-done | bytes 524320 | tf_op jit(solution)/shard_map/ppermute | solution.py:200
  178.7 37.0 %collective-permute-done.40 = bf16[256,2816]{1,0:T(8,128)(2,1)S(1)} collective-permute-done((bf16[256,2816]{1,0:T(8,128)(2,1)S(1)}, bf16[256,2816]{1,0:T(8,128)(2,1)S(1)}, u32[]{:S(2)}, u32[]{:S(2)}) %collective-permute-start.40) | collective-permute-done | bytes 1441824 | tf_op jit(solution)/shard_map/ppermute | solution.py:200
  222.4 44.5 %collective-permute-done.54 = bf16[1408,256]{1,0:T(8,128)(2,1)S(1)} collective-permute-done((bf16[1408,256]{1,0:T(8,128)(2,1)S(1)}, bf16[1408,256]{1,0:T(8,128)(2,1)S(1)}, u32[]{:S(2)}, u32[]{:S(2)}) %collective-permute-start.54) | collective-permute-done | bytes 720928 | tf_op jit(solution)/shard_map/ppermute | solution.py:200
  278.9 10.0 %fusion.5.proj_ref = bf16[1024,1536]{1,0:T(8,128)(2,1)S(1)} fusion(bf16[1024,2048]{1,0:T(8,128)(2,1)S(1)} %copy-done.22, bf16[2048,768]{1,0:T(8,128)(2,1)} %constant_dynamic-update-slice_fusion.24, bf16[2048,768]{1,0:T(8,128)(2,1)} %constant_dynamic-update-slice_fusion.16), kind=kOutput, calls=%fused_computation.26 | convolution fusion | flops 6456606720 | bytes 13631488 | tf_op jit(solution)/shard_map/dot_general | solution.py:20
  288.9 13.9 %mixer_forward.1 = (bf16[1024,512]{1,0:T(8,128)(2,1)S(1)}, bf16[1024,512]{1,0:T(8,128)(2,1)S(1)}, bf16[16,512,256]{2,1,0:T(8,128)(2,1)S(1)}) custom-call(bf16[1024,1536]{1,0:T(8,128)(2,1)S(1)} %fusion.5.proj_ref, f32[1024,16]{1,0:T(8,128)S(1)} %fusion.57.low_ref, f32[16,256]{1,0:T(8,128)S(1)} %copy-done, f32[1,256]{1,0:T(1,128)S(1)} %bitcast.61, ...), custom_call_target="tpu_custom_call" | custom-call | flops 20000000000 | bytes 10485760 | tf_op jit(solution)/shard_map/mixer_forward/pallas_call | solution.py:162
  310.0 4.1 collective-permute-done.16
  314.1 13.2 %collective-permute-done.15 = bf16[256,512]{1,0:T(8,128)(2,1)S(1)} collective-permute-done((bf16[256,512]{1,0:T(8,128)(2,1)S(1)}, bf16[256,512]{1,0:T(8,128)(2,1)S(1)}, u32[]{:S(2)}, u32[]{:S(2)}) %collective-permute-start.15) | collective-permute-done | bytes 262176 | tf_op jit(solution)/shard_map/ppermute | solution.py:200
  339.6 6.9 collective-permute-done.37
  352.3 6.5 collective-permute-done.63
  359.8 10.2 %collective-permute-done.34 = bf16[256,1024]{1,0:T(8,128)(2,1)S(1)} collective-permute-done((bf16[256,1024]{1,0:T(8,128)(2,1)S(1)}, bf16[256,1024]{1,0:T(8,128)(2,1)S(1)}, u32[]{:S(2)}, u32[]{:S(2)}) %collective-permute-start.34) | collective-permute-done | bytes 524320 | tf_op jit(solution)/shard_map/ppermute | solution.py:200
  370.0 11.2 %collective-permute-done.39 = bf16[256,1024]{1,0:T(8,128)(2,1)S(1)} collective-permute-done((bf16[256,1024]{1,0:T(8,128)(2,1)S(1)}, bf16[256,1024]{1,0:T(8,128)(2,1)S(1)}, u32[]{:S(2)}, u32[]{:S(2)}) %collective-permute-start.39) | collective-permute-done | bytes 524320 | tf_op jit(solution)/shard_map/ppermute | solution.py:200
  382.3 38.4 %fusion.42 = f32[1024,2816]{1,0:T(8,128)} fusion(bf16[2048,2816]{1,0:T(8,128)(2,1)} %constant_dynamic-update-slice_fusion.72, bf16[256,1024]{1,0:T(8,128)(2,1)S(1)} %collective-permute-done.39, bf16[256,1024]{1,0:T(8,128)(2,1)S(1)} %collective-permute-done.38, bf16[256,1024]{1,0:T(8,128)(2,1)S(1)} %collective-permute-done.37, ...), kind=kOutput, calls=%fused_computation.280 | convolution fusion | flops 11840520192 | bytes 27262976 | tf_op jit(solution)/shard_map/dot_general | solution.py:20
  422.7 18.6 %multiply_convert_fusion.1 = (bf16[1024,1408]{1,0:T(8,128)(2,1)}, bf16[1024,1408]{1,0:T(8,128)(2,1)}, bf16[1024,1408]{1,0:T(8,128)(2,1)}) fusion(f32[1024,2816]{1,0:T(8,128)} %fusion.42, bf16[1408,2048]{1,0:T(8,128)(2,1)} %copy-done.68, bf16[256,1024]{1,0:T(8,128)(2,1)} %copy-done.100, bf16[256,1024]{1,0:T(8,128)(2,1)} %copy-done.101, ...), kind=kOutput, calls=%fused_computation.10 | convolution fusion | flops 5956567040 | bytes 30146560 | tf_op jit(solution)/shard_map/dot_general | solution.py:20
  441.3 16.7 %convolution_convert_fusion.4 = bf16[1024,2048]{1,0:T(8,128)(2,1)S(1)} fusion(bf16[2048,2816]{1,0:T(8,128)(2,1)} %constant_dynamic-update-slice_fusion.72, bf16[1024,1408]{1,0:T(8,128)(2,1)} %get-tuple-element.75, bf16[1024,1408]{1,0:T(8,128)(2,1)} %get-tuple-element.74), kind=kOutput, calls=%fused_computation.25 | convolution fusion | flops 11824791552 | bytes 21495808 | tf_op jit(solution)/shard_map/dot_general | solution.py:20
  462.5 9.1 convolution_convert_fusion.5
  473.1 9.8 %convolution_convert_fusion.1 = bf16[1408,2048]{1,0:T(8,128)(2,1)S(1)} fusion(bf16[1024,1408]{1,0:T(8,128)(2,1)} %get-tuple-element.82, bf16[256,1024]{1,0:T(8,128)(2,1)} %copy-done.100, bf16[256,1024]{1,0:T(8,128)(2,1)} %copy-done.101, bf16[256,1024]{1,0:T(8,128)(2,1)} %collective-permute-done.65, bf16[256,1024]{1,0:T(8,128)(2,1)} %copy-done.98, ...), kind=kOutput, calls=%fused_computation.4 | convolution fusion | flops 5937823744 | bytes 12845056 | tf_op jit(solution)/shard_map/dot_general | solution.py:20
  487.0 20.7 %convolution_convert_fusion = bf16[2048,2816]{1,0:T(8,128)(2,1)} fusion(bf16[1024,1408]{1,0:T(8,128)(2,1)} %get-tuple-element.75, bf16[1024,1408]{1,0:T(8,128)(2,1)} %get-tuple-element.74, bf16[256,1024]{1,0:T(8,128)(2,1)} %copy-done.96, bf16[256,1024]{1,0:T(8,128)(2,1)} %copy-done.97, bf16[256,1024]{1,0:T(8,128)(2,1)} %copy-done.91, ...), kind=kOutput, calls=%fused_computation | convolution fusion | flops 11857821696 | bytes 21495808 | tf_op jit(solution)/shard_map/dot_general | solution.py:20
  510.8 5.1 fusion.44
  519.2 5.4 collective-permute-done.70
  531.6 4.3 collective-permute-done.60
  536.8 10.3 %collective-permute-done.58 = bf16[256,1024]{1,0:T(8,128)(2,1)S(1)} collective-permute-done((bf16[256,1024]{1,0:T(8,128)(2,1)S(1)}, bf16[256,1024]{1,0:T(8,128)(2,1)S(1)}, u32[]{:S(2)}, u32[]{:S(2)}) %collective-permute-start.58) | collective-permute-done | bytes 524320 | tf_op jit(solution)/shard_map/ppermute | solution.py:200
  554.1 13.1 %collective-permute-done.126 = bf16[1408,256]{1,0:T(8,128)(2,1)S(1)} collective-permute-done((bf16[1408,256]{1,0:T(8,128)(2,1)S(1)}, bf16[1408,256]{1,0:T(8,128)(2,1)S(1)}, u32[]{:S(2)}, u32[]{:S(2)}) %collective-permute-start.126) | collective-permute-done | bytes 720928 | tf_op jit(solution)/shard_map/ppermute | solution.py:200
  571.3 10.7 %collective-permute-done.73 = bf16[256,1024]{1,0:T(8,128)(2,1)S(1)} collective-permute-done((bf16[256,1024]{1,0:T(8,128)(2,1)S(1)}, bf16[256,1024]{1,0:T(8,128)(2,1)S(1)}, u32[]{:S(2)}, u32[]{:S(2)}) %collective-permute-start.73) | collective-permute-done | bytes 524320 | tf_op jit(solution)/shard_map/ppermute | solution.py:200
  584.0 6.6 collective-permute-done.61
  609.1 11.9 %collective-permute-done.75 = bf16[256,512]{1,0:T(8,128)(2,1)S(1)} collective-permute-done((bf16[256,512]{1,0:T(8,128)(2,1)S(1)}, bf16[256,512]{1,0:T(8,128)(2,1)S(1)}, u32[]{:S(2)}, u32[]{:S(2)}) %collective-permute-start.75) | collective-permute-done | bytes 262176 | tf_op jit(solution)/shard_map/ppermute | solution.py:200
  621.4 22.6 %mixer_backward.1 = (bf16[1024,1536]{1,0:T(8,128)(2,1)S(1)}, bf16[1024,16]{1,0:T(8,128)(2,1)S(1)}, f32[16,256]{1,0:T(8,128)S(1)}, f32[1,256]{1,0:T(1,128)S(1)}, f32[1,512]{1,0:T(1,128)S(1)}) custom-call(bf16[1024,1536]{1,0:T(8,128)(2,1)S(1)} %copy-done.9, f32[1024,16]{1,0:T(8,128)S(1)} %copy-done.7, f32[16,256]{1,0:T(8,128)S(1)} %copy-done.1, ...), custom_call_target="tpu_custom_call" | custom-call | flops 40000000000 | bytes 16777216 | tf_op jit(solution)/shard_map/mixer_backward/pallas_call | solution.py:180
  645.2 11.1 %multiply_reduce_fusion = (f32[2048]{0:T(1024)S(1)}, bf16[1024,2048]{1,0:T(8,128)(2,1)}) fusion(bf16[1024,2048]{1,0:T(8,128)(2,1)} %all-gather.2.cloned.1.call-done, f32[1024,2048]{1,0:T(8,128)S(1)} %fusion.58, bf16[1024,1536]{1,0:T(8,128)(2,1)S(1)} %get-tuple-element.27, bf16[2048,768]{1,0:T(8,128)(2,1)} %constant_dynamic-update-slice_fusion.24, ...), kind=kOutput, calls=%fused_computation.2 | convolution fusion | flops 6467614720 | bytes 26222592 | tf_op jit(solution)/shard_map/dot_general | solution.py:20
  660.3 7.7 convolution_convert_fusion.3
  688.2 17.7 %collective-permute-done.79 = f32[18,2048]{1,0:T(8,128)S(1)} collective-permute-done((f32[18,2048]{1,0:T(8,128)S(1)}, f32[18,2048]{1,0:T(8,128)S(1)}, u32[]{:S(2)}, u32[]{:S(2)}) %collective-permute-start.79) | collective-permute-done | bytes 147488 | tf_op jit(solution)/shard_map/ppermute | solution.py:200
  710.3 4.0 collective-permute-done.87
  716.3 13.4 %collective-permute-done.80 = f32[18,2048]{1,0:T(8,128)S(1)} collective-permute-done((f32[18,2048]{1,0:T(8,128)S(1)}, f32[18,2048]{1,0:T(8,128)S(1)}, u32[]{:S(2)}, u32[]{:S(2)}) %collective-permute-start.80) | collective-permute-done | bytes 147488 | tf_op jit(solution)/shard_map/ppermute | solution.py:200
  735.8 23.8 %collective-permute-done.81 = f32[18,2048]{1,0:T(8,128)S(1)} collective-permute-done((f32[18,2048]{1,0:T(8,128)S(1)}, f32[18,2048]{1,0:T(8,128)S(1)}, u32[]{:S(2)}, u32[]{:S(2)}) %collective-permute-start.81) | collective-permute-done | bytes 147488 | tf_op jit(solution)/shard_map/ppermute | solution.py:200
  763.3 10.7 %collective-permute-done.101 = bf16[1024,256]{1,0:T(8,128)(2,1)S(1)} collective-permute-done((bf16[1024,256]{1,0:T(8,128)(2,1)S(1)}, bf16[1024,256]{1,0:T(8,128)(2,1)S(1)}, u32[]{:S(2)}, u32[]{:S(2)}) %collective-permute-start.101) | collective-permute-done | bytes 524320 | tf_op jit(solution)/shard_map/ppermute | solution.py:200
  774.0 7.4 collective-permute-done.105
  792.1 36.2 %collective-permute-done.94 = bf16[256,768]{0,1:T(8,128)(2,1)S(1)} collective-permute-done((bf16[256,768]{0,1:T(8,128)(2,1)S(1)}, bf16[256,768]{0,1:T(8,128)(2,1)S(1)}, u32[]{:S(2)}, u32[]{:S(2)}) %collective-permute-start.94) | collective-permute-done | bytes 393248 | tf_op jit(solution)/shard_map/ppermute | solution.py:200
  830.9 11.1 %collective-permute-done.112 = bf16[1024,256]{1,0:T(8,128)(2,1)S(1)} collective-permute-done((bf16[1024,256]{1,0:T(8,128)(2,1)S(1)}, bf16[1024,256]{1,0:T(8,128)(2,1)S(1)}, u32[]{:S(2)}, u32[]{:S(2)}) %collective-permute-start.112) | collective-permute-done | bytes 524320 | tf_op jit(solution)/shard_map/ppermute | solution.py:200
  848.5 12.7 %collective-permute-done.131 = bf16[1408,256]{1,0:T(8,128)(2,1)S(1)} collective-permute-done((bf16[1408,256]{1,0:T(8,128)(2,1)S(1)}, bf16[1408,256]{1,0:T(8,128)(2,1)S(1)}, u32[]{:S(2)}, u32[]{:S(2)}) %collective-permute-start.131) | collective-permute-done | bytes 720928 | tf_op jit(solution)/shard_map/ppermute | solution.py:200
  866.6 6.6 collective-permute-done.95
  873.3 10.2 %collective-permute-done.113 = bf16[1024,256]{1,0:T(8,128)(2,1)S(1)} collective-permute-done((bf16[1024,256]{1,0:T(8,128)(2,1)S(1)}, bf16[1024,256]{1,0:T(8,128)(2,1)S(1)}, u32[]{:S(2)}, u32[]{:S(2)}) %collective-permute-start.113) | collective-permute-done | bytes 524320 | tf_op jit(solution)/shard_map/ppermute | solution.py:200
  897.0 4.2 collective-permute-done.106
  901.2 8.5 collective-permute-done.115
  909.7 39.4 %collective-permute-done.114 = bf16[512,256]{1,0:T(8,128)(2,1)} collective-permute-done((bf16[512,256]{1,0:T(8,128)(2,1)}, bf16[512,256]{1,0:T(8,128)(2,1)}, u32[]{:S(2)}, u32[]{:S(2)}) %collective-permute-start.114) | collective-permute-done | bytes 262176 | tf_op jit(solution)/shard_map/ppermute | solution.py:200
  (640 shorter events, 264.5 us)
Async XLA Ops:
  7.2 268.1 %all-gather.2.cloned.1.call-start = ((), (), s32[]{:S(2)}) async-start(), calls=%async_computation.1 | async-start | bytes 5242880 | tf_op jit(solution)/shard_map/all_gather | solution.py:350
  15.4 32.2 %collective-permute-start.8 = (bf16[256,768]{1,0:T(8,128)(2,1)}, bf16[256,768]{1,0:T(8,128)(2,1)}, u32[]{:S(2)}, u32[]{:S(2)}) collective-permute-start(bf16[256,768]{1,0:T(8,128)(2,1)} %get-tuple-element.154), channel_id=1, source_target_pairs={{0,8},{4,12},{8,0},{12,4},{16,24},{20,28},{24,16},{28,20},{1,9},{5... | collective-permute-start | bytes 1179656 | tf_op jit(solution)/shard_map/ppermute | solution.py:200
  27.5 928.1 %reduce-scatter.2.cloned.1.call-start = ((), (), s32[]{:S(2)}) async-start(), calls=%async_computation.2 | async-start | bytes 5242880 | tf_op jit(solution)/shard_map/reduce_scatter | solution.py:408
  37.9 76.6 %collective-permute-start.48 = (bf16[1408,256]{1,0:T(8,128)(2,1)}, bf16[1408,256]{1,0:T(8,128)(2,1)S(1)}, u32[]{:S(2)}, u32[]{:S(2)}) collective-permute-start(bf16[1408,256]{1,0:T(8,128)(2,1)} %param.30), channel_id=1, source_target_pairs={{0,2},{1,3},{2,0},{3,1},{4,6},{5,7},{6,4},{7,5},{8,10},{9,11},{10,... | collective-permute-start | bytes 2162696 | tf_op jit(solution)/shard_map/ppermute | solution.py:200
  44.2 72.1 %collective-permute-start.10 = (bf16[256,768]{1,0:T(8,128)(2,1)}, bf16[256,768]{1,0:T(8,128)(2,1)S(1)}, u32[]{:S(2)}, u32[]{:S(2)}) collective-permute-start(bf16[256,768]{1,0:T(8,128)(2,1)} %get-tuple-element.154), channel_id=1, source_target_pairs={{0,16},{4,20},{8,24},{12,28},{16,0},{20,4},{24,8},{28,12},{1,17},{... | collective-permute-start | bytes 1179656 | tf_op jit(solution)/shard_map/ppermute | solution.py:200
  47.5 70.4 %collective-permute-start.27 = (bf16[1024,256]{1,0:T(8,128)(2,1)S(1)}, bf16[1024,256]{1,0:T(8,128)(2,1)S(1)}, u32[]{:S(2)}, u32[]{:S(2)}) collective-permute-start(bf16[1024,256]{1,0:T(8,128)(2,1)S(1)} %get-tuple-element.159), channel_id=1, source_target_pairs={{0,4},{4,0},{8,12},{12,8},{16,20},{20,16},{24,28},{28,24},{1,5},{5... | collective-permute-start | bytes 1572872 | tf_op jit(solution)/shard_map/ppermute | solution.py:200
  49.4 68.5 %collective-permute-start.28 = (bf16[1024,256]{1,0:T(8,128)(2,1)S(1)}, bf16[1024,256]{1,0:T(8,128)(2,1)S(1)}, u32[]{:S(2)}, u32[]{:S(2)}) collective-permute-start(bf16[1024,256]{1,0:T(8,128)(2,1)S(1)} %get-tuple-element.159), channel_id=1, source_target_pairs={{0,8},{4,12},{8,0},{12,4},{16,24},{20,28},{24,16},{28,20},{1,9},{5... | collective-permute-start | bytes 1572872 | tf_op jit(solution)/shard_map/ppermute | solution.py:200
  53.6 65.0 %collective-permute-start.18 = (bf16[1024,256]{1,0:T(8,128)(2,1)}, bf16[1024,256]{1,0:T(8,128)(2,1)S(1)}, u32[]{:S(2)}, u32[]{:S(2)}) collective-permute-start(bf16[1024,256]{1,0:T(8,128)(2,1)} %get-tuple-element.155), channel_id=1, source_target_pairs={{0,4},{4,0},{8,12},{12,8},{16,20},{20,16},{24,28},{28,24},{1,5},{5... | collective-permute-start | bytes 1572872 | tf_op jit(solution)/shard_map/ppermute | solution.py:200
  153.5 62.1 %collective-permute-start.40 = (bf16[256,2816]{1,0:T(8,128)(2,1)S(1)}, bf16[256,2816]{1,0:T(8,128)(2,1)S(1)}, u32[]{:S(2)}, u32[]{:S(2)}) collective-permute-start(bf16[256,2816]{1,0:T(8,128)(2,1)S(1)} %constant_dynamic-update-slice_fusion.70), channel_id=1, source_target_pairs={{0,2},{1,3},{2,0},{3,1},{4,6},{5,7},{6,4},{7,5},{8,10},{9,11},{10,... | collective-permute-start | bytes 4325384 | tf_op jit(solution)/shard_map/ppermute | solution.py:200
  163.4 52.3 %collective-permute-start.50 = (bf16[1408,256]{1,0:T(8,128)(2,1)S(1)}, bf16[1408,256]{1,0:T(8,128)(2,1)S(1)}, u32[]{:S(2)}, u32[]{:S(2)}) collective-permute-start(bf16[1408,256]{1,0:T(8,128)(2,1)S(1)} %get-tuple-element.67), channel_id=1, source_target_pairs={{0,8},{4,12},{8,0},{12,4},{16,24},{20,28},{24,16},{28,20},{1,9},{5... | collective-permute-start | bytes 2162696 | tf_op jit(solution)/shard_map/ppermute | solution.py:200
  176.6 41.2 %collective-permute-start.49 = (bf16[1408,256]{1,0:T(8,128)(2,1)S(1)}, bf16[1408,256]{1,0:T(8,128)(2,1)S(1)}, u32[]{:S(2)}, u32[]{:S(2)}) collective-permute-start(bf16[1408,256]{1,0:T(8,128)(2,1)S(1)} %get-tuple-element.67), channel_id=1, source_target_pairs={{0,4},{4,0},{8,12},{12,8},{16,20},{20,16},{24,28},{28,24},{1,5},{5... | collective-permute-start | bytes 2162696 | tf_op jit(solution)/shard_map/ppermute | solution.py:200
  176.7 41.6 %collective-permute-start.52 = (bf16[1408,256]{1,0:T(8,128)(2,1)S(1)}, bf16[1408,256]{1,0:T(8,128)(2,1)S(1)}, u32[]{:S(2)}, u32[]{:S(2)}) collective-permute-start(bf16[1408,256]{1,0:T(8,128)(2,1)S(1)} %get-tuple-element.132), channel_id=1, source_target_pairs={{0,16},{4,20},{8,24},{12,28},{16,0},{20,4},{24,8},{28,12},{1,17},{... | collective-permute-start | bytes 2162696 | tf_op jit(solution)/shard_map/ppermute | solution.py:200
  178.3 41.6 %collective-permute-start.33 = (bf16[1024,256]{1,0:T(8,128)(2,1)S(1)}, bf16[1024,256]{1,0:T(8,128)(2,1)S(1)}, u32[]{:S(2)}, u32[]{:S(2)}) collective-permute-start(bf16[1024,256]{1,0:T(8,128)(2,1)S(1)} %collective-permute-done.32), channel_id=1, source_target_pairs={{0,4},{4,0},{8,12},{12,8},{16,20},{20,16},{24,28},{28,24},{1,5},{5... | collective-permute-start | bytes 1572872 | tf_op jit(solution)/shard_map/ppermute | solution.py:200
  217.8 51.0 %collective-permute-start.42 = (bf16[256,2816]{1,0:T(8,128)(2,1)S(1)}, bf16[256,2816]{1,0:T(8,128)(2,1)}, u32[]{:S(2)}, u32[]{:S(2)}) collective-permute-start(bf16[256,2816]{1,0:T(8,128)(2,1)S(1)} %get-tuple-element.69), channel_id=1, source_target_pairs={{0,8},{4,12},{8,0},{12,4},{16,24},{20,28},{24,16},{28,20},{1,9},{5... | collective-permute-start | bytes 4325384 | tf_op jit(solution)/shard_map/ppermute | solution.py:200
  218.3 48.5 %collective-permute-start.54 = (bf16[1408,256]{1,0:T(8,128)(2,1)S(1)}, bf16[1408,256]{1,0:T(8,128)(2,1)S(1)}, u32[]{:S(2)}, u32[]{:S(2)}) collective-permute-start(bf16[1408,256]{1,0:T(8,128)(2,1)S(1)} %collective-permute-done.52), channel_id=1, source_target_pairs={{0,8},{4,12},{8,0},{12,4},{16,24},{20,28},{24,16},{28,20},{1,9},{5... | collective-permute-start | bytes 2162696 | tf_op jit(solution)/shard_map/ppermute | solution.py:200
  219.9 49.2 %collective-permute-start.44 = (bf16[256,2816]{1,0:T(8,128)(2,1)S(1)}, bf16[256,2816]{1,0:T(8,128)(2,1)}, u32[]{:S(2)}, u32[]{:S(2)}) collective-permute-start(bf16[256,2816]{1,0:T(8,128)(2,1)S(1)} %get-tuple-element.129), channel_id=1, source_target_pairs={{0,16},{4,20},{8,24},{12,28},{16,0},{20,4},{24,8},{28,12},{1,17},{... | collective-permute-start | bytes 4325384 | tf_op jit(solution)/shard_map/ppermute | solution.py:200
  221.6 48.1 %collective-permute-start.41 = (bf16[256,2816]{1,0:T(8,128)(2,1)S(1)}, bf16[256,2816]{1,0:T(8,128)(2,1)S(1)}, u32[]{:S(2)}, u32[]{:S(2)}) collective-permute-start(bf16[256,2816]{1,0:T(8,128)(2,1)S(1)} %get-tuple-element.69), channel_id=1, source_target_pairs={{0,4},{4,0},{8,12},{12,8},{16,20},{20,16},{24,28},{28,24},{1,5},{5... | collective-permute-start | bytes 4325384 | tf_op jit(solution)/shard_map/ppermute | solution.py:200
  221.7 45.3 %collective-permute-start.53 = (bf16[1408,256]{1,0:T(8,128)(2,1)S(1)}, bf16[1408,256]{1,0:T(8,128)(2,1)S(1)}, u32[]{:S(2)}, u32[]{:S(2)}) collective-permute-start(bf16[1408,256]{1,0:T(8,128)(2,1)S(1)} %collective-permute-done.52), channel_id=1, source_target_pairs={{0,4},{4,0},{8,12},{12,8},{16,20},{20,16},{24,28},{28,24},{1,5},{5... | collective-permute-start | bytes 2162696 | tf_op jit(solution)/shard_map/ppermute | solution.py:200
  267.0 71.5 %collective-permute-start.65 = (bf16[256,1024]{1,0:T(8,128)(2,1)}, bf16[256,1024]{1,0:T(8,128)(2,1)}, u32[]{:S(2)}, u32[]{:S(2)}) collective-permute-start(bf16[256,1024]{1,0:T(8,128)(2,1)} %pad_maximum_fusion.21), channel_id=1, source_target_pairs={{0,16},{4,20},{8,24},{12,28},{16,0},{20,4},{24,8},{28,12},{1,17},{... | collective-permute-start | bytes 1572872 | tf_op jit(solution)/shard_map/ppermute | solution.py:200
  268.8 36.8 %collective-permute-start.43 = (bf16[256,2816]{1,0:T(8,128)(2,1)}, bf16[256,2816]{1,0:T(8,128)(2,1)}, u32[]{:S(2)}, u32[]{:S(2)}) collective-permute-start(bf16[256,2816]{1,0:T(8,128)(2,1)} %collective-permute-done.42), channel_id=1, source_target_pairs={{0,4},{4,0},{8,12},{12,8},{16,20},{20,16},{24,28},{28,24},{1,5},{5... | collective-permute-start | bytes 4325384 | tf_op jit(solution)/shard_map/ppermute | solution.py:200
  269.1 40.9 %collective-permute-start.46 = (bf16[256,2816]{1,0:T(8,128)(2,1)}, bf16[256,2816]{1,0:T(8,128)(2,1)}, u32[]{:S(2)}, u32[]{:S(2)}) collective-permute-start(bf16[256,2816]{1,0:T(8,128)(2,1)} %collective-permute-done.44), channel_id=1, source_target_pairs={{0,8},{4,12},{8,0},{12,4},{16,24},{20,28},{24,16},{28,20},{1,9},{5... | collective-permute-start | bytes 4325384 | tf_op jit(solution)/shard_map/ppermute | solution.py:200
  346.5 34.7 %collective-permute-start.39 = (bf16[256,1024]{1,0:T(8,128)(2,1)S(1)}, bf16[256,1024]{1,0:T(8,128)(2,1)S(1)}, u32[]{:S(2)}, u32[]{:S(2)}) collective-permute-start(bf16[256,1024]{1,0:T(8,128)(2,1)S(1)} %collective-permute-done.37), channel_id=1, source_target_pairs={{0,1},{1,0},{2,3},{3,2},{4,5},{5,4},{6,7},{7,6},{8,9},{9,8},{10,11... | collective-permute-start | bytes 1572872 | tf_op jit(solution)/shard_map/ppermute | solution.py:200
  347.5 34.7 %collective-permute-start.38 = (bf16[256,1024]{1,0:T(8,128)(2,1)S(1)}, bf16[256,1024]{1,0:T(8,128)(2,1)S(1)}, u32[]{:S(2)}, u32[]{:S(2)}) collective-permute-start(bf16[256,1024]{1,0:T(8,128)(2,1)S(1)} %collective-permute-done.35), channel_id=1, source_target_pairs={{0,16},{4,20},{8,24},{12,28},{16,0},{20,4},{24,8},{28,12},{1,17},{... | collective-permute-start | bytes 1572872 | tf_op jit(solution)/shard_map/ppermute | solution.py:200
  358.8 61.9 %collective-permute-start.64 = (bf16[256,1024]{1,0:T(8,128)(2,1)S(1)}, bf16[256,1024]{1,0:T(8,128)(2,1)S(1)}, u32[]{:S(2)}, u32[]{:S(2)}) collective-permute-start(bf16[256,1024]{1,0:T(8,128)(2,1)S(1)} %copy-done.46), channel_id=1, source_target_pairs={{0,16},{4,20},{8,24},{12,28},{16,0},{20,4},{24,8},{28,12},{1,17},{... | collective-permute-start | bytes 1572872 | tf_op jit(solution)/shard_map/ppermute | solution.py:200
  359.8 61.0 %collective-permute-start.62 = (bf16[256,1024]{1,0:T(8,128)(2,1)}, bf16[256,1024]{1,0:T(8,128)(2,1)S(1)}, u32[]{:S(2)}, u32[]{:S(2)}) collective-permute-start(bf16[256,1024]{1,0:T(8,128)(2,1)} %pad_maximum_fusion.21), channel_id=1, source_target_pairs={{0,1},{1,0},{2,3},{3,2},{4,5},{5,4},{6,7},{7,6},{8,9},{9,8},{10,11... | collective-permute-start | bytes 1572872 | tf_op jit(solution)/shard_map/ppermute | solution.py:200
  370.0 50.7 %collective-permute-start.67 = (bf16[256,1024]{1,0:T(8,128)(2,1)}, bf16[256,1024]{1,0:T(8,128)(2,1)S(1)}, u32[]{:S(2)}, u32[]{:S(2)}) collective-permute-start(bf16[256,1024]{1,0:T(8,128)(2,1)} %collective-permute-done.65), channel_id=1, source_target_pairs={{0,1},{1,0},{2,3},{3,2},{4,5},{5,4},{6,7},{7,6},{8,9},{9,8},{10,11... | collective-permute-start | bytes 1572872 | tf_op jit(solution)/shard_map/ppermute | solution.py:200
  381.3 39.5 %collective-permute-start.66 = (bf16[256,1024]{1,0:T(8,128)(2,1)S(1)}, bf16[256,1024]{1,0:T(8,128)(2,1)S(1)}, u32[]{:S(2)}, u32[]{:S(2)}) collective-permute-start(bf16[256,1024]{1,0:T(8,128)(2,1)S(1)} %collective-permute-done.63), channel_id=1, source_target_pairs={{0,16},{4,20},{8,24},{12,28},{16,0},{20,4},{24,8},{28,12},{1,17},{... | collective-permute-start | bytes 1572872 | tf_op jit(solution)/shard_map/ppermute | solution.py:200
  459.4 48.4 %collective-permute-start.69 = (bf16[256,1024]{1,0:T(8,128)(2,1)}, bf16[256,1024]{1,0:T(8,128)(2,1)}, u32[]{:S(2)}, u32[]{:S(2)}) collective-permute-start(bf16[256,1024]{1,0:T(8,128)(2,1)} %get-tuple-element.120), channel_id=1, source_target_pairs={{0,1},{1,0},{2,3},{3,2},{4,5},{5,4},{6,7},{7,6},{8,9},{9,8},{10,11... | collective-permute-start | bytes 1572872 | tf_op jit(solution)/shard_map/ppermute | solution.py:200
  459.4 50.4 %collective-permute-start.68 = (bf16[256,1024]{1,0:T(8,128)(2,1)}, bf16[256,1024]{1,0:T(8,128)(2,1)}, u32[]{:S(2)}, u32[]{:S(2)}) collective-permute-start(bf16[256,1024]{1,0:T(8,128)(2,1)} %get-tuple-element.117), channel_id=1, source_target_pairs={{0,1},{1,0},{2,3},{3,2},{4,5},{5,4},{6,7},{7,6},{8,9},{9,8},{10,11... | collective-permute-start | bytes 1572872 | tf_op jit(solution)/shard_map/ppermute | solution.py:200
  461.4 54.5 %collective-permute-start.72 = (bf16[256,1024]{1,0:T(8,128)(2,1)}, bf16[256,1024]{1,0:T(8,128)(2,1)}, u32[]{:S(2)}, u32[]{:S(2)}) collective-permute-start(bf16[256,1024]{1,0:T(8,128)(2,1)} %get-tuple-element.118), channel_id=1, source_target_pairs={{0,16},{4,20},{8,24},{12,28},{16,0},{20,4},{24,8},{28,12},{1,17},{... | collective-permute-start | bytes 1572872 | tf_op jit(solution)/shard_map/ppermute | solution.py:200
  473.0 42.9 %collective-permute-start.57 = (bf16[256,1024]{1,0:T(8,128)(2,1)}, bf16[256,1024]{1,0:T(8,128)(2,1)S(1)}, u32[]{:S(2)}, u32[]{:S(2)}) collective-permute-start(bf16[256,1024]{1,0:T(8,128)(2,1)} %get-tuple-element.126), channel_id=1, source_target_pairs={{0,1},{1,0},{2,3},{3,2},{4,5},{5,4},{6,7},{7,6},{8,9},{9,8},{10,11... | collective-permute-start | bytes 1572872 | tf_op jit(solution)/shard_map/ppermute | solution.py:200
  515.9 32.2 %collective-permute-start.117 = (bf16[256,2816]{1,0:T(8,128)(2,1)S(1)}, bf16[256,2816]{1,0:T(8,128)(2,1)S(1)}, u32[]{:S(2)}, u32[]{:S(2)}) collective-permute-start(bf16[256,2816]{1,0:T(8,128)(2,1)S(1)} %get-tuple-element.78), channel_id=1, source_target_pairs={{0,4},{4,0},{8,12},{12,8},{16,20},{20,16},{24,28},{28,24},{1,5},{5... | collective-permute-start | bytes 4325384 | tf_op jit(solution)/shard_map/ppermute | solution.py:200
  530.6 40.1 %collective-permute-start.71 = (bf16[256,1024]{1,0:T(8,128)(2,1)S(1)}, bf16[256,1024]{1,0:T(8,128)(2,1)S(1)}, u32[]{:S(2)}, u32[]{:S(2)}) collective-permute-start(bf16[256,1024]{1,0:T(8,128)(2,1)S(1)} %copy-done.52), channel_id=1, source_target_pairs={{0,16},{4,20},{8,24},{12,28},{16,0},{20,4},{24,8},{28,12},{1,17},{... | collective-permute-start | bytes 1572872 | tf_op jit(solution)/shard_map/ppermute | solution.py:200
  535.9 48.1 %collective-permute-start.59 = (bf16[256,1024]{1,0:T(8,128)(2,1)S(1)}, bf16[256,1024]{1,0:T(8,128)(2,1)S(1)}, u32[]{:S(2)}, u32[]{:S(2)}) collective-permute-start(bf16[256,1024]{1,0:T(8,128)(2,1)S(1)} %copy-done.51), channel_id=1, source_target_pairs={{0,16},{4,20},{8,24},{12,28},{16,0},{20,4},{24,8},{28,12},{1,17},{... | collective-permute-start | bytes 1572872 | tf_op jit(solution)/shard_map/ppermute | solution.py:200
  547.6 134.8 %collective-permute-start.128 = (bf16[1408,256]{1,0:T(8,128)(2,1)}, bf16[1408,256]{1,0:T(8,128)(2,1)S(1)}, u32[]{:S(2)}, u32[]{:S(2)}) collective-permute-start(bf16[1408,256]{1,0:T(8,128)(2,1)} %get-tuple-element.109), channel_id=1, source_target_pairs={{0,4},{4,0},{8,12},{12,8},{16,20},{20,16},{24,28},{28,24},{1,5},{5... | collective-permute-start | bytes 2162696 | tf_op jit(solution)/shard_map/ppermute | solution.py:200
  553.0 129.9 %collective-permute-start.130 = (bf16[1408,256]{1,0:T(8,128)(2,1)}, bf16[1408,256]{1,0:T(8,128)(2,1)}, u32[]{:S(2)}, u32[]{:S(2)}) collective-permute-start(bf16[1408,256]{1,0:T(8,128)(2,1)} %get-tuple-element.113), channel_id=1, source_target_pairs={{0,8},{4,12},{8,0},{12,4},{16,24},{20,28},{24,16},{28,20},{1,9},{5... | collective-permute-start | bytes 2162696 | tf_op jit(solution)/shard_map/ppermute | solution.py:200
  682.4 51.7 %collective-permute-start.127 = (bf16[1408,256]{1,0:T(8,128)(2,1)}, bf16[1408,256]{1,0:T(8,128)(2,1)S(1)}, u32[]{:S(2)}, u32[]{:S(2)}) collective-permute-start(bf16[1408,256]{1,0:T(8,128)(2,1)} %fusion.18), channel_id=1, source_target_pairs={{0,16},{4,20},{8,24},{12,28},{16,0},{20,4},{24,8},{28,12},{1,17},{... | collective-permute-start | bytes 2162696 | tf_op jit(solution)/shard_map/ppermute | solution.py:200
  682.9 32.7 %collective-permute-start.102 = (bf16[1024,256]{1,0:T(8,128)(2,1)}, bf16[1024,256]{1,0:T(8,128)(2,1)}, u32[]{:S(2)}, u32[]{:S(2)}) collective-permute-start(bf16[1024,256]{1,0:T(8,128)(2,1)} %get-tuple-element.90), channel_id=1, source_target_pairs={{0,4},{4,0},{8,12},{12,8},{16,20},{20,16},{24,28},{28,24},{1,5},{5... | collective-permute-start | bytes 1572872 | tf_op jit(solution)/shard_map/ppermute | solution.py:200
  715.7 44.0 %collective-permute-start.84 = (bf16[256,768]{0,1:T(8,128)(2,1)}, bf16[256,768]{0,1:T(8,128)(2,1)S(1)}, u32[]{:S(2)}, u32[]{:S(2)}) collective-permute-start(bf16[256,768]{0,1:T(8,128)(2,1)} %get-tuple-element.105), channel_id=1, source_target_pairs={{0,16},{4,20},{8,24},{12,28},{16,0},{20,4},{24,8},{28,12},{1,17},{... | collective-permute-start | bytes 1179656 | tf_op jit(solution)/shard_map/ppermute | solution.py:200
  734.1 49.2 %collective-permute-start.116 = (bf16[256,2816]{1,0:T(8,128)(2,1)}, bf16[256,2816]{1,0:T(8,128)(2,1)S(1)}, u32[]{:S(2)}, u32[]{:S(2)}) collective-permute-start(bf16[256,2816]{1,0:T(8,128)(2,1)} %get-tuple-element.79), channel_id=1, source_target_pairs={{0,4},{4,0},{8,12},{12,8},{16,20},{20,16},{24,28},{28,24},{1,5},{5... | collective-permute-start | bytes 4325384 | tf_op jit(solution)/shard_map/ppermute | solution.py:200
  734.2 49.7 %collective-permute-start.118 = (bf16[256,2816]{1,0:T(8,128)(2,1)}, bf16[256,2816]{1,0:T(8,128)(2,1)S(1)}, u32[]{:S(2)}, u32[]{:S(2)}) collective-permute-start(bf16[256,2816]{1,0:T(8,128)(2,1)} %get-tuple-element.81), channel_id=1, source_target_pairs={{0,8},{4,12},{8,0},{12,4},{16,24},{20,28},{24,16},{28,20},{1,9},{5... | collective-permute-start | bytes 4325384 | tf_op jit(solution)/shard_map/ppermute | solution.py:200
  763.2 80.0 %collective-permute-start.120 = (bf16[256,2816]{1,0:T(8,128)(2,1)S(1)}, bf16[256,2816]{1,0:T(8,128)(2,1)S(1)}, u32[]{:S(2)}, u32[]{:S(2)}) collective-permute-start(bf16[256,2816]{1,0:T(8,128)(2,1)S(1)} %copy-done.37), channel_id=1, source_target_pairs={{0,4},{4,0},{8,12},{12,8},{16,20},{20,16},{24,28},{28,24},{1,5},{5... | collective-permute-start | bytes 4325384 | tf_op jit(solution)/shard_map/ppermute | solution.py:200
  785.6 58.1 %collective-permute-start.122 = (bf16[256,2816]{1,0:T(8,128)(2,1)S(1)}, bf16[256,2816]{1,0:T(8,128)(2,1)S(1)}, u32[]{:S(2)}, u32[]{:S(2)}) collective-permute-start(bf16[256,2816]{1,0:T(8,128)(2,1)S(1)} %copy-done.38), channel_id=1, source_target_pairs={{0,8},{4,12},{8,0},{12,4},{16,24},{20,28},{24,16},{28,20},{1,9},{5... | collective-permute-start | bytes 4325384 | tf_op jit(solution)/shard_map/ppermute | solution.py:200
  787.7 57.5 %collective-permute-start.119 = (bf16[256,2816]{1,0:T(8,128)(2,1)S(1)}, bf16[256,2816]{1,0:T(8,128)(2,1)S(1)}, u32[]{:S(2)}, u32[]{:S(2)}) collective-permute-start(bf16[256,2816]{1,0:T(8,128)(2,1)S(1)} %fusion.16), channel_id=1, source_target_pairs={{0,16},{4,20},{8,24},{12,28},{16,0},{20,4},{24,8},{28,12},{1,17},{... | collective-permute-start | bytes 4325384 | tf_op jit(solution)/shard_map/ppermute | solution.py:200
  789.0 39.3 %collective-permute-start.94 = (bf16[256,768]{0,1:T(8,128)(2,1)S(1)}, bf16[256,768]{0,1:T(8,128)(2,1)S(1)}, u32[]{:S(2)}, u32[]{:S(2)}) collective-permute-start(bf16[256,768]{0,1:T(8,128)(2,1)S(1)} %get-tuple-element.108), channel_id=1, source_target_pairs={{0,8},{4,12},{8,0},{12,4},{16,24},{20,28},{24,16},{28,20},{1,9},{5... | collective-permute-start | bytes 1179656 | tf_op jit(solution)/shard_map/ppermute | solution.py:200
  791.9 38.9 %collective-permute-start.110 = (bf16[1024,256]{1,0:T(8,128)(2,1)S(1)}, bf16[1024,256]{1,0:T(8,128)(2,1)S(1)}, u32[]{:S(2)}, u32[]{:S(2)}) collective-permute-start(bf16[1024,256]{1,0:T(8,128)(2,1)S(1)} %get-tuple-element.85), channel_id=1, source_target_pairs={{0,4},{4,0},{8,12},{12,8},{16,20},{20,16},{24,28},{28,24},{1,5},{5... | collective-permute-start | bytes 1572872 | tf_op jit(solution)/shard_map/ppermute | solution.py:200
  863.2 88.0 %collective-permute-start.123 = (bf16[256,2816]{1,0:T(8,128)(2,1)}, bf16[256,2816]{1,0:T(8,128)(2,1)}, u32[]{:S(2)}, u32[]{:S(2)}) collective-permute-start(bf16[256,2816]{1,0:T(8,128)(2,1)} %broadcast_select_fusion), channel_id=1, source_target_pairs={{0,2},{1,3},{2,0},{3,1},{4,6},{5,7},{6,4},{7,5},{8,10},{9,11},{10,... | collective-permute-start | bytes 4325384 | tf_op jit(solution)/shard_map/ppermute | solution.py:200
  886.4 62.6 %collective-permute-start.114 = (bf16[512,256]{1,0:T(8,128)(2,1)}, bf16[512,256]{1,0:T(8,128)(2,1)}, u32[]{:S(2)}, u32[]{:S(2)}) collective-permute-start(bf16[512,256]{1,0:T(8,128)(2,1)} %get-tuple-element.151), channel_id=1, source_target_pairs={{0,2},{1,3},{2,0},{3,1},{4,6},{5,7},{6,4},{7,5},{8,10},{9,11},{10,... | collective-permute-start | bytes 786440 | tf_op jit(solution)/shard_map/ppermute | solution.py:200
  (189 other events, 4464.9 us)
Sparse Core Ops, SparseCore 0:
  27.6 110.8 all-gather.1
  707.2 83.3 reduce-scatter.1

commit v2 on v1

--- a/solution.py
+++ b/solution.py
@@ -9,6 +9,7 @@
 
 BLOCK = 64
 LEN = 1024
+LANES = 128
 HIGHEST = lax.Precision.HIGHEST
 EPS_NORM = 1e-06
 EPS_GROUP = 1.0
@@ -87,7 +88,7 @@
 
 
 def backward_kernel(kw, vw, proj_ref, low_ref, up_ref, bias_ref, gain_ref, mixed_ref,
-                    states_ref, grad_ref, out_ref, down_ref, upgrad_ref, sums_ref, gains_ref, state):
+                    states_ref, grad_ref, wide_ref, out_ref, upgrad_ref, sums_ref, gains_ref, state):
     blocks = proj_ref.shape[0] // BLOCK
     root = kw ** (-0.5)
     state[...] = jnp.zeros_like(state)
@@ -146,7 +147,7 @@
         grad_logit = grad_decay * (sigmoid(-logit) / 16.0)
         sums_ref[...] += jnp.sum(grad_logit, axis=0, keepdims=True)
         upgrad_ref[...] += dot(low, grad_logit, 0, 0, HIGHEST)
-        down_ref[rows, :] = dot(grad_logit, up_ref[...], 1, 1, HIGHEST).astype(BF)
+        out_ref[rows, 2 * kw + 2 * vw:] = dot(grad_logit, wide_ref[...], 1, 1, HIGHEST).astype(BF)
         return 0
 
     lax.fori_loop(0, blocks, step, 0)
@@ -177,22 +178,22 @@
 
 def mixer_backward(proj, lowrank, gate_up, gate_bias, gain, mixed, states, grad):
     rows, (rank, kw), vw = proj.shape[0], gate_up.shape, gain.shape[1]
+    wide = jnp.pad(gate_up, ((0, LANES - rank), (0, 0)))
     return pl.pallas_call(
         functools.partial(backward_kernel, kw, vw),
         out_shape=(
-            jax.ShapeDtypeStruct(proj.shape, BF),
-            jax.ShapeDtypeStruct((rows, rank), BF),
+            jax.ShapeDtypeStruct((rows, proj.shape[1] + LANES), BF),
             jax.ShapeDtypeStruct((rank, kw), F32),
             jax.ShapeDtypeStruct((1, kw), F32),
             jax.ShapeDtypeStruct((1, vw), F32),
         ),
-        in_specs=[vmem()] * 8,
-        out_specs=(vmem(),) * 5,
+        in_specs=[vmem()] * 9,
+        out_specs=(vmem(),) * 4,
         scratch_shapes=[pltpu.VMEM((vw, kw), F32)],
         compiler_params=pltpu.CompilerParams(vmem_limit_bytes=40 * 2**20),
         cost_estimate=pl.CostEstimate(flops=40_000_000_000, bytes_accessed=16 * 2**20, transcendentals=0),
         name="mixer_backward",
-    )(proj, lowrank, gate_up, gate_bias, gain, mixed, states, grad)
+    )(proj, lowrank, gate_up, gate_bias, gain, mixed, states, grad, wide)
 
 
 def swap(array, axis, bit):
@@ -200,127 +201,142 @@
     return lax.ppermute(array, axis, [(i, i ^ bit) for i in range(size)])
 
 
-def reorder(array, dim):
+def bits_of(size):
+    return [1 << k for k in range(size.bit_length() - 1)]
+
+
+def dp_bits():
+    bits = bits_of(lax.axis_size("dp"))
+    return bits[:1], bits[1:-1], bits[-1:]
+
+
+def index_at(place):
+    low, middle, top = dp_bits()
+    return sum(bit for k, bit in enumerate([*middle, *top, *low]) if place >> k & 1)
+
+
+def reorder(array, dim, back=False):
     me, size = lax.axis_index("dp"), lax.axis_size("dp")
     width = array.shape[dim] // size
-    return jnp.concatenate(
-        [lax.dynamic_slice_in_dim(array, (j ^ me) * width, width, dim) for j in range(size)], dim
-    )
-
-
-def bits_of(size):
-    return [1 << k for k in range(size.bit_length() - 1)]
-
-
-def gather_bits(pieces, bits):
+    to = [0] * size
+    for place in range(size):
+        to[index_at(place)] = place
+    places = []
+    for p in range(size):
+        if back:
+            source = jnp.asarray(to, jnp.int32)[p ^ me]
+        else:
+            source = index_at(p) ^ me
+        places.append(lax.dynamic_slice_in_dim(array, source * width, width, dim))
+    return jnp.concatenate(places, dim)
+
+
+class Flow:
+    def __init__(self):
+        self.fence, self.posted = (), []
+
+    def send(self, array, axis, bit):
+        got = swap(lax.optimization_barrier((array, self.fence))[0] if self.fence else array, axis, bit)
+        self.posted.append(got)
+        return got
+
+    def note(self, *arrays):
+        self.posted += arrays
+
+    def turn(self):
+        self.fence, self.posted = tuple(self.posted), []
+
+    def held(self, array):
+        return lax.optimization_barrier((array, self.fence))[0]
+
+
+def after(array, *earlier):
+    return lax.optimization_barrier((array, earlier))[0]
+
+
+def pick(array, dim, count, places):
+    width = array.shape[dim] // count
+    return jnp.concatenate([lax.slice_in_dim(array, p * width, (p + 1) * width, axis=dim) for p in places], dim)
+
+
+def grow(flow, array, bits, dim):
     for bit in bits:
-        pieces.update({i ^ bit: swap(piece, "dp", bit) for i, piece in list(pieces.items())})
-    return pieces
-
-
-def scatter_bits(pieces, bits):
+        array = jnp.concatenate([array, flow.send(array, "dp", bit)], dim)
+    return array
+
+
+def turned(array, dim):
+    count = lax.axis_size("dp") // 2
+    return pick(array, dim, count, [*range(0, count, 2), *range(1, count, 2)])
+
+
+def turned_back(array, dim):
+    count = lax.axis_size("dp") // 2
+    return pick(array, dim, count, [p for k in range(count // 2) for p in (k, count // 2 + k)])
+
+
+def shrink(flow, array, bits, dim):
     for bit in bits:
-        for i in [i for i in pieces if i & bit]:
-            pieces[i ^ bit] = pieces[i ^ bit] + swap(pieces.pop(i), "dp", bit)
-    return pieces
-
-
-def in_order(pieces, dim):
-    return jnp.concatenate([pieces[i] for i in range(len(pieces))], dim)
-
-
-def cut(array, dim, count):
-    return dict(enumerate(jnp.split(array, count, dim)))
-
-
-def dp_orders():
-    bits = bits_of(lax.axis_size("dp"))
-    top, middle = bits[-1], bits[1:-1]
-    return [[*middle, top, bits[0]], [top, *middle, bits[0]]]
-
-
-def gather_dp(shard, dim):
-    halves = [
-        in_order(gather_bits({0: half}, order), dim)
-        for half, order in zip(jnp.split(shard, 2, 1 - dim), dp_orders())
-    ]
-    return jnp.concatenate(halves, 1 - dim)
-
-
-def scatter_dp(array, dim):
-    halves = [
-        scatter_bits(cut(half, dim, lax.axis_size("dp")), order[::-1])[0]
-        for half, order in zip(jnp.split(array, 2, 1 - dim), dp_orders())
-    ]
-    return jnp.concatenate(halves, 1 - dim)
-
-
-def crossed():
-    high = lax.axis_index("tensor") // 2
-    return high != lax.axis_index("dp") // (lax.axis_size("dp") // 2)
-
-
-def gather_square(shard, dim):
-    other = swap(shard, "tensor", 2)
-    mine = jnp.where(crossed(), other, shard)
-    give = jnp.where(crossed(), shard, other)
-    bits = bits_of(lax.axis_size("dp"))
-    pieces = {0: mine, bits[-1]: swap(give, "dp", bits[-1])}
-    return in_order(gather_bits(pieces, [*bits[1:-1], bits[0]]), dim)
-
-
-def scatter_square(array, dim):
-    bits = bits_of(lax.axis_size("dp"))
-    pieces = scatter_bits(cut(array, dim, lax.axis_size("dp")), [bits[0], *bits[1:-1][::-1]])
-    mine, other = pieces[0], swap(pieces[bits[-1]], "dp", bits[-1])
-    keep = jnp.where(crossed(), other, mine)
-    send = jnp.where(crossed(), mine, other)
-    return keep.astype(F32) + swap(send, "tensor", 2).astype(F32)
-
-
-def across_y(array):
-    return swap(array, "dp", lax.axis_size("dp") // 2)
-
-
-def across_z(array):
-    return swap(array, "tensor", 1)
-
-
-def gather_tokens(own):
-    half = own.shape[1] // 2
-    left, right = own[:, :half], own[:, half:]
-    y_right, z_right = across_y(left), across_z(right)
-    z_left, d_right = across_z(left), across_z(y_right)
-    y_left, d_left = across_y(right), across_y(z_right)
-    return jnp.concatenate(
-        [
-            own,
-            jnp.concatenate([z_left, z_right], 1),
-            jnp.concatenate([y_left, y_right], 1),
-            jnp.concatenate([d_left, d_right], 1),
-        ],
-        0,
-    )
-
-
-def scatter_tokens(partial):
-    rows, half = partial.shape[0] // 4, partial.shape[1] // 2
-    part = lambda r, c: partial[r * rows:(r + 1) * rows, c * half:(c + 1) * half]
-    add = lambda a, b: a.astype(F32) + b.astype(F32)
-    y_one, y_two = across_y(part(2, 0)), across_y(part(3, 0))
-    z_one, z_two = across_z(part(1, 0)), across_z(part(3, 1))
-    right = add(part(0, 1), y_one)
-    left = add(part(0, 0), z_one)
-    right = add(right, across_z(add(part(1, 1), y_two).astype(BF)))
-    left = add(left, across_y(add(part(2, 1), z_two).astype(BF)))
-    return jnp.concatenate([left, right], 1)
-
-
-def everywhere(array, axes):
-    for axis in axes:
-        for bit in bits_of(lax.axis_size(axis)):
-            array = array + swap(array, axis, bit)
+        keep, give = jnp.split(array, 2, dim)
+        array = keep + flow.send(give, "dp", bit)
     return array
+
+
+def shrink_inner(flow, array, bits, dim):
+    for bit in reversed(bits):
+        keep = pick(array, dim, 4, [0, 2])
+        give = pick(array, dim, 4, [1, 3])
+        array = keep + flow.send(give, "dp", bit)
+    return array
+
+
+def gather_first(flow, one, two, dim):
+    low, middle, top = dp_bits()
+    return grow(flow, one, middle, dim), grow(flow, two, top, dim)
+
+
+def gather_second(flow, one, two, dim):
+    low, middle, top = dp_bits()
+    return grow(flow, one, top, dim), turned(grow(flow, two, middle, dim), dim)
+
+
+def gather_core(flow, one, two, dim):
+    low, middle, top = dp_bits()
+    return grow(flow, one, low, dim), grow(flow, two, low, dim)
+
+
+def scatter_core(flow, one, two, dim):
+    low, middle, top = dp_bits()
+    return shrink(flow, one, low, dim), shrink(flow, two, low, dim)
+
+
+def scatter_first(flow, one, two, dim):
+    low, middle, top = dp_bits()
+    return shrink(flow, one, top, dim), shrink_inner(flow, two, middle, dim)
+
+
+def scatter_second(flow, one, two, dim):
+    low, middle, top = dp_bits()
+    return shrink(flow, one, middle[::-1], dim), shrink(flow, two, top, dim)
+
+
+def gather_rows(array):
+    return lax.all_gather(array, "tensor", axis=0, tiled=True)
+
+
+def scatter_rows(array):
+    return lax.psum_scatter(array, "tensor", scatter_dimension=0, tiled=True)
+
+
+class Everywhere:
+    def __init__(self, flow, array, axes):
+        self.flow, self.array = flow, array
+        self.left = [(axis, bit) for axis in axes for bit in bits_of(lax.axis_size(axis))]
+
+    def step(self, count=1):
+        for axis, bit in self.left[:count]:
+            self.array = self.array + self.flow.send(self.array, axis, bit)
+        self.left = self.left[count:]
 
 
 def norm_scale(rows):
@@ -344,80 +360,171 @@
     gain_two = reorder(norm2_gain[None, :], 1)
     gate_down = reorder(gate_down, 0)
 
+    flow = Flow()
     inputs_wide = inputs.astype(F32)
     scale_one = norm_scale(inputs_wide)
     normed_one = (inputs_wide * scale_one * gain_one).astype(BF)
-    rows_one = lax.all_gather(normed_one, "tensor", axis=0, tiled=True)
-    into = gather_dp(jnp.concatenate([query_weight, key_weight, value_weight, outgate_weight], 1), 0)
-    shard_proj = jnp.concatenate([proj_weight] + [swap(proj_weight, "tensor", m) for m in range(1, heads)], 0)
-    proj_full = gather_dp(shard_proj, 1)
-    gate_up_full = gather_square(jnp.concatenate([ffn_gate, ffn_up], 1), 0)
-    down_full = gather_square(ffn_down, 1)
-    cot_rows = gather_tokens(cotangent)
-
-    projected = matmul(rows_one, into).astype(BF)
+
+    shard_proj = gather_rows(proj_weight)
+    rows_one = gather_rows(normed_one)
+    into_shard = jnp.concatenate([query_weight, key_weight, value_weight, outgate_weight], 1)
+    into = gather_first(flow, *jnp.split(into_shard, 2, 1), 0)
+    flow.turn()
+    into = gather_second(flow, *into, 0)
+    flow.turn()
+    into = gather_core(flow, *into, 0)
+    flow.turn()
+    proj_full = gather_first(flow, *jnp.split(shard_proj, 2, 0), 1)
+    flow.turn()
+    proj_full = gather_second(flow, *proj_full, 1)
+    flow.turn()
+    gate_up_full = gather_first(flow, ffn_gate, ffn_up, 0)
+    proj_full = jnp.concatenate(gather_core(flow, *proj_full, 1), 0)
+    flow.turn()
+    cot_rows = gather_rows(after(cotangent, shard_proj)).reshape(heads, 2, own_rows // 2, -1)
+    cot_rows = [cot_rows[:, k].reshape(heads * own_rows // 2, -1) for k in range(2)]
+
+    down_wide = jnp.pad(gate_down, ((0, 0), (0, LANES - gate_down.shape[1])))
+    into = jnp.concatenate([*into, down_wide], 1)
+    projected = matmul(flow.held(rows_one), into[:, :2 * kw + 2 * vw]).astype(BF)
     lowrank = matmul(rows_one, gate_down)
     gate_row, gain_row = gate_bias[None, :], group_gain[None, :]
     gated, mixed, states = mixer_forward(projected, lowrank, gate_up, gate_row, gain_row)
+    flow.note(gated)
+    flow.turn()
+
+    def exchange(pieces, dim):
+        come = jnp.stack([pieces[0]] + [swap(pieces[m], "tensor", m) for m in range(1, heads)], 0)
+        return jnp.concatenate(
+            [lax.dynamic_index_in_dim(come, head ^ t, 0, keepdims=False) for t in range(heads)], dim
+        )
     def rows_of(array, index):
         return lax.dynamic_slice_in_dim(array, index * own_rows, own_rows, 0)
-    gated_own = jnp.concatenate(
-        [rows_of(gated, head)]
-        + [swap(rows_of(gated, head ^ m), "tensor", m) for m in range(1, heads)],
-        1,
-    )
-    resid = inputs_wide + matmul(gated_own, proj_full)
+    gated_own = exchange([rows_of(gated, head ^ m) for m in range(heads)], 1)
+    gate_up_full = gather_second(flow, *gate_up_full, 0)
+    flow.turn()
+    resid = inputs_wide + lax.optimization_barrier(matmul(flow.held(after(gated_own, cot_rows)), proj_full))
     scale_two = norm_scale(resid)
     normed_two = (resid * scale_two * gain_two).astype(BF)
-
-    rows_two = gather_tokens(normed_two)
-    pre = matmul(rows_two, gate_up_full)
-    gate_pre, up_pre = pre[:, :units], pre[:, units:]
-    logistic = sigmoid(gate_pre)
-    act = gate_pre * logistic
-    hidden = (act * up_pre).astype(BF)
-    grad_hidden = times_transposed(cot_rows, down_full)
-    grad_up = (grad_hidden * act).astype(BF)
-    grad_gate = (grad_hidden * up_pre * (logistic * (1.0 + gate_pre * (1.0 - logistic)))).astype(BF)
-    grad_pre = jnp.concatenate([grad_gate, grad_up], 1)
-    grad_two = scatter_tokens(times_transposed(grad_pre, gate_up_full).astype(BF))
+    rows_two = [gather_rows(part) for part in jnp.split(normed_two, 2, 0)]
+    flow.note(normed_two)
+    flow.turn()
+
+    gate_full, up_full = gather_core(flow, *gate_up_full, 0)
+    down_full = gather_first(flow, *jnp.split(ffn_down, 2, 0), 1)
+    flow.turn()
+    down_full = gather_second(flow, *down_full, 1)
+    flow.turn()
+    down_full = jnp.concatenate(gather_core(flow, *down_full, 1), 0)
+    flow.turn()
+
+    def feed_forward(rows, cot):
+        gate_pre = matmul(rows, gate_full)
+        up_pre = matmul(rows, up_full)
+        logistic = sigmoid(gate_pre)
+        act = gate_pre * logistic
+        hidden = (act * up_pre).astype(BF)
+        grad_hidden = times_transposed(cot, down_full)
+        grad_up = (grad_hidden * act).astype(BF)
+        grad_gate = (grad_hidden * up_pre * (logistic * (1.0 + gate_pre * (1.0 - logistic)))).astype(BF)
+        back = (times_transposed(grad_gate, gate_full) + times_transposed(grad_up, up_full)).astype(BF)
+        return hidden, grad_gate, grad_up, back
+    first = feed_forward(rows_two[0], cot_rows[0])
+    rows_two[1] = after(rows_two[1], first[3])
+    hidden, grad_gate, grad_up, part_two = zip(first, feed_forward(rows_two[1], cot_rows[1]))
+
+    grad_two = jnp.concatenate([scatter_rows(part) for part in part_two], 0).astype(F32)
+    hidden, grad_gate, grad_up, rows_two, cot_rows = (
+        jnp.concatenate(parts, 0) for parts in (hidden, grad_gate, grad_up, rows_two, cot_rows)
+    )
+    flow.note(part_two)
+    flow.turn()
+    gate_sums = transposed_times(rows_two, flow.held(grad_gate)).astype(BF)
+    up_sums = transposed_times(rows_two, flow.held(grad_up)).astype(BF)
+    gate_sums, up_sums = scatter_core(flow, gate_sums, up_sums, 0)
+    flow.turn()
+    gate_sums, up_sums = scatter_first(flow, gate_sums, up_sums, 0)
+    down_sums = transposed_times(after(hidden, part_two), cot_rows).astype(BF)
+    part_out = matmul(after(hidden, part_two), down_full).astype(BF)
+    out_own = [scatter_rows(part) for part in jnp.split(part_out, 2, 0)]
+    flow.note(part_out, down_sums)
+    flow.turn()
+    grad_two = flow.held(grad_two)
     norm2_term = jnp.sum(grad_two * resid * scale_two, axis=0, keepdims=True)
     grad_resid = cotangent.astype(F32) + norm_back(grad_two, resid, scale_two, gain_two)
-    output = (resid + scatter_tokens(matmul(hidden, down_full).astype(BF))).astype(BF)
-    grad_gate_up_own = scatter_square(transposed_times(rows_two, grad_pre).astype(BF), 0)
-    grad_down_own = scatter_square(transposed_times(hidden, cot_rows).astype(BF), 1)
 
     grad_branch = grad_resid.astype(BF)
     grad_gated_own = times_transposed(grad_branch, proj_full).astype(BF)
-    pieces = [grad_gated_own[:, m * vw:(m + 1) * vw] for m in range(heads)]
-    pieces = jnp.stack([pieces[0]] + [swap(pieces[m], "tensor", m) for m in range(1, heads)], 0)
-    grad_gated = jnp.concatenate(
-        [lax.dynamic_index_in_dim(pieces, head ^ t, 0, keepdims=False) for t in range(heads)], 0
-    )
-    grad_into, grad_low, up_term, bias_term, group_term = mixer_backward(
-        projected, lowrank, gate_up, gate_row, gain_row, mixed, states, grad_gated
-    )
-    grad_proj_part = cut(scatter_dp(transposed_times(gated_own, grad_branch).astype(BF), 1), 0, heads)
-    grad_proj = grad_proj_part[0].astype(F32)
+    flow.note(grad_gated_own)
+    flow.turn()
+    grad_gated = exchange(
+        [lax.dynamic_slice_in_dim(grad_gated_own, (head ^ m) * vw, vw, 1) for m in range(heads)], 0
+    )
+    gate_sums, up_sums = scatter_second(flow, gate_sums, up_sums, 0)
+    grad_gate_own, grad_up_own = gate_sums.astype(F32), up_sums.astype(F32)
+    proj_sums = transposed_times(gated_own, flow.held(grad_branch)).astype(BF)
+    proj_sums = scatter_core(flow, *jnp.split(proj_sums, 2, 0), 1)
+    flow.turn()
+    proj_sums = scatter_first(flow, *proj_sums, 1)
+
+    grad_into, up_term, bias_term, group_term = mixer_backward(
+        projected, lowrank, gate_up, gate_row, gain_row, mixed, states, flow.held(grad_gated)
+    )
+    grad_low = grad_into[:, 2 * kw + 2 * vw:2 * kw + 2 * vw + gate_down.shape[1]]
+    flow.note(grad_into)
+    flow.turn()
+    output = (resid + jnp.concatenate(flow.held(out_own), 0).astype(F32)).astype(BF)
+    total_low = times_transposed(grad_into, into).astype(BF)
+    grad_one = scatter_rows(total_low).astype(F32)
+    proj_sums = scatter_second(flow, *proj_sums, 1)
+    flow.note(total_low)
+    flow.turn()
+    into_sums = transposed_times(rows_one, flow.held(grad_into)).astype(BF)
+    into_sums = scatter_core(flow, *jnp.split(into_sums[:, :2 * kw + 2 * vw], 2, 1), 0)
+    flow.turn()
+    into_sums = scatter_first(flow, *into_sums, 0)
+    norm1_term = jnp.sum(flow.held(total_low).astype(F32) * rows_one.astype(F32), axis=0, keepdims=True) / gain_one
+    down_term = transposed_times(grad_low, rows_one)
+    small = Everywhere(
+        flow, reorder(jnp.concatenate([down_term, norm1_term, norm2_term], 0), 1, True), ("dp", "tensor")
+    )
+    by_head = Everywhere(
+        flow, jnp.concatenate([up_term, bias_term, group_term[:, :kw], group_term[:, kw:]], 0), ("dp",)
+    )
+    by_head.step()
+    flow.note(small.array)
+    flow.turn()
+    into_sums = scatter_second(flow, *into_sums, 0)
+    small.step()
+    by_head.step()
+    flow.turn()
+    down_sums = scatter_core(flow, *jnp.split(down_sums, 2, 0), 1)
+    small.step()
+    by_head.step(len(by_head.left))
+    flow.turn()
+    down_sums = scatter_first(flow, *down_sums, 1)
+    small.step()
+    flow.note(grad_one)
+    flow.turn()
+    down_sums = scatter_second(flow, *down_sums, 1)
+    small.step(len(small.left) - 1)
+    flow.turn()
+    small.step(len(small.left))
+    proj_sums = jnp.concatenate(proj_sums, 0)
+    grad_proj = lax.dynamic_slice_in_dim(proj_sums, head * vw, vw, 0).astype(F32)
     for m in range(1, heads):
-        grad_proj = grad_proj + swap(grad_proj_part[m], "tensor", m).astype(F32)
-    grad_into_own = scatter_dp(transposed_times(rows_one, grad_into).astype(BF), 0).astype(F32)
-    total = (times_transposed(grad_into, into) + times_transposed(grad_low, gate_down)).astype(BF)
-    norm1_term = jnp.sum(total.astype(F32) * rows_one.astype(F32), axis=0, keepdims=True) / gain_one
-    down_term = transposed_times(grad_low, rows_one)
-    grad_one = lax.psum_scatter(total, "tensor", scatter_dimension=0, tiled=True).astype(F32)
+        part = lax.dynamic_slice_in_dim(proj_sums, (head ^ m) * vw, vw, 0)
+        grad_proj = grad_proj + flow.send(part, "tensor", m).astype(F32)
+    grad_into_own = jnp.concatenate(into_sums, 1).astype(F32)
+    grad_down_own = jnp.concatenate(down_sums, 0).astype(F32)
     grad_input = grad_resid + norm_back(grad_one, inputs_wide, scale_one, gain_one)
-
-    summed = everywhere(reorder(jnp.concatenate([down_term, norm1_term, norm2_term], 0), 1), ("dp", "tensor"))
+    summed, by_head = small.array, by_head.array
     rank = gate_down.shape[1]
-    by_head = everywhere(
-        jnp.concatenate([up_term, bias_term, group_term[:, :kw], group_term[:, kw:]], 0), ("dp",)
-    )
     splits = [kw, 2 * kw, 2 * kw + vw]
     grad_query, grad_key, grad_value, grad_outgate = jnp.split(grad_into_own, splits, 1)
     return (
-        reorder(output, 1),
-        reorder(grad_input, 1),
+        reorder(output, 1, True),
+        reorder(grad_input, 1, True),
         summed[rank],
         grad_query,
         grad_key,
@@ -429,8 +536,8 @@
         by_head[rank + 1:].reshape(-1),
         grad_proj,
         summed[rank + 1],
-        grad_gate_up_own[:, :units],
-        grad_gate_up_own[:, units:],
+        grad_gate_own,
+        grad_up_own,
         grad_down_own,
     )
 

time: 977 us -> 725 us (0.74)
  waiting for transfers between devices: 511 us -> 243 us
  other arithmetic: 59.9 us -> 101 us
  starting transfers between devices: 93.9 us -> 60 us
    ppermute x132 -> x65, waiting for transfers between devices: 511 us -> 181 us  [swap(): return lax.ppermute(array, axis, [(i, i ^ bit) for i in range(size)])]
    concatenate x3 -> x27, other arithmetic: 1.79 us -> 55.4 us  [the longest x1 24.6 us: on_device(): proj_full = jnp.concatenate(gather_core(flow, *proj_full, 1), 0)]
    all_gather x1 -> x5, waiting for transfers between devices: 0.01 us -> 41.5 us  [gather_rows(): return lax.all_gather(array, 'tensor', axis=0, tiled=True)]
    ppermute x132 -> x65, starting transfers between devices: 93.9 us -> 59.1 us  [swap(): return lax.ppermute(array, axis, [(i, i ^ bit) for i in range(size)])]
    reduce_scatter x1 -> x5, waiting for transfers between devices: 0.01 us -> 20.3 us  [scatter_rows(): return lax.psum_scatter(array, 'tensor', scatter_dimension=0, tiled=True)]
    add x32 -> x29, other arithmetic: 37.8 us -> 21.5 us  [the longest x16 18.4 us: shrink(): array = keep + flow.send(give, 'dp', bit)]
    unnamed x306 -> x358, local copies, waits for them, and re-layouts: 64.7 us -> 52.8 us
    split x6 -> x20, local copies, waits for them, and re-layouts: 10.8 us -> 19.8 us  [the longest x17 15.4 us: shrink(): keep, give = jnp.split(array, 2, dim)]
  transfers between devices with their start and end apart: 134 -> 75, of which waited for: 42 -> 28; matrix products, arithmetic and copies ran while one was open for 27% -> 40% of each run, Pallas kernels for 4% -> 5%
where the time goes in v2:
time: 725 us; the launch traced here: 719 us
  waiting for transfers between devices  243 us (34%)
  matrix products  153 us (21%)
  local copies, waits for them, and re-layouts  102 us (14%)
  other arithmetic  101 us (14%)
  starting transfers between devices  60 us (8%)
  Pallas kernels  37.7 us (5%)
  between operations  22.1 us (3%)
    ppermute x65, waiting for transfers between devices, swap(): return lax.ppermute(array, axis, [(i, i ^ bit) for i in range(size)])  181 us
    dot_general x22, matrix products, dot(): lax.dot_general(a, b, (((ca,), (cb,)), ((), ())), precision=precision, pr...  153 us
    ppermute x65, starting transfers between devices, swap(): return lax.ppermute(array, axis, [(i, i ^ bit) for i in range(size)])  59.1 us
    unnamed x358, local copies, waits for them, and re-layouts  52.8 us
    all_gather x5, waiting for transfers between devices, gather_rows(): return lax.all_gather(array, 'tensor', axis=0, tiled=True)  41.5 us
    concatenate x1, other arithmetic, on_device(): proj_full = jnp.concatenate(gather_core(flow, *proj_full, 1), 0)  24.6 us
    pallas_call x1, Pallas kernels, mixer_backward(): pl.pallas_call(functools.partial(backward_kernel, kw, vw), out_shape=(jax...  23.8 us
    reduce_scatter x5, waiting for transfers between devices, scatter_rows(): return lax.psum_scatter(array, 'tensor', scatter_dimension=0, tiled=True)  20.3 us
  transfers between devices with their start and end apart: 75, of which 28 were waited for; matrix products, arithmetic and copies ran while one was open for 40% of the time, Pallas kernels for 5%

profile of v2, /device:TPU:0, one launch (start us, length us, event | category | flops | bytes accessed | tf_op | source)
XLA Modules:
  0.0 718.8 jit_solution(9063698289463314868)
XLA Ops:
  27.8 16.0 %collective-permute-done.3 = bf16[512,768]{1,0:T(8,128)(2,1)S(1)} collective-permute-done((bf16[512,768]{1,0:T(8,128)(2,1)}, bf16[512,768]{1,0:T(8,128)(2,1)S(1)}, u32[]{:S(2)}, u32[]{:S(2)}) %collective-permute-start.3) | collective-permute-done | bytes 786464 | tf_op jit(solution)/shard_map/ppermute | solution.py:201
  54.5 13.4 %collective-permute-done.7 = bf16[1024,256]{1,0:T(8,128)(2,1)S(1)} collective-permute-done((bf16[1024,256]{1,0:T(8,128)(2,1)S(1)}, bf16[1024,256]{1,0:T(8,128)(2,1)S(1)}, u32[]{:S(2)}, u32[]{:S(2)}) %collective-permute-start.7) | collective-permute-done | bytes 524320 | tf_op jit(solution)/shard_map/ppermute | solution.py:201
  74.2 18.5 %collective-permute-done.9 = bf16[1024,512]{1,0:T(8,128)(2,1)S(1)} collective-permute-done((bf16[1024,512]{1,0:T(8,128)(2,1)S(1)}, bf16[1024,512]{1,0:T(8,128)(2,1)S(1)}, u32[]{:S(2)}, u32[]{:S(2)}) %collective-permute-start.9) | collective-permute-done | bytes 1048608 | tf_op jit(solution)/shard_map/ppermute | solution.py:201
  107.7 11.8 %collective-permute-done.11 = bf16[256,1408]{1,0:T(8,128)(2,1)} collective-permute-done((bf16[256,1408]{1,0:T(8,128)(2,1)S(1)}, bf16[256,1408]{1,0:T(8,128)(2,1)}, u32[]{:S(2)}, u32[]{:S(2)}) %collective-permute-start.11) | collective-permute-done | bytes 720928 | tf_op jit(solution)/shard_map/ppermute | solution.py:201
  124.1 3.6 fusion.78.low_ref
  127.7 9.6 %fusion.28.proj_ref = bf16[1024,1536]{1,0:T(8,128)(2,1)S(1)} fusion(bf16[1024,2048]{1,0:T(8,128)(2,1)S(1)} %copy-done.23, bf16[2048,768]{1,0:T(8,128)(2,1)} %constant_dynamic-update-slice_fusion.16, bf16[1024,768]{1,0:T(8,128)(2,1)} %collective-permute-done.4, bf16[512,768]{1,0:T(8,128)(2,1)} %collective-permute-done.2, ...), kind=kOutput, calls=%fused_computation.43 | convolution fusion | flops 6475481088 | bytes 13631488 | tf_op jit(solution)/shard_map/dot_general | solution.py:21
  137.4 13.9 %mixer_forward.1 = (bf16[1024,512]{1,0:T(8,128)(2,1)S(1)}, bf16[1024,512]{1,0:T(8,128)(2,1)S(1)}, bf16[16,512,256]{2,1,0:T(8,128)(2,1)S(1)}) custom-call(bf16[1024,1536]{1,0:T(8,128)(2,1)S(1)} %fusion.28.proj_ref, f32[1024,16]{1,0:T(8,128)S(1)} %fusion.78.low_ref, f32[16,256]{1,0:T(8,128)S(1)} %copy-done, f32[1,256]{1,0:T(1,128)S(1)} %bitcast.105, ...), custom_call_target="tpu_custom_call" | custom-call | flops 20000000000 | bytes 10485760 | tf_op jit(solution)/shard_map/mixer_forward/pallas_call | solution.py:163
  161.6 24.6 %pad_maximum_fusion = bf16[2048,2048]{1,0:T(8,128)(2,1)} fusion(bf16[1024,2048]{1,0:T(8,128)(2,1)} %constant_dynamic-update-slice_fusion.37, bf16[1024,1024]{1,0:T(8,128)(2,1)} %collective-permute-done.12, bf16[1024,512]{1,0:T(8,128)(2,1)S(1)} %copy-done.48, bf16[1024,256]{1,0:T(8,128)(2,1)S(1)} %collective-permute-done.6, ...), kind=kLoop, calls=%fused_computation.2 | loop fusion | flops 41943040 | bytes 16777216 | tf_op jit(solution)/shard_map/concatenate | solution.py:382
  186.2 5.8 collective-permute-done.16
  196.5 3.4 pad_maximum_fusion.2
  200.9 5.8 pad_maximum_fusion.3
  206.7 20.5 %all-gather.10.cloned.1.call-done = bf16[1024,2048]{1,0:T(8,128)(2,1)} async-done(((bf16[256,2048]{1,0:T(8,128)(2,1)}), bf16[1024,2048]{1,0:T(8,128)(2,1)}) %all-gather.10.cloned.1.call-update) | async-done | bytes 4194320 | tf_op jit(solution)/shard_map/all_gather | solution.py:324
  227.2 4.9 fusion.65
  232.0 5.7 fusion.79
  248.2 4.4 collective-permute-done.21
  259.1 3.6 constant_dynamic-update-slice_fusion.54
  262.7 9.3 %collective-permute-done.23 = bf16[704,512]{1,0:T(8,128)(2,1)} collective-permute-done((bf16[704,512]{1,0:T(8,128)(2,1)S(1)}, bf16[704,512]{1,0:T(8,128)(2,1)}, u32[]{:S(2)}, u32[]{:S(2)}) %collective-permute-start.23) | collective-permute-done | bytes 720928 | tf_op jit(solution)/shard_map/ppermute | solution.py:201
  276.0 3.7 constant_dynamic-update-slice_fusion.50
  279.7 6.2 all-gather.12.cloned.1.call-done
  285.9 7.0 fusion.80
  295.1 6.6 fusion.60
  301.8 5.1 multiply_convert_fusion.5
  306.9 3.4 fusion.81
  310.4 7.4 %add_convert_fusion.1 = bf16[512,2048]{1,0:T(8,128)(2,1)} fusion(f32[512,2048]{1,0:T(8,128)S(1)} %fusion.81, bf16[512,1408]{1,0:T(8,128)(2,1)S(1)} %get-tuple-element.212, bf16[2048,1408]{1,0:T(8,128)(2,1)} %constant_dynamic-update-slice_fusion.50), kind=kOutput, calls=%fused_computation.37 | convolution fusion | flops 2954887168 | bytes 13500416 | tf_op jit(solution)/shard_map/dot_general | solution.py:21
  317.7 14.8 %all-gather.14.cloned.1.call-done = bf16[512,2048]{1,0:T(8,128)(2,1)} async-done(((bf16[128,2048]{1,0:T(8,128)(2,1)}), bf16[512,2048]{1,0:T(8,128)(2,1)}) %all-gather.14.cloned.1.call-update) | async-done | bytes 2097168 | tf_op jit(solution)/shard_map/all_gather | solution.py:324
  332.6 6.7 fusion.82
  339.3 5.2 fusion.59
  344.6 8.3 %multiply_convert_fusion.1 = (bf16[512,1408]{1,0:T(8,128)(2,1)S(1)}, bf16[512,1408]{1,0:T(8,128)(2,1)S(1)}, bf16[512,1408]{1,0:T(8,128)(2,1)}) fusion(f32[512,1408]{1,0:T(8,128)S(1)} %fusion.59, f32[512,1408]{1,0:T(8,128)S(1)} %fusion.82, bf16[512,2048]{1,0:T(8,128)(2,1)S(1)} %copy-done.59, bf16[2048,1408]{1,0:T(8,128)(2,1)} %constant_dynamic-update-slice_fusion.50), kind=kOutput, calls=%fused_computation.55 | convolution fusion | flops 2963603456 | bytes 17956864 | tf_op jit(solution)/shard_map/dot_general | solution.py:21
  352.9 3.5 fusion.83
  356.4 7.4 %add_convert_fusion = bf16[512,2048]{1,0:T(8,128)(2,1)} fusion(f32[512,2048]{1,0:T(8,128)S(1)} %fusion.83, bf16[512,1408]{1,0:T(8,128)(2,1)S(1)} %get-tuple-element.208, bf16[2048,1408]{1,0:T(8,128)(2,1)} %constant_dynamic-update-slice_fusion.50), kind=kOutput, calls=%fused_computation.36 | convolution fusion | flops 2954887168 | bytes 13500416 | tf_op jit(solution)/shard_map/dot_general | solution.py:21
  367.5 7.3 %convolution_convert_fusion.3 = bf16[2048,1408]{1,0:T(8,128)(2,1)S(1)} fusion(bf16[1024,2048]{1,0:T(8,128)(2,1)S(1)} %constant_dynamic-update-slice_fusion.64, bf16[1024,1408]{1,0:T(8,128)(2,1)S(1)} %pad_maximum_fusion.6), kind=kOutput, calls=%fused_computation.7 | convolution fusion | flops 5908463616 | bytes 12845056 | tf_op jit(solution)/shard_map/dot_general | solution.py:21
  380.4 9.5 %convolution_convert_fusion.4 = bf16[2048,1408]{1,0:T(8,128)(2,1)S(1)} fusion(bf16[1024,2048]{1,0:T(8,128)(2,1)} %copy-done.87, bf16[1024,1408]{1,0:T(8,128)(2,1)S(1)} %pad_maximum_fusion.5), kind=kOutput, calls=%fused_computation.8 | convolution fusion | flops 5908463616 | bytes 12845056 | tf_op jit(solution)/shard_map/dot_general | solution.py:21
  395.7 12.1 %convolution_convert_fusion.5 = bf16[1024,2048]{1,0:T(8,128)(2,1)S(1)} fusion(bf16[1024,1408]{1,0:T(8,128)(2,1)S(1)} %pad_maximum_fusion.4, bf16[704,2048]{1,0:T(8,128)(2,1)S(1)} %copy-done.116, bf16[704,1024]{1,0:T(8,128)(2,1)} %collective-permute-done.25, bf16[704,512]{1,0:T(8,128)(2,1)} %collective-permute-done.23, bf16[704,256]{1,0:T(8,128)(2,1)S(1)} %copy-done.85, ...), kind=kOutput, calls=%fused_computation.44 | convolution fusion | flops 5936513024 | bytes 12845056 | tf_op jit(solution)/shard_map/dot_general | solution.py:21
  423.7 8.1 %convolution_convert_fusion.2 = bf16[1408,2048]{1,0:T(8,128)(2,1)} fusion(bf16[1024,1408]{1,0:T(8,128)(2,1)S(1)} %pad_maximum_fusion.4, bf16[512,2048]{1,0:T(8,128)(2,1)S(1)} %bitcast.113, bf16[512,2048]{1,0:T(8,128)(2,1)S(1)} %bitcast.115), kind=kOutput, calls=%fused_computation.6 | convolution fusion | flops 5916852224 | bytes 12845056 | tf_op jit(solution)/shard_map/dot_general | solution.py:21
  431.8 20.3 %reduce-scatter.10.cloned.1.call-done = bf16[128,2048]{1,0:T(8,128)(2,1)} async-done(((bf16[512,2048]{1,0:T(8,128)(2,1)}), bf16[128,2048]{1,0:T(8,128)(2,1)}) %reduce-scatter.10.cloned.1.call-update) | async-done | bytes 524304 | tf_op jit(solution)/shard_map/reduce_scatter | solution.py:328
  459.5 5.9 convolution_convert_fusion.6
  479.7 3.8 fusion.63
  496.0 10.7 %collective-permute-done.37 = bf16[256,512]{1,0:T(8,128)(2,1)S(1)} collective-permute-done((bf16[256,512]{1,0:T(8,128)(2,1)S(1)}, bf16[256,512]{1,0:T(8,128)(2,1)S(1)}, u32[]{:S(2)}, u32[]{:S(2)}) %collective-permute-start.37) | collective-permute-done | bytes 262176 | tf_op jit(solution)/shard_map/ppermute | solution.py:201
  508.2 6.4 collective-permute-done.39
  516.4 8.4 %collective-permute-done.32 = bf16[256,1408]{1,0:T(8,128)(2,1)S(1)} collective-permute-done((bf16[256,1408]{1,0:T(8,128)(2,1)S(1)}, bf16[256,1408]{1,0:T(8,128)(2,1)S(1)}, u32[]{:S(2)}, u32[]{:S(2)}) %collective-permute-start.32) | collective-permute-done | bytes 720928 | tf_op jit(solution)/shard_map/ppermute | solution.py:201
  529.8 23.8 %mixer_backward.1 = (bf16[1024,1664]{1,0:T(8,128)(2,1)S(1)}, f32[16,256]{1,0:T(8,128)S(1)}, f32[1,256]{1,0:T(1,128)S(1)}, f32[1,512]{1,0:T(1,128)S(1)}) custom-call(bf16[1024,1536]{1,0:T(8,128)(2,1)S(1)} %copy-done.16, f32[1024,16]{1,0:T(8,128)S(1)} %copy-done.12, f32[16,256]{1,0:T(8,128)S(1)} %copy-done.2, f32[1,256]{1,0:T(1,128)S(1)} %bitcast.106, ...), custom_call_target="tpu_custom_call" | custom-call | flops 40000000000 | bytes 16777216 | tf_op jit(solution)/shard_map/mixer_backward/pallas_call | solution.py:182
  557.5 14.9 %fusion.31 = bf16[1024,2048]{1,0:T(8,128)(2,1)} fusion(bf16[1024,1664]{1,0:T(8,128)(2,1)S(1)} %get-tuple-element.146, bf16[2048,16]{1,0:T(8,128)(2,1)S(1)} %copy-done.101, bf16[2048,768]{1,0:T(8,128)(2,1)S(1)} %copy-done.112, bf16[1024,768]{1,0:T(8,128)(2,1)} %collective-permute-done.4, bf16[512,768]{1,0:T(8,128)(2,1)} %collective-permute-done.2, ...), kind=kOutput, calls=%fused_computation.45 | convolution fusion | flops 7029129216 | bytes 13959168 | tf_op jit(solution)/shard_map/dot_general | solution.py:21
  572.4 9.9 %convolution_convert_fusion = bf16[2048,1664]{1,0:T(8,128)(2,1)S(1)} fusion(bf16[1024,2048]{1,0:T(8,128)(2,1)} %all-gather.6.cloned.1.call-done, bf16[1024,1664]{1,0:T(8,128)(2,1)S(1)} %get-tuple-element.146), kind=kOutput, calls=%fused_computation.4 | convolution fusion | flops 6982729728 | bytes 14417920 | tf_op jit(solution)/shard_map/dot_general | solution.py:21
  587.7 3.5 fusion.51
  602.8 14.3 %collective-permute-done.45 = bf16[512,768]{1,0:T(8,128)(2,1)S(1)} collective-permute-done((bf16[512,768]{1,0:T(8,128)(2,1)S(1)}, bf16[512,768]{1,0:T(8,128)(2,1)S(1)}, u32[]{:S(2)}, u32[]{:S(2)}) %collective-permute-start.45) | collective-permute-done | bytes 786464 | tf_op jit(solution)/shard_map/ppermute | solution.py:201
  622.3 8.1 %collective-permute-done.50 = f32[19,256]{1,0:T(8,128)S(1)} collective-permute-done((f32[19,256]{1,0:T(8,128)S(1)}, f32[19,256]{1,0:T(8,128)S(1)}, u32[]{:S(2)}, u32[]{:S(2)}) %collective-permute-start.50) | collective-permute-done | bytes 19488 | tf_op jit(solution)/shard_map/ppermute | solution.py:201
  649.3 14.5 %collective-permute-done.55 = f32[18,2048]{1,0:T(8,128)S(1)} collective-permute-done((f32[18,2048]{1,0:T(8,128)S(1)}, f32[18,2048]{1,0:T(8,128)S(1)}, u32[]{:S(2)}, u32[]{:S(2)}) %collective-permute-start.55) | collective-permute-done | bytes 147488 | tf_op jit(solution)/shard_map/ppermute | solution.py:201
  683.5 25.7 %collective-permute-done.61 = f32[18,2048]{1,0:T(8,128)S(1)} collective-permute-done((f32[18,2048]{1,0:T(8,128)S(1)}, f32[18,2048]{1,0:T(8,128)S(1)}, u32[]{:S(2)}, u32[]{:S(2)}) %collective-permute-start.61) | collective-permute-done | bytes 147488 | tf_op jit(solution)/shard_map/ppermute | solution.py:201
  (633 shorter events, 229.7 us)
Async XLA Ops:
  7.2 43.8 %all-gather.8.cloned.1.call-start = ((), (), s32[]{:S(2)}) async-start(), calls=%async_computation.6 | async-start | bytes 1310720 | tf_op jit(solution)/shard_map/all_gather | solution.py:324
  13.7 110.4 %all-gather.6.cloned.1.call-start = ((), (), s32[]{:S(2)}) async-start(), calls=%async_computation.5 | async-start | bytes 5242880 | tf_op jit(solution)/shard_map/all_gather | solution.py:324
  24.8 18.9 %collective-permute-start.3 = (bf16[512,768]{1,0:T(8,128)(2,1)}, bf16[512,768]{1,0:T(8,128)(2,1)S(1)}, u32[]{:S(2)}, u32[]{:S(2)}) collective-permute-start(bf16[512,768]{1,0:T(8,128)(2,1)} %pad_maximum_fusion.24), channel_id=1, source_target_pairs={{0,8},{4,12},{8,0},{12,4},{16,24},{20,28},{24,16},{28,20},{1,9},{5... | collective-permute-start | bytes 2359304 | tf_op jit(solution)/shard_map/ppermute | solution.py:201
  26.3 21.1 %collective-permute-start.2 = (bf16[512,768]{1,0:T(8,128)(2,1)}, bf16[512,768]{1,0:T(8,128)(2,1)}, u32[]{:S(2)}, u32[]{:S(2)}) collective-permute-start(bf16[512,768]{1,0:T(8,128)(2,1)} %pad_maximum_fusion.23), channel_id=1, source_target_pairs={{0,16},{4,20},{8,24},{12,28},{16,0},{20,4},{24,8},{28,12},{1,17},{... | collective-permute-start | bytes 2359304 | tf_op jit(solution)/shard_map/ppermute | solution.py:201
  27.7 199.5 %all-gather.10.cloned.1.call-start = ((), (), s32[]{:S(2)}) async-start(), calls=%async_computation.7 | async-start | bytes 5242880 | tf_op jit(solution)/shard_map/all_gather | solution.py:324
  68.1 24.7 %collective-permute-start.9 = (bf16[1024,512]{1,0:T(8,128)(2,1)S(1)}, bf16[1024,512]{1,0:T(8,128)(2,1)S(1)}, u32[]{:S(2)}, u32[]{:S(2)}) collective-permute-start(bf16[1024,512]{1,0:T(8,128)(2,1)S(1)} %pad_maximum_fusion.17), channel_id=1, source_target_pairs={{0,8},{4,12},{8,0},{12,4},{16,24},{20,28},{24,16},{28,20},{1,9},{5... | collective-permute-start | bytes 3145736 | tf_op jit(solution)/shard_map/ppermute | solution.py:201
  71.8 25.2 %collective-permute-start.8 = (bf16[1024,512]{1,0:T(8,128)(2,1)S(1)}, bf16[1024,512]{1,0:T(8,128)(2,1)S(1)}, u32[]{:S(2)}, u32[]{:S(2)}) collective-permute-start(bf16[1024,512]{1,0:T(8,128)(2,1)S(1)} %pad_maximum_fusion.16), channel_id=1, source_target_pairs={{0,16},{4,20},{8,24},{12,28},{16,0},{20,4},{24,8},{28,12},{1,17},{... | collective-permute-start | bytes 3145736 | tf_op jit(solution)/shard_map/ppermute | solution.py:201
  97.0 30.7 %collective-permute-start.13 = (bf16[1024,1024]{1,0:T(8,128)(2,1)}, bf16[1024,1024]{1,0:T(8,128)(2,1)}, u32[]{:S(2)}, u32[]{:S(2)}) collective-permute-start(bf16[1024,1024]{1,0:T(8,128)(2,1)} %pad_maximum_fusion.8), channel_id=1, source_target_pairs={{0,4},{4,0},{8,12},{12,8},{16,20},{20,16},{24,28},{28,24},{1,5},{5... | collective-permute-start | bytes 6291464 | tf_op jit(solution)/shard_map/ppermute | solution.py:201
  98.7 29.0 %collective-permute-start.12 = (bf16[1024,1024]{1,0:T(8,128)(2,1)}, bf16[1024,1024]{1,0:T(8,128)(2,1)}, u32[]{:S(2)}, u32[]{:S(2)}) collective-permute-start(bf16[1024,1024]{1,0:T(8,128)(2,1)} %pad_maximum_fusion.7), channel_id=1, source_target_pairs={{0,4},{4,0},{8,12},{12,8},{16,20},{20,16},{24,28},{28,24},{1,5},{5... | collective-permute-start | bytes 6291464 | tf_op jit(solution)/shard_map/ppermute | solution.py:201
  101.3 18.2 %collective-permute-start.11 = (bf16[256,1408]{1,0:T(8,128)(2,1)S(1)}, bf16[256,1408]{1,0:T(8,128)(2,1)}, u32[]{:S(2)}, u32[]{:S(2)}) collective-permute-start(bf16[256,1408]{1,0:T(8,128)(2,1)S(1)} %copy-done.30), channel_id=1, source_target_pairs={{0,16},{4,20},{8,24},{12,28},{16,0},{20,4},{24,8},{28,12},{1,17},{... | collective-permute-start | bytes 2162696 | tf_op jit(solution)/shard_map/ppermute | solution.py:201
  103.2 18.5 %collective-permute-start.10 = (bf16[256,1408]{1,0:T(8,128)(2,1)S(1)}, bf16[256,1408]{1,0:T(8,128)(2,1)}, u32[]{:S(2)}, u32[]{:S(2)}) collective-permute-start(bf16[256,1408]{1,0:T(8,128)(2,1)S(1)} %copy-done.31), channel_id=1, source_target_pairs={{0,8},{4,12},{8,0},{12,4},{16,24},{20,28},{24,16},{28,20},{1,9},{5... | collective-permute-start | bytes 2162696 | tf_op jit(solution)/shard_map/ppermute | solution.py:201
  105.0 180.9 %all-gather.12.cloned.1.call-start = ((), (), s32[]{:S(2)}) async-start(), calls=%async_computation.8 | async-start | bytes 2621440 | tf_op jit(solution)/shard_map/all_gather | solution.py:324
  151.4 42.1 %collective-permute-start.18 = (bf16[512,1408]{1,0:T(8,128)(2,1)S(1)}, bf16[512,1408]{1,0:T(8,128)(2,1)S(1)}, u32[]{:S(2)}, u32[]{:S(2)}) collective-permute-start(bf16[512,1408]{1,0:T(8,128)(2,1)S(1)} %copy-done.69), channel_id=1, source_target_pairs={{0,8},{4,12},{8,0},{12,4},{16,24},{20,28},{24,16},{28,20},{1,9},{5... | collective-permute-start | bytes 4325384 | tf_op jit(solution)/shard_map/ppermute | solution.py:201
  152.5 44.0 %collective-permute-start.17 = (bf16[512,1408]{1,0:T(8,128)(2,1)S(1)}, bf16[512,1408]{1,0:T(8,128)(2,1)S(1)}, u32[]{:S(2)}, u32[]{:S(2)}) collective-permute-start(bf16[512,1408]{1,0:T(8,128)(2,1)S(1)} %copy-done.68), channel_id=1, source_target_pairs={{0,16},{4,20},{8,24},{12,28},{16,0},{20,4},{24,8},{28,12},{1,17},{... | collective-permute-start | bytes 4325384 | tf_op jit(solution)/shard_map/ppermute | solution.py:201
  154.0 32.2 %collective-permute-start.14 = (bf16[256,512]{1,0:T(8,128)(2,1)S(1)}, bf16[256,512]{1,0:T(8,128)(2,1)S(1)}, u32[]{:S(2)}, u32[]{:S(2)}) collective-permute-start(bf16[256,512]{1,0:T(8,128)(2,1)S(1)} %get-tuple-element.263), channel_id=1, source_target_pairs={{0,1},{1,0},{2,3},{3,2},{4,5},{5,4},{6,7},{7,6},{8,9},{9,8},{10,11... | collective-permute-start | bytes 786440 | tf_op jit(solution)/shard_map/ppermute | solution.py:201
  155.2 31.0 %collective-permute-start.15 = (bf16[256,512]{1,0:T(8,128)(2,1)S(1)}, bf16[256,512]{1,0:T(8,128)(2,1)S(1)}, u32[]{:S(2)}, u32[]{:S(2)}) collective-permute-start(bf16[256,512]{1,0:T(8,128)(2,1)S(1)} %get-tuple-element.262), channel_id=1, source_target_pairs={{0,2},{1,3},{2,0},{3,1},{4,6},{5,7},{6,4},{7,5},{8,10},{9,11},{10,... | collective-permute-start | bytes 786440 | tf_op jit(solution)/shard_map/ppermute | solution.py:201
  157.8 34.2 %collective-permute-start.16 = (bf16[256,512]{1,0:T(8,128)(2,1)S(1)}, bf16[256,512]{1,0:T(8,128)(2,1)S(1)}, u32[]{:S(2)}, u32[]{:S(2)}) collective-permute-start(bf16[256,512]{1,0:T(8,128)(2,1)S(1)} %get-tuple-element.261), channel_id=1, source_target_pairs={{0,3},{1,2},{2,1},{3,0},{4,7},{5,6},{6,5},{7,4},{8,11},{9,10},{10,... | collective-permute-start | bytes 786440 | tf_op jit(solution)/shard_map/ppermute | solution.py:201
  241.4 91.2 %all-gather.14.cloned.1.call-start = ((), (), s32[]{:S(2)}) async-start(), calls=%async_computation.9 | async-start | bytes 2621440 | tf_op jit(solution)/shard_map/all_gather | solution.py:324
  254.8 17.2 %collective-permute-start.23 = (bf16[704,512]{1,0:T(8,128)(2,1)S(1)}, bf16[704,512]{1,0:T(8,128)(2,1)}, u32[]{:S(2)}, u32[]{:S(2)}) collective-permute-start(bf16[704,512]{1,0:T(8,128)(2,1)S(1)} %pad_maximum_fusion.26), channel_id=1, source_target_pairs={{0,16},{4,20},{8,24},{12,28},{16,0},{20,4},{24,8},{28,12},{1,17},{... | collective-permute-start | bytes 2162696 | tf_op jit(solution)/shard_map/ppermute | solution.py:201
  259.0 172.8 %reduce-scatter.12.cloned.1.call-start = ((), (), s32[]{:S(2)}) async-start(), calls=%async_computation.13 | async-start | bytes 2621440 | tf_op jit(solution)/shard_map/reduce_scatter | solution.py:328
  274.4 20.4 %collective-permute-start.25 = (bf16[704,1024]{1,0:T(8,128)(2,1)}, bf16[704,1024]{1,0:T(8,128)(2,1)}, u32[]{:S(2)}, u32[]{:S(2)}) collective-permute-start(bf16[704,1024]{1,0:T(8,128)(2,1)} %pad_maximum_fusion.13), channel_id=1, source_target_pairs={{0,4},{4,0},{8,12},{12,8},{16,20},{20,16},{24,28},{28,24},{1,5},{5... | collective-permute-start | bytes 4325384 | tf_op jit(solution)/shard_map/ppermute | solution.py:201
  275.4 17.5 %collective-permute-start.26 = (bf16[704,1024]{1,0:T(8,128)(2,1)S(1)}, bf16[704,1024]{1,0:T(8,128)(2,1)}, u32[]{:S(2)}, u32[]{:S(2)}) collective-permute-start(bf16[704,1024]{1,0:T(8,128)(2,1)S(1)} %pad_maximum_fusion.14), channel_id=1, source_target_pairs={{0,4},{4,0},{8,12},{12,8},{16,20},{20,16},{24,28},{28,24},{1,5},{5... | collective-permute-start | bytes 4325384 | tf_op jit(solution)/shard_map/ppermute | solution.py:201
  363.8 88.4 %reduce-scatter.10.cloned.1.call-start = ((), (), s32[]{:S(2)}) async-start(), calls=%async_computation.12 | async-start | bytes 2621440 | tf_op jit(solution)/shard_map/reduce_scatter | solution.py:328
  379.0 31.9 %collective-permute-start.28 = (bf16[1024,1408]{1,0:T(8,128)(2,1)}, bf16[1024,1408]{1,0:T(8,128)(2,1)}, u32[]{:S(2)}, u32[]{:S(2)}) collective-permute-start(bf16[1024,1408]{1,0:T(8,128)(2,1)} %split.231), channel_id=1, source_target_pairs={{0,4},{4,0},{8,12},{12,8},{16,20},{20,16},{24,28},{28,24},{1,5},{5... | collective-permute-start | bytes 8650760 | tf_op jit(solution)/shard_map/ppermute | solution.py:201
  380.3 210.8 %reduce-scatter.6.cloned.1.call-start = ((), (), s32[]{:S(2)}) async-start(), calls=%async_computation.10 | async-start | bytes 2621440 | tf_op jit(solution)/shard_map/reduce_scatter | solution.py:328
  391.7 25.0 %collective-permute-start.27 = (bf16[1024,1408]{1,0:T(8,128)(2,1)}, bf16[1024,1408]{1,0:T(8,128)(2,1)}, u32[]{:S(2)}, u32[]{:S(2)}) collective-permute-start(bf16[1024,1408]{1,0:T(8,128)(2,1)} %split.229), channel_id=1, source_target_pairs={{0,4},{4,0},{8,12},{12,8},{16,20},{20,16},{24,28},{28,24},{1,5},{5... | collective-permute-start | bytes 8650760 | tf_op jit(solution)/shard_map/ppermute | solution.py:201
  410.4 180.8 %reduce-scatter.8.cloned.1.call-start = ((), (), s32[]{:S(2)}) async-start(), calls=%async_computation.11 | async-start | bytes 2621440 | tf_op jit(solution)/shard_map/reduce_scatter | solution.py:328
  416.6 37.0 %collective-permute-start.30 = (bf16[512,1408]{1,0:T(8,128)(2,1)}, bf16[512,1408]{1,0:T(8,128)(2,1)}, u32[]{:S(2)}, u32[]{:S(2)}) collective-permute-start(bf16[512,1408]{1,0:T(8,128)(2,1)} %pad_maximum_fusion.15), channel_id=1, source_target_pairs={{0,8},{4,12},{8,0},{12,4},{16,24},{20,28},{24,16},{28,20},{1,9},{5... | collective-permute-start | bytes 4325384 | tf_op jit(solution)/shard_map/ppermute | solution.py:201
  421.7 33.3 %collective-permute-start.29 = (bf16[512,1408]{1,0:T(8,128)(2,1)}, bf16[512,1408]{1,0:T(8,128)(2,1)}, u32[]{:S(2)}, u32[]{:S(2)}) collective-permute-start(bf16[512,1408]{1,0:T(8,128)(2,1)} %split.230), channel_id=1, source_target_pairs={{0,16},{4,20},{8,24},{12,28},{16,0},{20,4},{24,8},{28,12},{1,17},{... | collective-permute-start | bytes 4325384 | tf_op jit(solution)/shard_map/ppermute | solution.py:201
  479.7 187.7 %reduce-scatter.14.cloned.1.call-start = ((), (), s32[]{:S(2)}) async-start(), calls=%async_computation.14 | async-start | bytes 5242880 | tf_op jit(solution)/shard_map/reduce_scatter | solution.py:328
  483.6 23.1 %collective-permute-start.37 = (bf16[256,512]{1,0:T(8,128)(2,1)S(1)}, bf16[256,512]{1,0:T(8,128)(2,1)S(1)}, u32[]{:S(2)}, u32[]{:S(2)}) collective-permute-start(bf16[256,512]{1,0:T(8,128)(2,1)S(1)} %get-tuple-element.247), channel_id=1, source_target_pairs={{0,1},{1,0},{2,3},{3,2},{4,5},{5,4},{6,7},{7,6},{8,9},{9,8},{10,11... | collective-permute-start | bytes 786440 | tf_op jit(solution)/shard_map/ppermute | solution.py:201
  483.6 24.5 %collective-permute-start.38 = (bf16[256,512]{1,0:T(8,128)(2,1)S(1)}, bf16[256,512]{1,0:T(8,128)(2,1)S(1)}, u32[]{:S(2)}, u32[]{:S(2)}) collective-permute-start(bf16[256,512]{1,0:T(8,128)(2,1)S(1)} %get-tuple-element.246), channel_id=1, source_target_pairs={{0,2},{1,3},{2,0},{3,1},{4,6},{5,7},{6,4},{7,5},{8,10},{9,11},{10,... | collective-permute-start | bytes 786440 | tf_op jit(solution)/shard_map/ppermute | solution.py:201
  485.9 28.7 %collective-permute-start.39 = (bf16[256,512]{1,0:T(8,128)(2,1)S(1)}, bf16[256,512]{1,0:T(8,128)(2,1)S(1)}, u32[]{:S(2)}, u32[]{:S(2)}) collective-permute-start(bf16[256,512]{1,0:T(8,128)(2,1)S(1)} %get-tuple-element.245), channel_id=1, source_target_pairs={{0,3},{1,2},{2,1},{3,0},{4,7},{5,6},{6,5},{7,4},{8,11},{9,10},{10,... | collective-permute-start | bytes 786440 | tf_op jit(solution)/shard_map/ppermute | solution.py:201
  490.6 34.2 %collective-permute-start.31 = (bf16[1024,1024]{0,1:T(8,128)(2,1)S(1)}, bf16[1024,1024]{0,1:T(8,128)(2,1)S(1)}, u32[]{:S(2)}, u32[]{:S(2)}) collective-permute-start(bf16[1024,1024]{0,1:T(8,128)(2,1)S(1)} %get-tuple-element.132), channel_id=1, source_target_pairs={{0,4},{4,0},{8,12},{12,8},{16,20},{20,16},{24,28},{28,24},{1,5},{5... | collective-permute-start | bytes 6291464 | tf_op jit(solution)/shard_map/ppermute | solution.py:201
  492.7 22.2 %collective-permute-start.33 = (bf16[256,1408]{1,0:T(8,128)(2,1)S(1)}, bf16[256,1408]{1,0:T(8,128)(2,1)S(1)}, u32[]{:S(2)}, u32[]{:S(2)}) collective-permute-start(bf16[256,1408]{1,0:T(8,128)(2,1)S(1)} %split.238), channel_id=1, source_target_pairs={{0,16},{4,20},{8,24},{12,28},{16,0},{20,4},{24,8},{28,12},{1,17},{... | collective-permute-start | bytes 2162696 | tf_op jit(solution)/shard_map/ppermute | solution.py:201
  506.7 18.2 %collective-permute-start.32 = (bf16[256,1408]{1,0:T(8,128)(2,1)S(1)}, bf16[256,1408]{1,0:T(8,128)(2,1)S(1)}, u32[]{:S(2)}, u32[]{:S(2)}) collective-permute-start(bf16[256,1408]{1,0:T(8,128)(2,1)S(1)} %split.237), channel_id=1, source_target_pairs={{0,8},{4,12},{8,0},{12,4},{16,24},{20,28},{24,16},{28,20},{1,9},{5... | collective-permute-start | bytes 2162696 | tf_op jit(solution)/shard_map/ppermute | solution.py:201
  524.9 28.8 %collective-permute-start.36 = (bf16[1024,512]{0,1:T(8,128)(2,1)S(1)}, bf16[1024,512]{0,1:T(8,128)(2,1)S(1)}, u32[]{:S(2)}, u32[]{:S(2)}) collective-permute-start(bf16[1024,512]{0,1:T(8,128)(2,1)S(1)} %pad_maximum_fusion.20), channel_id=1, source_target_pairs={{0,8},{4,12},{8,0},{12,4},{16,24},{20,28},{24,16},{28,20},{1,9},{5... | collective-permute-start | bytes 3145736 | tf_op jit(solution)/shard_map/ppermute | solution.py:201
  528.2 26.7 %collective-permute-start.35 = (bf16[1024,512]{0,1:T(8,128)(2,1)S(1)}, bf16[1024,512]{0,1:T(8,128)(2,1)S(1)}, u32[]{:S(2)}, u32[]{:S(2)}) collective-permute-start(bf16[1024,512]{0,1:T(8,128)(2,1)S(1)} %split.235), channel_id=1, source_target_pairs={{0,16},{4,20},{8,24},{12,28},{16,0},{20,4},{24,8},{28,12},{1,17},{... | collective-permute-start | bytes 3145736 | tf_op jit(solution)/shard_map/ppermute | solution.py:201
  554.9 17.5 %collective-permute-start.41 = (bf16[1024,256]{0,1:T(8,128)(2,1)}, bf16[1024,256]{0,1:T(8,128)(2,1)}, u32[]{:S(2)}, u32[]{:S(2)}) collective-permute-start(bf16[1024,256]{0,1:T(8,128)(2,1)} %split.243), channel_id=1, source_target_pairs={{0,16},{4,20},{8,24},{12,28},{16,0},{20,4},{24,8},{28,12},{1,17},{... | collective-permute-start | bytes 1572872 | tf_op jit(solution)/shard_map/ppermute | solution.py:201
  593.4 23.9 %collective-permute-start.46 = (f32[19,256]{1,0:T(8,128)S(1)}, f32[19,256]{1,0:T(8,128)S(1)}, u32[]{:S(2)}, u32[]{:S(2)}) collective-permute-start(f32[19,256]{1,0:T(8,128)S(1)} %pad_maximum_fusion.34), channel_id=1, source_target_pairs={{0,4},{4,0},{8,12},{12,8},{16,20},{20,16},{24,28},{28,24},{1,5},{5... | collective-permute-start | bytes 58376 | tf_op jit(solution)/shard_map/ppermute | solution.py:201
  597.5 19.6 %collective-permute-start.45 = (bf16[512,768]{1,0:T(8,128)(2,1)S(1)}, bf16[512,768]{1,0:T(8,128)(2,1)S(1)}, u32[]{:S(2)}, u32[]{:S(2)}) collective-permute-start(bf16[512,768]{1,0:T(8,128)(2,1)S(1)} %pad_maximum_fusion.25), channel_id=1, source_target_pairs={{0,8},{4,12},{8,0},{12,4},{16,24},{20,28},{24,16},{28,20},{1,9},{5... | collective-permute-start | bytes 2359304 | tf_op jit(solution)/shard_map/ppermute | solution.py:201
  599.0 19.3 %collective-permute-start.44 = (bf16[512,768]{1,0:T(8,128)(2,1)S(1)}, bf16[512,768]{1,0:T(8,128)(2,1)S(1)}, u32[]{:S(2)}, u32[]{:S(2)}) collective-permute-start(bf16[512,768]{1,0:T(8,128)(2,1)S(1)} %split.247), channel_id=1, source_target_pairs={{0,16},{4,20},{8,24},{12,28},{16,0},{20,4},{24,8},{28,12},{1,17},{... | collective-permute-start | bytes 2359304 | tf_op jit(solution)/shard_map/ppermute | solution.py:201
  642.5 21.3 %collective-permute-start.56 = (bf16[704,512]{1,0:T(8,128)(2,1)S(1)}, bf16[704,512]{1,0:T(8,128)(2,1)S(1)}, u32[]{:S(2)}, u32[]{:S(2)}) collective-permute-start(bf16[704,512]{1,0:T(8,128)(2,1)S(1)} %split.255), channel_id=1, source_target_pairs={{0,16},{4,20},{8,24},{12,28},{16,0},{20,4},{24,8},{28,12},{1,17},{... | collective-permute-start | bytes 2162696 | tf_op jit(solution)/shard_map/ppermute | solution.py:201
  644.1 21.4 %collective-permute-start.57 = (bf16[704,512]{1,0:T(8,128)(2,1)S(1)}, bf16[704,512]{1,0:T(8,128)(2,1)S(1)}, u32[]{:S(2)}, u32[]{:S(2)}) collective-permute-start(bf16[704,512]{1,0:T(8,128)(2,1)S(1)} %pad_maximum_fusion.28), channel_id=1, source_target_pairs={{0,8},{4,12},{8,0},{12,4},{16,24},{20,28},{24,16},{28,20},{1,9},{5... | collective-permute-start | bytes 2162696 | tf_op jit(solution)/shard_map/ppermute | solution.py:201
  676.6 33.9 %collective-permute-start.62 = (bf16[512,256]{0,1:T(8,128)(2,1)S(1)}, bf16[512,256]{0,1:T(8,128)(2,1)S(1)}, u32[]{:S(2)}, u32[]{:S(2)}) collective-permute-start(bf16[512,256]{0,1:T(8,128)(2,1)S(1)} %copy-done.104), channel_id=1, source_target_pairs={{0,1},{1,0},{2,3},{3,2},{4,5},{5,4},{6,7},{7,6},{8,9},{9,8},{10,11... | collective-permute-start | bytes 786440 | tf_op jit(solution)/shard_map/ppermute | solution.py:201
  677.3 33.2 %collective-permute-start.63 = (bf16[512,256]{0,1:T(8,128)(2,1)S(1)}, bf16[512,256]{0,1:T(8,128)(2,1)S(1)}, u32[]{:S(2)}, u32[]{:S(2)}) collective-permute-start(bf16[512,256]{0,1:T(8,128)(2,1)S(1)} %copy-done.103), channel_id=1, source_target_pairs={{0,2},{1,3},{2,0},{3,1},{4,6},{5,7},{6,4},{7,5},{8,10},{9,11},{10,... | collective-permute-start | bytes 786440 | tf_op jit(solution)/shard_map/ppermute | solution.py:201
  680.0 30.5 %collective-permute-start.64 = (bf16[512,256]{0,1:T(8,128)(2,1)S(1)}, bf16[512,256]{0,1:T(8,128)(2,1)S(1)}, u32[]{:S(2)}, u32[]{:S(2)}) collective-permute-start(bf16[512,256]{0,1:T(8,128)(2,1)S(1)} %copy-done.102), channel_id=1, source_target_pairs={{0,3},{1,2},{2,1},{3,0},{4,7},{5,6},{6,5},{7,4},{8,11},{9,10},{10,... | collective-permute-start | bytes 786440 | tf_op jit(solution)/shard_map/ppermute | solution.py:201
  681.0 28.2 %collective-permute-start.61 = (f32[18,2048]{1,0:T(8,128)S(1)}, f32[18,2048]{1,0:T(8,128)S(1)}, u32[]{:S(2)}, u32[]{:S(2)}) collective-permute-start(f32[18,2048]{1,0:T(8,128)S(1)} %add.467), channel_id=1, source_target_pairs={{0,2},{1,3},{2,0},{3,1},{4,6},{5,7},{6,4},{7,5},{8,10},{9,11},{10,... | collective-permute-start | bytes 442376 | tf_op jit(solution)/shard_map/ppermute | solution.py:201
  (168 other events, 1752.2 us)
Sparse Core Ops, SparseCore 0:
  13.8 27.2 all-gather.7
  43.3 80.2 all-gather.5
  125.7 101.3 all-gather.9
  241.5 44.3 all-gather.11
  287.9 44.6 all-gather.13
  363.9 42.5 reduce-scatter.11
  408.9 43.1 reduce-scatter.9
  454.4 51.7 reduce-scatter.5
  508.6 45.3 reduce-scatter.7
  587.7 76.4 reduce-scatter.13

commit v3 on v2

--- a/solution.py
+++ b/solution.py
@@ -331,7 +331,8 @@
 class Everywhere:
     def __init__(self, flow, array, axes):
         self.flow, self.array = flow, array
-        self.left = [(axis, bit) for axis in axes for bit in bits_of(lax.axis_size(axis))]
+        bits = [[(axis, bit) for bit in bits_of(lax.axis_size(axis))] for axis in axes]
+        self.left = [some[k] for k in range(max(map(len, bits))) for some in bits if k < len(some)]
 
     def step(self, count=1):
         for axis, bit in self.left[:count]:
@@ -486,7 +487,7 @@
     norm1_term = jnp.sum(flow.held(total_low).astype(F32) * rows_one.astype(F32), axis=0, keepdims=True) / gain_one
     down_term = transposed_times(grad_low, rows_one)
     small = Everywhere(
-        flow, reorder(jnp.concatenate([down_term, norm1_term, norm2_term], 0), 1, True), ("dp", "tensor")
+        flow, reorder(jnp.concatenate([down_term, norm1_term, norm2_term], 0), 1, True), ("tensor", "dp")
     )
     by_head = Everywhere(
         flow, jnp.concatenate([up_term, bias_term, group_term[:, :kw], group_term[:, kw:]], 0), ("dp",)
@@ -506,15 +507,15 @@
     small.step()
     flow.note(grad_one)
     flow.turn()
-    down_sums = scatter_second(flow, *down_sums, 1)
-    small.step(len(small.left) - 1)
-    flow.turn()
-    small.step(len(small.left))
     proj_sums = jnp.concatenate(proj_sums, 0)
     grad_proj = lax.dynamic_slice_in_dim(proj_sums, head * vw, vw, 0).astype(F32)
     for m in range(1, heads):
         part = lax.dynamic_slice_in_dim(proj_sums, (head ^ m) * vw, vw, 0)
-        grad_proj = grad_proj + flow.send(part, "tensor", m).astype(F32)
+        grad_proj = grad_proj + swap(flow.held(part), "tensor", m).astype(F32)
+    down_sums = scatter_second(flow, *down_sums, 1)
+    small.step(len(small.left) - 1)
+    flow.turn()
+    small.step(len(small.left))
     grad_into_own = jnp.concatenate(into_sums, 1).astype(F32)
     grad_down_own = jnp.concatenate(down_sums, 0).astype(F32)
     grad_input = grad_resid + norm_back(grad_one, inputs_wide, scale_one, gain_one)

time: 725 us -> 722 us (level)
  waiting for transfers between devices: 243 us -> 235 us
    ppermute x65, waiting for transfers between devices: 181 us -> 173 us  [swap(): return lax.ppermute(array, axis, [(i, i ^ bit) for i in range(size)])]
    unnamed x358 -> x354, local copies, waits for them, and re-layouts: 52.8 us -> 52.8 us
  transfers between devices with their start and end apart: 75 -> 75, of which waited for: 28 -> 27; matrix products, arithmetic and copies ran while one was open for 40% -> 41% of each run, Pallas kernels for 5% -> 5%
where the time goes in v3:
time: 722 us; the launch traced here: 714 us
  waiting for transfers between devices  235 us (33%)
  matrix products  153 us (21%)
  other arithmetic  102 us (14%)
  local copies, waits for them, and re-layouts  102 us (14%)
  starting transfers between devices  61.9 us (9%)
  Pallas kernels  37.7 us (5%)
  between operations  22.1 us (3%)
    ppermute x65, waiting for transfers between devices, swap(): return lax.ppermute(array, axis, [(i, i ^ bit) for i in range(size)])  173 us
    dot_general x22, matrix products, dot(): lax.dot_general(a, b, (((ca,), (cb,)), ((), ())), precision=precision, pr...  153 us
    ppermute x65, starting transfers between devices, swap(): return lax.ppermute(array, axis, [(i, i ^ bit) for i in range(size)])  61 us
    unnamed x354, local copies, waits for them, and re-layouts  52.8 us
    all_gather x5, waiting for transfers between devices, gather_rows(): return lax.all_gather(array, 'tensor', axis=0, tiled=True)  41.5 us
    concatenate x1, other arithmetic, on_device(): proj_full = jnp.concatenate(gather_core(flow, *proj_full, 1), 0)  24.6 us
    pallas_call x1, Pallas kernels, mixer_backward(): pl.pallas_call(functools.partial(backward_kernel, kw, vw), out_shape=(jax...  23.8 us
    reduce_scatter x5, waiting for transfers between devices, scatter_rows(): return lax.psum_scatter(array, 'tensor', scatter_dimension=0, tiled=True)  20.4 us
  transfers between devices with their start and end apart: 75, of which 27 were waited for; matrix products, arithmetic and copies ran while one was open for 41% of the time, Pallas kernels for 5%

profile of v3, /device:TPU:0, one launch (start us, length us, event | category | flops | bytes accessed | tf_op | source)
XLA Modules:
  0.0 714.1 jit_solution(13803255678994416440)
XLA Ops:
  27.8 15.9 %collective-permute-done.3 = bf16[512,768]{1,0:T(8,128)(2,1)S(1)} collective-permute-done((bf16[512,768]{1,0:T(8,128)(2,1)}, bf16[512,768]{1,0:T(8,128)(2,1)S(1)}, u32[]{:S(2)}, u32[]{:S(2)}) %collective-permute-start.3) | collective-permute-done | bytes 786464 | tf_op jit(solution)/shard_map/ppermute | solution.py:201
  54.5 13.4 %collective-permute-done.7 = bf16[1024,256]{1,0:T(8,128)(2,1)S(1)} collective-permute-done((bf16[1024,256]{1,0:T(8,128)(2,1)S(1)}, bf16[1024,256]{1,0:T(8,128)(2,1)S(1)}, u32[]{:S(2)}, u32[]{:S(2)}) %collective-permute-start.7) | collective-permute-done | bytes 524320 | tf_op jit(solution)/shard_map/ppermute | solution.py:201
  74.2 18.5 %collective-permute-done.9 = bf16[1024,512]{1,0:T(8,128)(2,1)S(1)} collective-permute-done((bf16[1024,512]{1,0:T(8,128)(2,1)S(1)}, bf16[1024,512]{1,0:T(8,128)(2,1)S(1)}, u32[]{:S(2)}, u32[]{:S(2)}) %collective-permute-start.9) | collective-permute-done | bytes 1048608 | tf_op jit(solution)/shard_map/ppermute | solution.py:201
  107.7 11.8 %collective-permute-done.11 = bf16[256,1408]{1,0:T(8,128)(2,1)} collective-permute-done((bf16[256,1408]{1,0:T(8,128)(2,1)S(1)}, bf16[256,1408]{1,0:T(8,128)(2,1)}, u32[]{:S(2)}, u32[]{:S(2)}) %collective-permute-start.11) | collective-permute-done | bytes 720928 | tf_op jit(solution)/shard_map/ppermute | solution.py:201
  124.1 3.6 fusion.78.low_ref
  127.7 9.6 %fusion.28.proj_ref = bf16[1024,1536]{1,0:T(8,128)(2,1)S(1)} fusion(bf16[1024,2048]{1,0:T(8,128)(2,1)S(1)} %copy-done.23, bf16[2048,768]{1,0:T(8,128)(2,1)} %constant_dynamic-update-slice_fusion.16, bf16[1024,768]{1,0:T(8,128)(2,1)} %collective-permute-done.4, bf16[512,768]{1,0:T(8,128)(2,1)} %collective-permute-done.2, ...), kind=kOutput, calls=%fused_computation.43 | convolution fusion | flops 6475481088 | bytes 13631488 | tf_op jit(solution)/shard_map/dot_general | solution.py:21
  137.4 13.9 %mixer_forward.1 = (bf16[1024,512]{1,0:T(8,128)(2,1)S(1)}, bf16[1024,512]{1,0:T(8,128)(2,1)S(1)}, bf16[16,512,256]{2,1,0:T(8,128)(2,1)S(1)}) custom-call(bf16[1024,1536]{1,0:T(8,128)(2,1)S(1)} %fusion.28.proj_ref, f32[1024,16]{1,0:T(8,128)S(1)} %fusion.78.low_ref, f32[16,256]{1,0:T(8,128)S(1)} %copy-done, f32[1,256]{1,0:T(1,128)S(1)} %bitcast.105, ...), custom_call_target="tpu_custom_call" | custom-call | flops 20000000000 | bytes 10485760 | tf_op jit(solution)/shard_map/mixer_forward/pallas_call | solution.py:163
  161.6 24.6 %pad_maximum_fusion = bf16[2048,2048]{1,0:T(8,128)(2,1)} fusion(bf16[1024,2048]{1,0:T(8,128)(2,1)} %constant_dynamic-update-slice_fusion.37, bf16[1024,1024]{1,0:T(8,128)(2,1)} %collective-permute-done.12, bf16[1024,512]{1,0:T(8,128)(2,1)S(1)} %copy-done.48, bf16[1024,256]{1,0:T(8,128)(2,1)S(1)} %collective-permute-done.6, ...), kind=kLoop, calls=%fused_computation.2 | loop fusion | flops 41943040 | bytes 16777216 | tf_op jit(solution)/shard_map/concatenate | solution.py:383
  186.2 5.8 collective-permute-done.16
  200.9 5.8 pad_maximum_fusion.3
  206.7 20.5 %all-gather.10.cloned.1.call-done = bf16[1024,2048]{1,0:T(8,128)(2,1)} async-done(((bf16[256,2048]{1,0:T(8,128)(2,1)}), bf16[1024,2048]{1,0:T(8,128)(2,1)}) %all-gather.10.cloned.1.call-update) | async-done | bytes 4194320 | tf_op jit(solution)/shard_map/all_gather | solution.py:324
  227.2 4.8 fusion.65
  232.0 5.7 fusion.79
  248.2 4.4 collective-permute-done.21
  259.1 3.6 constant_dynamic-update-slice_fusion.54
  262.7 9.3 %collective-permute-done.23 = bf16[704,512]{1,0:T(8,128)(2,1)} collective-permute-done((bf16[704,512]{1,0:T(8,128)(2,1)S(1)}, bf16[704,512]{1,0:T(8,128)(2,1)}, u32[]{:S(2)}, u32[]{:S(2)}) %collective-permute-start.23) | collective-permute-done | bytes 720928 | tf_op jit(solution)/shard_map/ppermute | solution.py:201
  276.0 3.7 constant_dynamic-update-slice_fusion.50
  279.7 6.2 all-gather.12.cloned.1.call-done
  285.9 7.0 fusion.80
  295.1 6.7 fusion.60
  301.8 5.1 multiply_convert_fusion.5
  310.4 7.3 %add_convert_fusion.1 = bf16[512,2048]{1,0:T(8,128)(2,1)} fusion(f32[512,2048]{1,0:T(8,128)S(1)} %fusion.81, bf16[512,1408]{1,0:T(8,128)(2,1)S(1)} %get-tuple-element.212, bf16[2048,1408]{1,0:T(8,128)(2,1)} %constant_dynamic-update-slice_fusion.50), kind=kOutput, calls=%fused_computation.37 | convolution fusion | flops 2954887168 | bytes 13500416 | tf_op jit(solution)/shard_map/dot_general | solution.py:21
  317.7 14.8 %all-gather.14.cloned.1.call-done = bf16[512,2048]{1,0:T(8,128)(2,1)} async-done(((bf16[128,2048]{1,0:T(8,128)(2,1)}), bf16[512,2048]{1,0:T(8,128)(2,1)}) %all-gather.14.cloned.1.call-update) | async-done | bytes 2097168 | tf_op jit(solution)/shard_map/all_gather | solution.py:324
  332.6 6.7 fusion.82
  339.3 5.2 fusion.59
  344.5 8.3 %multiply_convert_fusion.1 = (bf16[512,1408]{1,0:T(8,128)(2,1)S(1)}, bf16[512,1408]{1,0:T(8,128)(2,1)S(1)}, bf16[512,1408]{1,0:T(8,128)(2,1)}) fusion(f32[512,1408]{1,0:T(8,128)S(1)} %fusion.59, f32[512,1408]{1,0:T(8,128)S(1)} %fusion.82, bf16[512,2048]{1,0:T(8,128)(2,1)S(1)} %copy-done.59, bf16[2048,1408]{1,0:T(8,128)(2,1)} %constant_dynamic-update-slice_fusion.50), kind=kOutput, calls=%fused_computation.55 | convolution fusion | flops 2963603456 | bytes 17956864 | tf_op jit(solution)/shard_map/dot_general | solution.py:21
  356.3 7.4 %add_convert_fusion = bf16[512,2048]{1,0:T(8,128)(2,1)} fusion(f32[512,2048]{1,0:T(8,128)S(1)} %fusion.83, bf16[512,1408]{1,0:T(8,128)(2,1)S(1)} %get-tuple-element.208, bf16[2048,1408]{1,0:T(8,128)(2,1)} %constant_dynamic-update-slice_fusion.50), kind=kOutput, calls=%fused_computation.36 | convolution fusion | flops 2954887168 | bytes 13500416 | tf_op jit(solution)/shard_map/dot_general | solution.py:21
  367.5 7.3 %convolution_convert_fusion.3 = bf16[2048,1408]{1,0:T(8,128)(2,1)S(1)} fusion(bf16[1024,2048]{1,0:T(8,128)(2,1)S(1)} %constant_dynamic-update-slice_fusion.64, bf16[1024,1408]{1,0:T(8,128)(2,1)S(1)} %pad_maximum_fusion.6), kind=kOutput, calls=%fused_computation.7 | convolution fusion | flops 5908463616 | bytes 12845056 | tf_op jit(solution)/shard_map/dot_general | solution.py:21
  380.4 9.5 %convolution_convert_fusion.4 = bf16[2048,1408]{1,0:T(8,128)(2,1)S(1)} fusion(bf16[1024,2048]{1,0:T(8,128)(2,1)} %copy-done.87, bf16[1024,1408]{1,0:T(8,128)(2,1)S(1)} %pad_maximum_fusion.5), kind=kOutput, calls=%fused_computation.8 | convolution fusion | flops 5908463616 | bytes 12845056 | tf_op jit(solution)/shard_map/dot_general | solution.py:21
  395.7 12.1 %convolution_convert_fusion.5 = bf16[1024,2048]{1,0:T(8,128)(2,1)S(1)} fusion(bf16[1024,1408]{1,0:T(8,128)(2,1)S(1)} %pad_maximum_fusion.4, bf16[704,2048]{1,0:T(8,128)(2,1)S(1)} %copy-done.114, bf16[704,1024]{1,0:T(8,128)(2,1)} %collective-permute-done.25, bf16[704,512]{1,0:T(8,128)(2,1)} %collective-permute-done.23, bf16[704,256]{1,0:T(8,128)(2,1)S(1)} %copy-done.85, ...), kind=kOutput, calls=%fused_computation.44 | convolution fusion | flops 5936513024 | bytes 12845056 | tf_op jit(solution)/shard_map/dot_general | solution.py:21
  423.7 8.1 %convolution_convert_fusion.2 = bf16[1408,2048]{1,0:T(8,128)(2,1)} fusion(bf16[1024,1408]{1,0:T(8,128)(2,1)S(1)} %pad_maximum_fusion.4, bf16[512,2048]{1,0:T(8,128)(2,1)S(1)} %bitcast.113, bf16[512,2048]{1,0:T(8,128)(2,1)S(1)} %bitcast.115), kind=kOutput, calls=%fused_computation.6 | convolution fusion | flops 5916852224 | bytes 12845056 | tf_op jit(solution)/shard_map/dot_general | solution.py:21
  431.8 20.3 %reduce-scatter.10.cloned.1.call-done = bf16[128,2048]{1,0:T(8,128)(2,1)} async-done(((bf16[512,2048]{1,0:T(8,128)(2,1)}), bf16[128,2048]{1,0:T(8,128)(2,1)}) %reduce-scatter.10.cloned.1.call-update) | async-done | bytes 524304 | tf_op jit(solution)/shard_map/reduce_scatter | solution.py:328
  459.5 5.9 convolution_convert_fusion.6
  479.7 3.7 fusion.63
  496.0 10.7 %collective-permute-done.37 = bf16[256,512]{1,0:T(8,128)(2,1)S(1)} collective-permute-done((bf16[256,512]{1,0:T(8,128)(2,1)S(1)}, bf16[256,512]{1,0:T(8,128)(2,1)S(1)}, u32[]{:S(2)}, u32[]{:S(2)}) %collective-permute-start.37) | collective-permute-done | bytes 262176 | tf_op jit(solution)/shard_map/ppermute | solution.py:201
  508.2 6.4 collective-permute-done.39
  516.4 8.4 %collective-permute-done.32 = bf16[256,1408]{1,0:T(8,128)(2,1)S(1)} collective-permute-done((bf16[256,1408]{1,0:T(8,128)(2,1)S(1)}, bf16[256,1408]{1,0:T(8,128)(2,1)S(1)}, u32[]{:S(2)}, u32[]{:S(2)}) %collective-permute-start.32) | collective-permute-done | bytes 720928 | tf_op jit(solution)/shard_map/ppermute | solution.py:201
  529.8 23.8 %mixer_backward.1 = (bf16[1024,1664]{1,0:T(8,128)(2,1)S(1)}, f32[16,256]{1,0:T(8,128)S(1)}, f32[1,256]{1,0:T(1,128)S(1)}, f32[1,512]{1,0:T(1,128)S(1)}) custom-call(bf16[1024,1536]{1,0:T(8,128)(2,1)S(1)} %copy-done.16, f32[1024,16]{1,0:T(8,128)S(1)} %copy-done.12, f32[16,256]{1,0:T(8,128)S(1)} %copy-done.2, f32[1,256]{1,0:T(1,128)S(1)} %bitcast.106, ...), custom_call_target="tpu_custom_call" | custom-call | flops 40000000000 | bytes 16777216 | tf_op jit(solution)/shard_map/mixer_backward/pallas_call | solution.py:182
  557.5 14.9 %fusion.31 = bf16[1024,2048]{1,0:T(8,128)(2,1)} fusion(bf16[1024,1664]{1,0:T(8,128)(2,1)S(1)} %get-tuple-element.146, bf16[2048,16]{1,0:T(8,128)(2,1)S(1)} %copy-done.101, bf16[2048,768]{1,0:T(8,128)(2,1)S(1)} %copy-done.110, bf16[1024,768]{1,0:T(8,128)(2,1)} %collective-permute-done.4, bf16[512,768]{1,0:T(8,128)(2,1)} %collective-permute-done.2, ...), kind=kOutput, calls=%fused_computation.45 | convolution fusion | flops 7029129216 | bytes 13959168 | tf_op jit(solution)/shard_map/dot_general | solution.py:21
  572.4 9.9 %convolution_convert_fusion = bf16[2048,1664]{1,0:T(8,128)(2,1)S(1)} fusion(bf16[1024,2048]{1,0:T(8,128)(2,1)} %all-gather.6.cloned.1.call-done, bf16[1024,1664]{1,0:T(8,128)(2,1)S(1)} %get-tuple-element.146), kind=kOutput, calls=%fused_computation.4 | convolution fusion | flops 6982729728 | bytes 14417920 | tf_op jit(solution)/shard_map/dot_general | solution.py:21
  587.6 3.5 fusion.51
  602.8 14.3 %collective-permute-done.45 = bf16[512,768]{1,0:T(8,128)(2,1)S(1)} collective-permute-done((bf16[512,768]{1,0:T(8,128)(2,1)S(1)}, bf16[512,768]{1,0:T(8,128)(2,1)S(1)}, u32[]{:S(2)}, u32[]{:S(2)}) %collective-permute-start.45) | collective-permute-done | bytes 786464 | tf_op jit(solution)/shard_map/ppermute | solution.py:201
  622.3 8.1 %collective-permute-done.50 = f32[19,256]{1,0:T(8,128)S(1)} collective-permute-done((f32[19,256]{1,0:T(8,128)S(1)}, f32[19,256]{1,0:T(8,128)S(1)}, u32[]{:S(2)}, u32[]{:S(2)}) %collective-permute-start.50) | collective-permute-done | bytes 19488 | tf_op jit(solution)/shard_map/ppermute | solution.py:201
  630.3 4.9 collective-permute-done.47
  651.8 20.3 %collective-permute-done.55 = f32[18,2048]{1,0:T(8,128)S(1)} collective-permute-done((f32[18,2048]{1,0:T(8,128)S(1)}, f32[18,2048]{1,0:T(8,128)S(1)}, u32[]{:S(2)}, u32[]{:S(2)}) %collective-permute-start.55) | collective-permute-done | bytes 147488 | tf_op jit(solution)/shard_map/ppermute | solution.py:201
  677.3 4.3 collective-permute-start.64
  686.0 4.5 collective-permute-done.58
  692.0 6.8 collective-permute-done.63
  (629 shorter events, 234.7 us)
Async XLA Ops:
  7.2 43.7 %all-gather.8.cloned.1.call-start = ((), (), s32[]{:S(2)}) async-start(), calls=%async_computation.6 | async-start | bytes 1310720 | tf_op jit(solution)/shard_map/all_gather | solution.py:324
  13.7 110.4 %all-gather.6.cloned.1.call-start = ((), (), s32[]{:S(2)}) async-start(), calls=%async_computation.5 | async-start | bytes 5242880 | tf_op jit(solution)/shard_map/all_gather | solution.py:324
  24.8 18.9 %collective-permute-start.3 = (bf16[512,768]{1,0:T(8,128)(2,1)}, bf16[512,768]{1,0:T(8,128)(2,1)S(1)}, u32[]{:S(2)}, u32[]{:S(2)}) collective-permute-start(bf16[512,768]{1,0:T(8,128)(2,1)} %pad_maximum_fusion.24), channel_id=1, source_target_pairs={{0,8},{4,12},{8,0},{12,4},{16,24},{20,28},{24,16},{28,20},{1,9},{5... | collective-permute-start | bytes 2359304 | tf_op jit(solution)/shard_map/ppermute | solution.py:201
  26.3 21.1 %collective-permute-start.2 = (bf16[512,768]{1,0:T(8,128)(2,1)}, bf16[512,768]{1,0:T(8,128)(2,1)}, u32[]{:S(2)}, u32[]{:S(2)}) collective-permute-start(bf16[512,768]{1,0:T(8,128)(2,1)} %pad_maximum_fusion.23), channel_id=1, source_target_pairs={{0,16},{4,20},{8,24},{12,28},{16,0},{20,4},{24,8},{28,12},{1,17},{... | collective-permute-start | bytes 2359304 | tf_op jit(solution)/shard_map/ppermute | solution.py:201
  27.7 199.5 %all-gather.10.cloned.1.call-start = ((), (), s32[]{:S(2)}) async-start(), calls=%async_computation.7 | async-start | bytes 5242880 | tf_op jit(solution)/shard_map/all_gather | solution.py:324
  68.1 24.7 %collective-permute-start.9 = (bf16[1024,512]{1,0:T(8,128)(2,1)S(1)}, bf16[1024,512]{1,0:T(8,128)(2,1)S(1)}, u32[]{:S(2)}, u32[]{:S(2)}) collective-permute-start(bf16[1024,512]{1,0:T(8,128)(2,1)S(1)} %pad_maximum_fusion.17), channel_id=1, source_target_pairs={{0,8},{4,12},{8,0},{12,4},{16,24},{20,28},{24,16},{28,20},{1,9},{5... | collective-permute-start | bytes 3145736 | tf_op jit(solution)/shard_map/ppermute | solution.py:201
  71.8 25.2 %collective-permute-start.8 = (bf16[1024,512]{1,0:T(8,128)(2,1)S(1)}, bf16[1024,512]{1,0:T(8,128)(2,1)S(1)}, u32[]{:S(2)}, u32[]{:S(2)}) collective-permute-start(bf16[1024,512]{1,0:T(8,128)(2,1)S(1)} %pad_maximum_fusion.16), channel_id=1, source_target_pairs={{0,16},{4,20},{8,24},{12,28},{16,0},{20,4},{24,8},{28,12},{1,17},{... | collective-permute-start | bytes 3145736 | tf_op jit(solution)/shard_map/ppermute | solution.py:201
  97.0 30.7 %collective-permute-start.13 = (bf16[1024,1024]{1,0:T(8,128)(2,1)}, bf16[1024,1024]{1,0:T(8,128)(2,1)}, u32[]{:S(2)}, u32[]{:S(2)}) collective-permute-start(bf16[1024,1024]{1,0:T(8,128)(2,1)} %pad_maximum_fusion.8), channel_id=1, source_target_pairs={{0,4},{4,0},{8,12},{12,8},{16,20},{20,16},{24,28},{28,24},{1,5},{5... | collective-permute-start | bytes 6291464 | tf_op jit(solution)/shard_map/ppermute | solution.py:201
  98.7 29.0 %collective-permute-start.12 = (bf16[1024,1024]{1,0:T(8,128)(2,1)}, bf16[1024,1024]{1,0:T(8,128)(2,1)}, u32[]{:S(2)}, u32[]{:S(2)}) collective-permute-start(bf16[1024,1024]{1,0:T(8,128)(2,1)} %pad_maximum_fusion.7), channel_id=1, source_target_pairs={{0,4},{4,0},{8,12},{12,8},{16,20},{20,16},{24,28},{28,24},{1,5},{5... | collective-permute-start | bytes 6291464 | tf_op jit(solution)/shard_map/ppermute | solution.py:201
  101.3 18.2 %collective-permute-start.11 = (bf16[256,1408]{1,0:T(8,128)(2,1)S(1)}, bf16[256,1408]{1,0:T(8,128)(2,1)}, u32[]{:S(2)}, u32[]{:S(2)}) collective-permute-start(bf16[256,1408]{1,0:T(8,128)(2,1)S(1)} %copy-done.30), channel_id=1, source_target_pairs={{0,16},{4,20},{8,24},{12,28},{16,0},{20,4},{24,8},{28,12},{1,17},{... | collective-permute-start | bytes 2162696 | tf_op jit(solution)/shard_map/ppermute | solution.py:201
  103.2 18.5 %collective-permute-start.10 = (bf16[256,1408]{1,0:T(8,128)(2,1)S(1)}, bf16[256,1408]{1,0:T(8,128)(2,1)}, u32[]{:S(2)}, u32[]{:S(2)}) collective-permute-start(bf16[256,1408]{1,0:T(8,128)(2,1)S(1)} %copy-done.31), channel_id=1, source_target_pairs={{0,8},{4,12},{8,0},{12,4},{16,24},{20,28},{24,16},{28,20},{1,9},{5... | collective-permute-start | bytes 2162696 | tf_op jit(solution)/shard_map/ppermute | solution.py:201
  105.0 180.9 %all-gather.12.cloned.1.call-start = ((), (), s32[]{:S(2)}) async-start(), calls=%async_computation.8 | async-start | bytes 2621440 | tf_op jit(solution)/shard_map/all_gather | solution.py:324
  151.4 42.1 %collective-permute-start.18 = (bf16[512,1408]{1,0:T(8,128)(2,1)S(1)}, bf16[512,1408]{1,0:T(8,128)(2,1)S(1)}, u32[]{:S(2)}, u32[]{:S(2)}) collective-permute-start(bf16[512,1408]{1,0:T(8,128)(2,1)S(1)} %copy-done.69), channel_id=1, source_target_pairs={{0,8},{4,12},{8,0},{12,4},{16,24},{20,28},{24,16},{28,20},{1,9},{5... | collective-permute-start | bytes 4325384 | tf_op jit(solution)/shard_map/ppermute | solution.py:201
  152.5 44.0 %collective-permute-start.17 = (bf16[512,1408]{1,0:T(8,128)(2,1)S(1)}, bf16[512,1408]{1,0:T(8,128)(2,1)S(1)}, u32[]{:S(2)}, u32[]{:S(2)}) collective-permute-start(bf16[512,1408]{1,0:T(8,128)(2,1)S(1)} %copy-done.68), channel_id=1, source_target_pairs={{0,16},{4,20},{8,24},{12,28},{16,0},{20,4},{24,8},{28,12},{1,17},{... | collective-permute-start | bytes 4325384 | tf_op jit(solution)/shard_map/ppermute | solution.py:201
  154.1 32.2 %collective-permute-start.14 = (bf16[256,512]{1,0:T(8,128)(2,1)S(1)}, bf16[256,512]{1,0:T(8,128)(2,1)S(1)}, u32[]{:S(2)}, u32[]{:S(2)}) collective-permute-start(bf16[256,512]{1,0:T(8,128)(2,1)S(1)} %get-tuple-element.263), channel_id=1, source_target_pairs={{0,1},{1,0},{2,3},{3,2},{4,5},{5,4},{6,7},{7,6},{8,9},{9,8},{10,11... | collective-permute-start | bytes 786440 | tf_op jit(solution)/shard_map/ppermute | solution.py:201
  155.2 31.0 %collective-permute-start.15 = (bf16[256,512]{1,0:T(8,128)(2,1)S(1)}, bf16[256,512]{1,0:T(8,128)(2,1)S(1)}, u32[]{:S(2)}, u32[]{:S(2)}) collective-permute-start(bf16[256,512]{1,0:T(8,128)(2,1)S(1)} %get-tuple-element.262), channel_id=1, source_target_pairs={{0,2},{1,3},{2,0},{3,1},{4,6},{5,7},{6,4},{7,5},{8,10},{9,11},{10,... | collective-permute-start | bytes 786440 | tf_op jit(solution)/shard_map/ppermute | solution.py:201
  157.8 34.2 %collective-permute-start.16 = (bf16[256,512]{1,0:T(8,128)(2,1)S(1)}, bf16[256,512]{1,0:T(8,128)(2,1)S(1)}, u32[]{:S(2)}, u32[]{:S(2)}) collective-permute-start(bf16[256,512]{1,0:T(8,128)(2,1)S(1)} %get-tuple-element.261), channel_id=1, source_target_pairs={{0,3},{1,2},{2,1},{3,0},{4,7},{5,6},{6,5},{7,4},{8,11},{9,10},{10,... | collective-permute-start | bytes 786440 | tf_op jit(solution)/shard_map/ppermute | solution.py:201
  241.4 91.2 %all-gather.14.cloned.1.call-start = ((), (), s32[]{:S(2)}) async-start(), calls=%async_computation.9 | async-start | bytes 2621440 | tf_op jit(solution)/shard_map/all_gather | solution.py:324
  254.8 17.2 %collective-permute-start.23 = (bf16[704,512]{1,0:T(8,128)(2,1)S(1)}, bf16[704,512]{1,0:T(8,128)(2,1)}, u32[]{:S(2)}, u32[]{:S(2)}) collective-permute-start(bf16[704,512]{1,0:T(8,128)(2,1)S(1)} %pad_maximum_fusion.26), channel_id=1, source_target_pairs={{0,16},{4,20},{8,24},{12,28},{16,0},{20,4},{24,8},{28,12},{1,17},{... | collective-permute-start | bytes 2162696 | tf_op jit(solution)/shard_map/ppermute | solution.py:201
  259.0 172.8 %reduce-scatter.12.cloned.1.call-start = ((), (), s32[]{:S(2)}) async-start(), calls=%async_computation.13 | async-start | bytes 2621440 | tf_op jit(solution)/shard_map/reduce_scatter | solution.py:328
  274.4 20.4 %collective-permute-start.25 = (bf16[704,1024]{1,0:T(8,128)(2,1)}, bf16[704,1024]{1,0:T(8,128)(2,1)}, u32[]{:S(2)}, u32[]{:S(2)}) collective-permute-start(bf16[704,1024]{1,0:T(8,128)(2,1)} %pad_maximum_fusion.13), channel_id=1, source_target_pairs={{0,4},{4,0},{8,12},{12,8},{16,20},{20,16},{24,28},{28,24},{1,5},{5... | collective-permute-start | bytes 4325384 | tf_op jit(solution)/shard_map/ppermute | solution.py:201
  275.4 17.5 %collective-permute-start.26 = (bf16[704,1024]{1,0:T(8,128)(2,1)S(1)}, bf16[704,1024]{1,0:T(8,128)(2,1)}, u32[]{:S(2)}, u32[]{:S(2)}) collective-permute-start(bf16[704,1024]{1,0:T(8,128)(2,1)S(1)} %pad_maximum_fusion.14), channel_id=1, source_target_pairs={{0,4},{4,0},{8,12},{12,8},{16,20},{20,16},{24,28},{28,24},{1,5},{5... | collective-permute-start | bytes 4325384 | tf_op jit(solution)/shard_map/ppermute | solution.py:201
  363.8 88.3 %reduce-scatter.10.cloned.1.call-start = ((), (), s32[]{:S(2)}) async-start(), calls=%async_computation.12 | async-start | bytes 2621440 | tf_op jit(solution)/shard_map/reduce_scatter | solution.py:328
  379.1 31.8 %collective-permute-start.28 = (bf16[1024,1408]{1,0:T(8,128)(2,1)}, bf16[1024,1408]{1,0:T(8,128)(2,1)}, u32[]{:S(2)}, u32[]{:S(2)}) collective-permute-start(bf16[1024,1408]{1,0:T(8,128)(2,1)} %split.231), channel_id=1, source_target_pairs={{0,4},{4,0},{8,12},{12,8},{16,20},{20,16},{24,28},{28,24},{1,5},{5... | collective-permute-start | bytes 8650760 | tf_op jit(solution)/shard_map/ppermute | solution.py:201
  380.3 210.8 %reduce-scatter.6.cloned.1.call-start = ((), (), s32[]{:S(2)}) async-start(), calls=%async_computation.10 | async-start | bytes 2621440 | tf_op jit(solution)/shard_map/reduce_scatter | solution.py:328
  391.7 25.0 %collective-permute-start.27 = (bf16[1024,1408]{1,0:T(8,128)(2,1)}, bf16[1024,1408]{1,0:T(8,128)(2,1)}, u32[]{:S(2)}, u32[]{:S(2)}) collective-permute-start(bf16[1024,1408]{1,0:T(8,128)(2,1)} %split.229), channel_id=1, source_target_pairs={{0,4},{4,0},{8,12},{12,8},{16,20},{20,16},{24,28},{28,24},{1,5},{5... | collective-permute-start | bytes 8650760 | tf_op jit(solution)/shard_map/ppermute | solution.py:201
  410.4 180.8 %reduce-scatter.8.cloned.1.call-start = ((), (), s32[]{:S(2)}) async-start(), calls=%async_computation.11 | async-start | bytes 2621440 | tf_op jit(solution)/shard_map/reduce_scatter | solution.py:328
  416.6 37.0 %collective-permute-start.30 = (bf16[512,1408]{1,0:T(8,128)(2,1)}, bf16[512,1408]{1,0:T(8,128)(2,1)}, u32[]{:S(2)}, u32[]{:S(2)}) collective-permute-start(bf16[512,1408]{1,0:T(8,128)(2,1)} %pad_maximum_fusion.15), channel_id=1, source_target_pairs={{0,8},{4,12},{8,0},{12,4},{16,24},{20,28},{24,16},{28,20},{1,9},{5... | collective-permute-start | bytes 4325384 | tf_op jit(solution)/shard_map/ppermute | solution.py:201
  421.7 33.4 %collective-permute-start.29 = (bf16[512,1408]{1,0:T(8,128)(2,1)}, bf16[512,1408]{1,0:T(8,128)(2,1)}, u32[]{:S(2)}, u32[]{:S(2)}) collective-permute-start(bf16[512,1408]{1,0:T(8,128)(2,1)} %split.230), channel_id=1, source_target_pairs={{0,16},{4,20},{8,24},{12,28},{16,0},{20,4},{24,8},{28,12},{1,17},{... | collective-permute-start | bytes 4325384 | tf_op jit(solution)/shard_map/ppermute | solution.py:201
  479.7 196.1 %reduce-scatter.14.cloned.1.call-start = ((), (), s32[]{:S(2)}) async-start(), calls=%async_computation.14 | async-start | bytes 5242880 | tf_op jit(solution)/shard_map/reduce_scatter | solution.py:328
  483.6 23.1 %collective-permute-start.37 = (bf16[256,512]{1,0:T(8,128)(2,1)S(1)}, bf16[256,512]{1,0:T(8,128)(2,1)S(1)}, u32[]{:S(2)}, u32[]{:S(2)}) collective-permute-start(bf16[256,512]{1,0:T(8,128)(2,1)S(1)} %get-tuple-element.247), channel_id=1, source_target_pairs={{0,1},{1,0},{2,3},{3,2},{4,5},{5,4},{6,7},{7,6},{8,9},{9,8},{10,11... | collective-permute-start | bytes 786440 | tf_op jit(solution)/shard_map/ppermute | solution.py:201
  483.6 24.5 %collective-permute-start.38 = (bf16[256,512]{1,0:T(8,128)(2,1)S(1)}, bf16[256,512]{1,0:T(8,128)(2,1)S(1)}, u32[]{:S(2)}, u32[]{:S(2)}) collective-permute-start(bf16[256,512]{1,0:T(8,128)(2,1)S(1)} %get-tuple-element.246), channel_id=1, source_target_pairs={{0,2},{1,3},{2,0},{3,1},{4,6},{5,7},{6,4},{7,5},{8,10},{9,11},{10,... | collective-permute-start | bytes 786440 | tf_op jit(solution)/shard_map/ppermute | solution.py:201
  485.9 28.7 %collective-permute-start.39 = (bf16[256,512]{1,0:T(8,128)(2,1)S(1)}, bf16[256,512]{1,0:T(8,128)(2,1)S(1)}, u32[]{:S(2)}, u32[]{:S(2)}) collective-permute-start(bf16[256,512]{1,0:T(8,128)(2,1)S(1)} %get-tuple-element.245), channel_id=1, source_target_pairs={{0,3},{1,2},{2,1},{3,0},{4,7},{5,6},{6,5},{7,4},{8,11},{9,10},{10,... | collective-permute-start | bytes 786440 | tf_op jit(solution)/shard_map/ppermute | solution.py:201
  490.6 34.2 %collective-permute-start.31 = (bf16[1024,1024]{0,1:T(8,128)(2,1)S(1)}, bf16[1024,1024]{0,1:T(8,128)(2,1)S(1)}, u32[]{:S(2)}, u32[]{:S(2)}) collective-permute-start(bf16[1024,1024]{0,1:T(8,128)(2,1)S(1)} %get-tuple-element.132), channel_id=1, source_target_pairs={{0,4},{4,0},{8,12},{12,8},{16,20},{20,16},{24,28},{28,24},{1,5},{5... | collective-permute-start | bytes 6291464 | tf_op jit(solution)/shard_map/ppermute | solution.py:201
  492.7 22.2 %collective-permute-start.33 = (bf16[256,1408]{1,0:T(8,128)(2,1)S(1)}, bf16[256,1408]{1,0:T(8,128)(2,1)S(1)}, u32[]{:S(2)}, u32[]{:S(2)}) collective-permute-start(bf16[256,1408]{1,0:T(8,128)(2,1)S(1)} %split.238), channel_id=1, source_target_pairs={{0,16},{4,20},{8,24},{12,28},{16,0},{20,4},{24,8},{28,12},{1,17},{... | collective-permute-start | bytes 2162696 | tf_op jit(solution)/shard_map/ppermute | solution.py:201
  506.7 18.2 %collective-permute-start.32 = (bf16[256,1408]{1,0:T(8,128)(2,1)S(1)}, bf16[256,1408]{1,0:T(8,128)(2,1)S(1)}, u32[]{:S(2)}, u32[]{:S(2)}) collective-permute-start(bf16[256,1408]{1,0:T(8,128)(2,1)S(1)} %split.237), channel_id=1, source_target_pairs={{0,8},{4,12},{8,0},{12,4},{16,24},{20,28},{24,16},{28,20},{1,9},{5... | collective-permute-start | bytes 2162696 | tf_op jit(solution)/shard_map/ppermute | solution.py:201
  524.9 28.8 %collective-permute-start.36 = (bf16[1024,512]{0,1:T(8,128)(2,1)S(1)}, bf16[1024,512]{0,1:T(8,128)(2,1)S(1)}, u32[]{:S(2)}, u32[]{:S(2)}) collective-permute-start(bf16[1024,512]{0,1:T(8,128)(2,1)S(1)} %pad_maximum_fusion.20), channel_id=1, source_target_pairs={{0,8},{4,12},{8,0},{12,4},{16,24},{20,28},{24,16},{28,20},{1,9},{5... | collective-permute-start | bytes 3145736 | tf_op jit(solution)/shard_map/ppermute | solution.py:201
  528.2 26.7 %collective-permute-start.35 = (bf16[1024,512]{0,1:T(8,128)(2,1)S(1)}, bf16[1024,512]{0,1:T(8,128)(2,1)S(1)}, u32[]{:S(2)}, u32[]{:S(2)}) collective-permute-start(bf16[1024,512]{0,1:T(8,128)(2,1)S(1)} %split.235), channel_id=1, source_target_pairs={{0,16},{4,20},{8,24},{12,28},{16,0},{20,4},{24,8},{28,12},{1,17},{... | collective-permute-start | bytes 3145736 | tf_op jit(solution)/shard_map/ppermute | solution.py:201
  554.9 17.5 %collective-permute-start.41 = (bf16[1024,256]{0,1:T(8,128)(2,1)}, bf16[1024,256]{0,1:T(8,128)(2,1)}, u32[]{:S(2)}, u32[]{:S(2)}) collective-permute-start(bf16[1024,256]{0,1:T(8,128)(2,1)} %split.243), channel_id=1, source_target_pairs={{0,16},{4,20},{8,24},{12,28},{16,0},{20,4},{24,8},{28,12},{1,17},{... | collective-permute-start | bytes 1572872 | tf_op jit(solution)/shard_map/ppermute | solution.py:201
  593.4 23.9 %collective-permute-start.46 = (f32[19,256]{1,0:T(8,128)S(1)}, f32[19,256]{1,0:T(8,128)S(1)}, u32[]{:S(2)}, u32[]{:S(2)}) collective-permute-start(f32[19,256]{1,0:T(8,128)S(1)} %pad_maximum_fusion.34), channel_id=1, source_target_pairs={{0,4},{4,0},{8,12},{12,8},{16,20},{20,16},{24,28},{28,24},{1,5},{5... | collective-permute-start | bytes 58376 | tf_op jit(solution)/shard_map/ppermute | solution.py:201
  597.5 19.6 %collective-permute-start.45 = (bf16[512,768]{1,0:T(8,128)(2,1)S(1)}, bf16[512,768]{1,0:T(8,128)(2,1)S(1)}, u32[]{:S(2)}, u32[]{:S(2)}) collective-permute-start(bf16[512,768]{1,0:T(8,128)(2,1)S(1)} %pad_maximum_fusion.25), channel_id=1, source_target_pairs={{0,8},{4,12},{8,0},{12,4},{16,24},{20,28},{24,16},{28,20},{1,9},{5... | collective-permute-start | bytes 2359304 | tf_op jit(solution)/shard_map/ppermute | solution.py:201
  599.0 19.3 %collective-permute-start.44 = (bf16[512,768]{1,0:T(8,128)(2,1)S(1)}, bf16[512,768]{1,0:T(8,128)(2,1)S(1)}, u32[]{:S(2)}, u32[]{:S(2)}) collective-permute-start(bf16[512,768]{1,0:T(8,128)(2,1)S(1)} %split.247), channel_id=1, source_target_pairs={{0,16},{4,20},{8,24},{12,28},{16,0},{20,4},{24,8},{28,12},{1,17},{... | collective-permute-start | bytes 2359304 | tf_op jit(solution)/shard_map/ppermute | solution.py:201
  644.0 28.2 %collective-permute-start.56 = (bf16[704,512]{1,0:T(8,128)(2,1)S(1)}, bf16[704,512]{1,0:T(8,128)(2,1)S(1)}, u32[]{:S(2)}, u32[]{:S(2)}) collective-permute-start(bf16[704,512]{1,0:T(8,128)(2,1)S(1)} %split.255), channel_id=1, source_target_pairs={{0,16},{4,20},{8,24},{12,28},{16,0},{20,4},{24,8},{28,12},{1,17},{... | collective-permute-start | bytes 2162696 | tf_op jit(solution)/shard_map/ppermute | solution.py:201
  644.9 29.1 %collective-permute-start.57 = (bf16[704,512]{1,0:T(8,128)(2,1)S(1)}, bf16[704,512]{1,0:T(8,128)(2,1)S(1)}, u32[]{:S(2)}, u32[]{:S(2)}) collective-permute-start(bf16[704,512]{1,0:T(8,128)(2,1)S(1)} %pad_maximum_fusion.28), channel_id=1, source_target_pairs={{0,8},{4,12},{8,0},{12,4},{16,24},{20,28},{24,16},{28,20},{1,9},{5... | collective-permute-start | bytes 2162696 | tf_op jit(solution)/shard_map/ppermute | solution.py:201
  649.5 22.6 %collective-permute-start.55 = (f32[18,2048]{1,0:T(8,128)S(1)}, f32[18,2048]{1,0:T(8,128)S(1)}, u32[]{:S(2)}, u32[]{:S(2)}) collective-permute-start(f32[18,2048]{1,0:T(8,128)S(1)} %add.462), channel_id=1, source_target_pairs={{0,2},{1,3},{2,0},{3,1},{4,6},{5,7},{6,4},{7,5},{8,10},{9,11},{10,... | collective-permute-start | bytes 442376 | tf_op jit(solution)/shard_map/ppermute | solution.py:201
  675.7 24.3 %collective-permute-start.59 = (bf16[704,256]{1,0:T(8,128)(2,1)}, bf16[704,256]{1,0:T(8,128)(2,1)}, u32[]{:S(2)}, u32[]{:S(2)}) collective-permute-start(bf16[704,256]{1,0:T(8,128)(2,1)} %split.258), channel_id=1, source_target_pairs={{0,8},{4,12},{8,0},{12,4},{16,24},{20,28},{24,16},{28,20},{1,9},{5... | collective-permute-start | bytes 1081352 | tf_op jit(solution)/shard_map/ppermute | solution.py:201
  677.2 21.6 %collective-permute-start.63 = (bf16[512,256]{0,1:T(8,128)(2,1)}, bf16[512,256]{0,1:T(8,128)(2,1)S(1)}, u32[]{:S(2)}, u32[]{:S(2)}) collective-permute-start(bf16[512,256]{0,1:T(8,128)(2,1)} %get-tuple-element.172), channel_id=1, source_target_pairs={{0,2},{1,3},{2,0},{3,1},{4,6},{5,7},{6,4},{7,5},{8,10},{9,11},{10,... | collective-permute-start | bytes 786440 | tf_op jit(solution)/shard_map/ppermute | solution.py:201
  677.3 21.5 %collective-permute-start.64 = (bf16[512,256]{0,1:T(8,128)(2,1)}, bf16[512,256]{0,1:T(8,128)(2,1)S(1)}, u32[]{:S(2)}, u32[]{:S(2)}) collective-permute-start(bf16[512,256]{0,1:T(8,128)(2,1)} %get-tuple-element.173), channel_id=1, source_target_pairs={{0,3},{1,2},{2,1},{3,0},{4,7},{5,6},{6,5},{7,4},{8,11},{9,10},{10,... | collective-permute-start | bytes 786440 | tf_op jit(solution)/shard_map/ppermute | solution.py:201
  (166 other events, 1728.1 us)
Sparse Core Ops, SparseCore 0:
  13.8 27.2 all-gather.7
  43.3 80.2 all-gather.5
  125.7 101.3 all-gather.9
  241.5 44.3 all-gather.11
  287.9 44.6 all-gather.13
  363.9 42.5 reduce-scatter.11
  408.9 43.1 reduce-scatter.9
  454.4 51.7 reduce-scatter.5
  508.6 45.3 reduce-scatter.7
  587.7 84.5 reduce-scatter.13
